TPU v7x, 32 devices: a whole 2x2x4 slice. The times are simulated.
32 devices in a mesh: dp: 8 (over z, core), tensor: 4 (over y, x).
Axes of the slice: x: 2, y: 2, z: 4, core: 2. Of those that a mesh axis runs over, the one named last changes fastest.
Arguments:
- inputs: bfloat16 [32, 1024, 1024], P('dp', 'tensor'), may hold values from -6 to 6
- encoded: bfloat16 [32, 1024, 1024], P('dp', 'tensor'), may hold values from -6 to 6
- source_lengths: int32 [32], P('dp'), may hold values from 1 to 1024, as said below
- query_weight: bfloat16 [1024, 1024], P(None, 'tensor'), may hold values from -0.1875 to 0.1875
- key_weight: bfloat16 [1024, 1024], P(None, 'tensor'), may hold values from -0.1875 to 0.1875
- value_weight: bfloat16 [1024, 1024], P(None, 'tensor'), may hold values from -0.1875 to 0.1875
- output_weight: bfloat16 [1024, 1024], P('tensor'), may hold values from -0.75 to 0.75
- cross_query: bfloat16 [1024, 1024], P(None, 'tensor'), may hold values from -0.1875 to 0.1875
- cross_key: bfloat16 [1024, 1024], P(None, 'tensor'), may hold values from -0.1875 to 0.1875
- cross_value: bfloat16 [1024, 1024], P(None, 'tensor'), may hold values from -0.1875 to 0.1875
- cross_output: bfloat16 [1024, 1024], P('tensor'), may hold values from -0.75 to 0.75
- up_weight: bfloat16 [1024, 4096], P(None, 'tensor'), may hold values from -0.1875 to 0.1875
- down_weight: bfloat16 [4096, 1024], P('tensor'), may hold values from -0.09375 to 0.09375
- adapter_in: bfloat16 [1024, 512], P(None, 'tensor'), may hold values from -0.1875 to 0.1875
- adapter_out: bfloat16 [512, 1024], P('tensor'), may hold values from -0.125 to 0.125
- adapter_bias: float32 [512], P('tensor'), may hold values from -3 to 3
- adapter_shift: float32 [1024], replicated, may hold values from -1.2 to 1.2
- norm_gains: float32 [3, 1024], replicated, may hold values from 0.5 to 1.5
- norm_shifts: float32 [3, 1024], replicated, may hold values from -1.8 to 1.8
- output_grad: bfloat16 [32, 1024, 1024], P('dp', 'tensor'), may hold values from -6 to 6
Outputs:
- result: bfloat16 [32, 1024, 1024], P('dp', 'tensor')
- input_grad: bfloat16 [32, 1024, 1024], P('dp', 'tensor')
- encoded_grad: bfloat16 [32, 1024, 1024], P('dp', 'tensor')
- adapter_in_grad: float32 [1024, 512], P(None, 'tensor')
- adapter_out_grad: float32 [512, 1024], P('tensor')
- adapter_bias_grad: float32 [512], P('tensor')
- adapter_shift_grad: float32 [1024], replicated
- gains_grad: float32 [3, 1024], replicated
- shifts_grad: float32 [3, 1024], replicated
Inputs may be any that keep to these rules, and one draw needn't show every extreme that they name: `source_lengths`: in each group of 4 consecutive sequences one has more than 1024 - 1024 // 4 live source positions.
All inputs are finite; a program needn't handle non-finite values.
Results may differ from a plain program's by a relative error of at most 0.034.
Values may be sent and summed in bfloat16 or wider, within the bound.
No kernel may reach another device: no remote copies, remote signals or barrier semaphores. Data moves between devices by JAX's collectives and lax.ppermute only.
A program may use at most 512 MiB of HBM per device.

v0:
```python
import jax
import jax.numpy as jnp
from jax import lax
from jax.sharding import PartitionSpec as P

HEAD = 64


def gelu_tanh(values):
    return jax.nn.gelu(values, approximate=True)


def multiply(left, right):
    return jnp.dot(left, right, preferred_element_type=jnp.float32)


def multiply_by_transpose(left, right):
    return lax.dot_general(
        left, right, (((1,), (1,)), ((), ())), preferred_element_type=jnp.float32
    )


def multiply_transposed_left(left, right):
    return lax.dot_general(
        left, right, (((0,), (0,)), ((), ())), preferred_element_type=jnp.float32
    )


def layer_norm(values, gain, shift):
    center = values - jnp.mean(values, axis=-1, keepdims=True)
    scale = lax.rsqrt(jnp.mean(center * center, axis=-1, keepdims=True) + 1e-05)
    normed = center * scale
    return (normed * gain + shift, normed, scale)


def norm_back(grad, normed, scale, gain):
    inner = grad * gain
    middle = jnp.mean(inner, axis=-1, keepdims=True)
    along = jnp.mean(inner * normed, axis=-1, keepdims=True)
    return (
        scale * (inner - middle - normed * along),
        jnp.sum(grad * normed, axis=(0, 1)),
        jnp.sum(grad, axis=(0, 1)),
    )


def attend(query_low, key_low, value_low, keep_for):
    count = query_low.shape[1]
    block = min(512, count)
    factor = query_low.shape[-1] ** (-0.5)
    contexts = []
    totals = []
    for first in range(0, count, block):
        scores = (
            jnp.einsum(
                "sqhe,skhe->shqk",
                query_low[:, first : first + block],
                key_low,
                preferred_element_type=jnp.float32,
            )
            * factor
        )
        scores = jnp.where(keep_for(first, block), scores, -1000000000.0)
        top_score = jnp.max(scores, axis=-1, keepdims=True)
        weights = jnp.exp(scores - top_score)
        denom = jnp.sum(weights, axis=-1, keepdims=True)
        probs_low = (weights / denom).astype(jnp.bfloat16)
        contexts.append(
            jnp.einsum("shqk,skhe->sqhe", probs_low, value_low, preferred_element_type=jnp.float32)
        )
        totals.append(top_score + jnp.log(denom))
    return (jnp.concatenate(contexts, axis=1), jnp.concatenate(totals, axis=2))


def attend_back(query_low, key_low, value_low, grad_low, totals, keep_for):
    count = query_low.shape[1]
    block = min(512, count)
    factor = query_low.shape[-1] ** (-0.5)
    key_grad = jnp.zeros(key_low.shape, jnp.float32)
    value_grad = jnp.zeros(value_low.shape, jnp.float32)
    query_grads = []
    for first in range(0, count, block):
        query_part = query_low[:, first : first + block]
        grad_part = grad_low[:, first : first + block]
        scores = (
            jnp.einsum("sqhe,skhe->shqk", query_part, key_low, preferred_element_type=jnp.float32)
            * factor
        )
        scores = jnp.where(keep_for(first, block), scores, -1000000000.0)
        probs = jnp.exp(scores - totals[:, :, first : first + block])
        probs_low = probs.astype(jnp.bfloat16)
        prob_grad = jnp.einsum(
            "sqhe,skhe->shqk", grad_part, value_low, preferred_element_type=jnp.float32
        )
        value_grad = value_grad + jnp.einsum(
            "shqk,sqhe->skhe", probs_low, grad_part, preferred_element_type=jnp.float32
        )
        along = jnp.sum(prob_grad * probs, axis=-1, keepdims=True)
        score_grad = (probs * (prob_grad - along)).astype(jnp.bfloat16)
        query_grads.append(
            jnp.einsum("shqk,skhe->sqhe", score_grad, key_low, preferred_element_type=jnp.float32)
            * factor
        )
        key_grad = (
            key_grad
            + jnp.einsum(
                "shqk,sqhe->skhe", score_grad, query_part, preferred_element_type=jnp.float32
            )
            * factor
        )
    return (jnp.concatenate(query_grads, axis=1), key_grad, value_grad)


def local(
    inputs,
    encoded,
    source_lengths,
    query_weight,
    key_weight,
    value_weight,
    output_weight,
    cross_query,
    cross_key,
    cross_value,
    cross_output,
    up_weight,
    down_weight,
    adapter_in,
    adapter_out,
    adapter_bias,
    adapter_shift,
    norm_gains,
    norm_shifts,
    output_grad,
):
    parts = lax.axis_size("tensor")
    place = lax.axis_index("tensor")
    sequences, share, width = inputs.shape
    length = share * parts
    rows = sequences * length
    heads = query_weight.shape[1] // HEAD
    local_width = heads * HEAD
    whole_inputs, whole_encoded = (
        lax.all_gather(inputs, "tensor", axis=1, tiled=True),
        lax.all_gather(encoded, "tensor", axis=1, tiled=True),
    )
    sources = whole_encoded.shape[1]
    flat_inputs = whole_inputs.reshape(rows, width)
    flat_encoded = whole_encoded.reshape(sequences * sources, width)

    def split_heads(values, count):
        return values.astype(jnp.bfloat16).reshape(sequences, count, heads, HEAD)

    def causal(first, block):
        query_pos = first + lax.broadcasted_iota(jnp.int32, (block, length), 0)
        key_pos = lax.broadcasted_iota(jnp.int32, (block, length), 1)
        return (key_pos <= query_pos)[None, None]

    def padded(first, block):
        key_pos = lax.broadcasted_iota(jnp.int32, (sequences, 1, 1, sources), 3)
        return key_pos < source_lengths[:, None, None, None]

    self_query = split_heads(multiply(flat_inputs, query_weight), length)
    self_key = split_heads(multiply(flat_inputs, key_weight), length)
    self_value = split_heads(multiply(flat_inputs, value_weight), length)
    self_context, self_totals = attend(self_query, self_key, self_value, causal)
    self_context_low = self_context.astype(jnp.bfloat16).reshape(rows, local_width)
    self_partial = multiply(self_context_low, output_weight).reshape(sequences, length, width)
    self_full = lax.psum(self_partial.astype(jnp.bfloat16), "tensor").astype(jnp.float32)
    first_full, normed_full, scale_full = layer_norm(
        whole_inputs.astype(jnp.float32) + self_full, norm_gains[0], norm_shifts[0]
    )
    first_low = first_full.astype(jnp.bfloat16)
    first_share = lax.dynamic_slice_in_dim(first_full, place * share, share, 1)
    normed_one = lax.dynamic_slice_in_dim(normed_full, place * share, share, 1)
    scale_one = lax.dynamic_slice_in_dim(scale_full, place * share, share, 1)
    flat_first = first_low.reshape(rows, width)
    cross_q = split_heads(multiply(flat_first, cross_query), length)
    cross_k = split_heads(multiply(flat_encoded, cross_key), sources)
    cross_v = split_heads(multiply(flat_encoded, cross_value), sources)
    cross_context, cross_totals = attend(cross_q, cross_k, cross_v, padded)
    cross_context_low = cross_context.astype(jnp.bfloat16).reshape(rows, local_width)
    cross_partial = multiply(cross_context_low, cross_output).reshape(sequences, length, width)
    cross_share = lax.psum_scatter(
        cross_partial.astype(jnp.bfloat16), "tensor", scatter_dimension=1, tiled=True
    ).astype(jnp.float32)
    second_share, normed_two, scale_two = layer_norm(
        first_share + cross_share, norm_gains[1], norm_shifts[1]
    )
    second_low = lax.all_gather(second_share.astype(jnp.bfloat16), "tensor", axis=1, tiled=True)
    flat_second = second_low.reshape(rows, width)
    hidden = multiply(flat_second, up_weight)
    hidden_low = gelu_tanh(hidden).astype(jnp.bfloat16)
    adapted = multiply(flat_second, adapter_in) + adapter_bias
    adapted_low = gelu_tanh(adapted).astype(jnp.bfloat16)
    branch_partial = multiply(hidden_low, down_weight) + 4.0 * multiply(adapted_low, adapter_out)
    branch_share = lax.psum_scatter(
        branch_partial.reshape(sequences, length, width).astype(jnp.bfloat16),
        "tensor",
        scatter_dimension=1,
        tiled=True,
    ).astype(jnp.float32)
    third_input = second_share + branch_share + 4.0 * adapter_shift
    outcome, normed_three, scale_three = layer_norm(third_input, norm_gains[2], norm_shifts[2])
    grad_three, gain_grad_three, shift_grad_three = norm_back(
        output_grad.astype(jnp.float32), normed_three, scale_three, norm_gains[2]
    )
    shift_grad_adapter = 4.0 * jnp.sum(grad_three, axis=(0, 1))
    branch_grad = lax.all_gather(
        grad_three.astype(jnp.bfloat16), "tensor", axis=1, tiled=True
    ).reshape(rows, width)
    hidden_grad = multiply_by_transpose(branch_grad, down_weight)
    hidden_unused, hidden_pull = jax.vjp(gelu_tanh, hidden)
    hidden_grad_low = hidden_pull(hidden_grad)[0].astype(jnp.bfloat16)
    adapted_grad = 4.0 * multiply_by_transpose(branch_grad, adapter_out)
    adapted_unused, adapted_pull = jax.vjp(gelu_tanh, adapted)
    adapted_grad = adapted_pull(adapted_grad)[0]
    bias_grad = jnp.sum(adapted_grad, axis=0)
    adapted_grad_low = adapted_grad.astype(jnp.bfloat16)
    in_grad = multiply_transposed_left(flat_second, adapted_grad_low)
    out_grad = 4.0 * multiply_transposed_left(adapted_low, branch_grad)
    second_partial = multiply_by_transpose(hidden_grad_low, up_weight) + multiply_by_transpose(
        adapted_grad_low, adapter_in
    )
    second_grad = grad_three + lax.psum_scatter(
        second_partial.reshape(sequences, length, width).astype(jnp.bfloat16),
        "tensor",
        scatter_dimension=1,
        tiled=True,
    ).astype(jnp.float32)
    grad_two, gain_grad_two, shift_grad_two = norm_back(
        second_grad, normed_two, scale_two, norm_gains[1]
    )
    cross_grad = lax.all_gather(
        grad_two.astype(jnp.bfloat16), "tensor", axis=1, tiled=True
    ).reshape(rows, width)
    cross_context_grad = multiply_by_transpose(cross_grad, cross_output).astype(jnp.bfloat16)
    cross_context_grad = cross_context_grad.reshape(sequences, length, heads, HEAD)
    cq_grad, ck_grad, cv_grad = attend_back(
        cross_q, cross_k, cross_v, cross_context_grad, cross_totals, padded
    )
    first_partial = multiply_by_transpose(
        cq_grad.astype(jnp.bfloat16).reshape(rows, local_width), cross_query
    )
    encoded_partial = multiply_by_transpose(
        ck_grad.astype(jnp.bfloat16).reshape(sequences * sources, local_width), cross_key
    ) + multiply_by_transpose(
        cv_grad.astype(jnp.bfloat16).reshape(sequences * sources, local_width), cross_value
    )
    first_back, encoded_share = (
        lax.psum_scatter(
            first_partial.reshape(sequences, length, width).astype(jnp.bfloat16),
            "tensor",
            scatter_dimension=1,
            tiled=True,
        ).astype(jnp.float32),
        lax.psum_scatter(
            encoded_partial.reshape(sequences, sources, width).astype(jnp.bfloat16),
            "tensor",
            scatter_dimension=1,
            tiled=True,
        ).astype(jnp.float32),
    )
    grad_one, gain_grad_one, shift_grad_one = norm_back(
        grad_two + first_back, normed_one, scale_one, norm_gains[0]
    )
    self_grad = lax.all_gather(grad_one.astype(jnp.bfloat16), "tensor", axis=1, tiled=True).reshape(
        rows, width
    )
    self_context_grad = multiply_by_transpose(self_grad, output_weight).astype(jnp.bfloat16)
    self_context_grad = self_context_grad.reshape(sequences, length, heads, HEAD)
    sq_grad, sk_grad, sv_grad = attend_back(
        self_query, self_key, self_value, self_context_grad, self_totals, causal
    )
    input_partial = (
        multiply_by_transpose(sq_grad.astype(jnp.bfloat16).reshape(rows, local_width), query_weight)
        + multiply_by_transpose(sk_grad.astype(jnp.bfloat16).reshape(rows, local_width), key_weight)
        + multiply_by_transpose(
            sv_grad.astype(jnp.bfloat16).reshape(rows, local_width), value_weight
        )
    )
    small_grads = jnp.stack(
        [
            gain_grad_one,
            gain_grad_two,
            gain_grad_three,
            shift_grad_one,
            shift_grad_two,
            shift_grad_three,
            shift_grad_adapter,
        ]
    )
    spread = jnp.broadcast_to(small_grads[:, None, :], (7, parts, width))
    input_back, small_back = (
        lax.psum_scatter(
            input_partial.reshape(sequences, length, width).astype(jnp.bfloat16),
            "tensor",
            scatter_dimension=1,
            tiled=True,
        ).astype(jnp.float32),
        lax.psum_scatter(
            spread.astype(jnp.bfloat16), "tensor", scatter_dimension=1, tiled=True
        ).astype(jnp.float32),
    )
    input_result = (grad_one + input_back).astype(jnp.bfloat16)
    encoded_result = encoded_share.astype(jnp.bfloat16)
    in_total, out_total, bias_total, small_total = (
        lax.psum(in_grad.astype(jnp.bfloat16), "dp").astype(jnp.float32),
        lax.psum(out_grad.astype(jnp.bfloat16), "dp").astype(jnp.float32),
        lax.psum(bias_grad.astype(jnp.bfloat16), "dp").astype(jnp.float32),
        lax.psum(small_back[:, 0].astype(jnp.bfloat16), "dp").astype(jnp.float32),
    )
    return (
        outcome.astype(jnp.bfloat16),
        input_result,
        encoded_result,
        in_total,
        out_total,
        bias_total,
        small_total[6],
        small_total[0:3],
        small_total[3:6],
    )


def solution(mesh):
    placed = (
        P("dp", "tensor", None),
        P("dp", "tensor", None),
        P("dp"),
        P(None, "tensor"),
        P(None, "tensor"),
        P(None, "tensor"),
        P("tensor", None),
        P(None, "tensor"),
        P(None, "tensor"),
        P(None, "tensor"),
        P("tensor", None),
        P(None, "tensor"),
        P("tensor", None),
        P(None, "tensor"),
        P("tensor", None),
        P("tensor"),
        P(),
        P(),
        P(),
        P("dp", "tensor", None),
    )
    return jax.shard_map(
        local,
        mesh=mesh,
        in_specs=placed,
        out_specs=(
            P("dp", "tensor", None),
            P("dp", "tensor", None),
            P("dp", "tensor", None),
            P(None, "tensor"),
            P("tensor", None),
            P("tensor"),
            P(),
            P(),
            P(),
        ),
        check_vma=False,
    )
```

profile of v0, /device:TPU:0, one launch (start us, length us, event | category | flops | bytes accessed | tf_op | source)
XLA Modules:
  0.0 2036.3 jit_solution(15124928660212700898)
XLA Ops:
  10.1 90.2 %all-gather.7.cloned.1.call-done = bf16[4,1024,1024]{2,1,0:T(8,128)(2,1)} async-done(((bf16[4,256,1024]{2,1,0:T(8,128)(2,1)}), bf16[4,1024,1024]{2,1,0:T(8,128)(2,1)}) %all-gather.7.cloned.1.call-update) | async-done | bytes 8388624 | tf_op jit(solution)/shard_map/all_gather | solution.py:144
  148.4 15.6 fusion.37
  164.1 15.4 fusion.1
  179.5 16.1 fusion.36
  310.9 127.3 %all-reduce.6.cloned.1.call-done = bf16[4,1024,1024]{2,1,0:T(8,128)(2,1)} async-done(((bf16[4,1024,1024]{2,1,0:T(8,128)(2,1)}), bf16[4,1024,1024]{2,1,0:T(8,128)(2,1)}) %all-reduce.6.cloned.1.call-update) | async-done | bytes 8388624 | tf_op jit(solution)/shard_map/psum | solution.py:169
  497.3 17.9 fusion.129
  515.2 22.8 %fusion.34 = (f32[4,4,512]{2,1,0:T(4,128)S(1)}, f32[4,4,512]{2,1,0:T(4,128)S(1)}, f32[4,4,512,1024]{3,2,1,0:T(8,128)}) fusion(pred[4,1024]{1,0:T(4,128)(4,1)S(1)} %iota_compare_fusion.2, f32[4,4,512,1024]{3,2,1,0:T(8,128)} %fusion.129, bf16[4,512,4,64]{1,3,2,0:T(8,128)(2,1)S(1)} %copy.157, bf16[4,1024,4,64]{1,3,2,0:T(8,128)(2,1)S(1)} %copy-done.10), kind=kOutput, calls=%fused_computation.64 | convolution fusion | flops 1124057088 | bytes 70324224 | tf_op jit(solution)/shard_map/sqhe,skhe->shqk/dot_general | solution.py:55
  538.1 24.7 %fusion.2 = (f32[4,4,512]{2,1,0:T(4,128)S(1)}, f32[4,4,512]{2,1,0:T(4,128)S(1)}) fusion(f32[4,4,512]{2,1,0:T(4,128)S(1)} %get-tuple-element.25, f32[4,4,512,1024]{3,2,1,0:T(8,128)} %get-tuple-element.68, pred[4,1024]{1,0:T(4,128)(4,1)S(1)} %iota_compare_fusion.2, f32[4,4,512]{2,1,0:T(4,128)S(1)} %get-tuple-element.26, f32[4,4,512,1024]{3,2,1,0:T(8,128)} %fusion.129), kind=kLoop, calls=%fused_computation.26 | loop fusion | flops 67092480 | bytes 67244032 | tf_op jit(solution)/shard_map/reduce_sum | solution.py:66
  597.2 87.2 %reduce-scatter.10.cloned.1.call-done = bf16[4,256,1024]{2,1,0:T(8,128)(2,1)} async-done(((bf16[4,1024,1024]{2,1,0:T(8,128)(2,1)}), bf16[4,256,1024]{2,1,0:T(8,128)(2,1)}) %reduce-scatter.10.cloned.1.call-update) | async-done | bytes 2097168 | tf_op jit(solution)/shard_map/reduce_scatter | solution.py:184
  691.8 87.7 %all-gather.11.cloned.1.call-done = bf16[4,1024,1024]{2,1,0:T(8,128)(2,1)} async-done(((bf16[4,256,1024]{2,1,0:T(8,128)(2,1)}), bf16[4,1024,1024]{2,1,0:T(8,128)(2,1)}) %all-gather.11.cloned.1.call-update) | async-done | bytes 8388624 | tf_op jit(solution)/shard_map/all_gather | solution.py:190
  779.5 16.5 fusion.130
  798.3 18.1 fusion.38
  826.5 85.9 %reduce-scatter.12.cloned.1.call-done = bf16[4,256,1024]{2,1,0:T(8,128)(2,1)} async-done(((bf16[4,1024,1024]{2,1,0:T(8,128)(2,1)}), bf16[4,256,1024]{2,1,0:T(8,128)(2,1)}) %reduce-scatter.12.cloned.1.call-update) | async-done | bytes 2097168 | tf_op jit(solution)/shard_map/reduce_scatter | solution.py:197
  923.1 87.7 %all-gather.13.cloned.1.call-done = bf16[4,1024,1024]{2,1,0:T(8,128)(2,1)} async-done(((bf16[4,256,1024]{2,1,0:T(8,128)(2,1)}), bf16[4,1024,1024]{2,1,0:T(8,128)(2,1)}) %all-gather.13.cloned.1.call-update) | async-done | bytes 8388624 | tf_op jit(solution)/shard_map/all_gather | solution.py:209
  1010.8 33.6 %fusion.43 = f32[4096,1024]{1,0:T(8,128)} fusion(bf16[1024,1024]{1,0:T(8,128)(2,1)} %param.31, f32[4096,1024]{1,0:T(8,128)} %fusion.130, bf16[4096,1024]{1,0:T(8,128)(2,1)} %bitcast.202, bf16[1024,1024]{1,0:T(8,128)(2,1)S(1)} %copy-done), kind=kOutput, calls=%fused_computation.73 | convolution fusion | flops 17263755264 | bytes 46137344 | tf_op jit(solution)/shard_map/dot_general | solution.py:18
  1063.9 86.5 %reduce-scatter.14.cloned.1.call-done = bf16[4,256,1024]{2,1,0:T(8,128)(2,1)} async-done(((bf16[4,1024,1024]{2,1,0:T(8,128)(2,1)}), bf16[4,256,1024]{2,1,0:T(8,128)(2,1)}) %reduce-scatter.14.cloned.1.call-update) | async-done | bytes 2097168 | tf_op jit(solution)/shard_map/reduce_scatter | solution.py:225
  1162.7 87.6 %all-gather.15.cloned.1.call-done = bf16[4,1024,1024]{2,1,0:T(8,128)(2,1)} async-done(((bf16[4,256,1024]{2,1,0:T(8,128)(2,1)}), bf16[4,1024,1024]{2,1,0:T(8,128)(2,1)}) %all-gather.15.cloned.1.call-update) | async-done | bytes 8388624 | tf_op jit(solution)/shard_map/all_gather | solution.py:234
  1285.8 44.0 %multiply_reduce_fusion.3 = (f32[4,4,512]{2,1,0:T(4,128)S(1)}, f32[4,4,512]{2,1,0:T(4,128)S(1)}, f32[4,4,512,1024]{3,2,1,0:T(8,128)}) fusion(f32[4,4,512]{2,1,0:T(4,128)S(1)} %bitcast.221, f32[4,4,512,1024]{3,2,1,0:T(8,128)} %get-tuple-element.68, pred[4,1024]{1,0:T(4,128)(4,1)S(1)} %copy-done.54, f32[4,4,512,1024]{3,2,1,0:T(8,128)} %fusion.131, ...), kind=kOutput, calls=%fused_computation.10 | convolution fusion | flops 1157611520 | bytes 137498624 | tf_op jit(solution)/shard_map/sqhe,skhe->shqk/dot_general | solution.py:92
  1329.8 54.3 %multiply_convert_fusion.3 = (bf16[4,4,512,1024]{3,2,1,0:T(8,128)(2,1)}, bf16[4,4,512,1024]{3,2,1,0:T(8,128)(2,1)}) fusion(f32[4,4,512,1024]{3,2,1,0:T(8,128)} %get-tuple-element.69, f32[4,4,512]{2,1,0:T(4,128)S(1)} %get-tuple-element.21, f32[4,4,512]{2,1,0:T(4,128)S(1)} %bitcast.222, f32[4,4,512,1024]{3,2,1,0:T(8,128)} %get-tuple-element.68, ...), kind=kLoop, calls=%fused_computation.9 | loop fusion | flops 100663296 | bytes 167907328 | tf_op jit(solution)/shard_map/convert_element_type | solution.py:99
  1415.1 85.8 %reduce-scatter.16.cloned.1.call-done = bf16[4,256,1024]{2,1,0:T(8,128)(2,1)} async-done(((bf16[4,1024,1024]{2,1,0:T(8,128)(2,1)}), bf16[4,256,1024]{2,1,0:T(8,128)(2,1)}) %reduce-scatter.16.cloned.1.call-update) | async-done | bytes 2097168 | tf_op jit(solution)/shard_map/reduce_scatter | solution.py:251
  1530.4 71.7 %all-gather.17.cloned.1.call-done = bf16[4,1024,1024]{2,1,0:T(8,128)(2,1)} async-done(((bf16[4,256,1024]{2,1,0:T(8,128)(2,1)}), bf16[4,1024,1024]{2,1,0:T(8,128)(2,1)}) %all-gather.17.cloned.1.call-update) | async-done | bytes 8388624 | tf_op jit(solution)/shard_map/all_gather | solution.py:267
  1618.6 26.2 %multiply_reduce_fusion.1 = (f32[4,4,512]{2,1,0:T(4,128)S(1)}, f32[4,4,512,1024]{3,2,1,0:T(8,128)}) fusion(f32[4,4,512]{2,1,0:T(4,128)S(1)} %bitcast.214, f32[4,4,512,1024]{3,2,1,0:T(8,128)} %get-tuple-element.67, pred[512,1024]{1,0:T(8,128)(4,1)S(1)} %copy-done.9, bf16[4,512,4,64]{1,3,2,0:T(8,128)(2,1)S(1)} %copy.161, bf16[4,1024,4,64]{1,3,2,0:T(8,128)(2,1)} %copy.101), kind=kOutput, calls=%fused_computation.4 | convolution fusion | flops 1115676672 | bytes 70844416 | tf_op jit(solution)/shard_map/sqhe,skhe->shqk/dot_general | solution.py:92
  1644.8 28.1 %multiply_convert_fusion.1 = bf16[4,4,512,1024]{3,2,1,0:T(8,128)(2,1)} fusion(f32[4,4,512,1024]{3,2,1,0:T(8,128)} %get-tuple-element.73, f32[4,4,512]{2,1,0:T(4,128)S(1)} %get-tuple-element.72, f32[4,4,512]{2,1,0:T(4,128)S(1)} %bitcast.215, f32[4,4,512,1024]{3,2,1,0:T(8,128)} %get-tuple-element.67, pred[512,1024]{1,0:T(8,128)(4,1)S(1)} %copy-done.9), kind=kLoop, calls=%fused_computation.3 | loop fusion | flops 50331648 | bytes 84475904 | tf_op jit(solution)/shard_map/convert_element_type | solution.py:99
  1700.4 16.7 fusion.15
  1717.0 25.5 %multiply_reduce_fusion = (f32[4,4,512]{2,1,0:T(4,128)S(1)}, f32[4,4,512,1024]{3,2,1,0:T(8,128)}) fusion(f32[4,4,512]{2,1,0:T(4,128)S(1)} %bitcast.212, f32[4,4,512,1024]{3,2,1,0:T(8,128)} %get-tuple-element.65, pred[512,1024]{1,0:T(8,128)(4,1)S(1)} %copy-done.7, bf16[4,512,4,64]{1,3,2,0:T(8,128)(2,1)} %copy-done.34, bf16[4,1024,4,64]{1,3,2,0:T(8,128)(2,1)S(1)} %copy-done.20), kind=kOutput, calls=%fused_computation.1 | convolution fusion | flops 1115676672 | bytes 70844416 | tf_op jit(solution)/shard_map/sqhe,skhe->shqk/dot_general | solution.py:92
  1742.6 17.2 fusion.60
  1765.2 28.2 %multiply_convert_fusion = bf16[4,4,512,1024]{3,2,1,0:T(8,128)(2,1)} fusion(f32[4,4,512,1024]{3,2,1,0:T(8,128)} %get-tuple-element.71, f32[4,4,512]{2,1,0:T(4,128)S(1)} %get-tuple-element.70, f32[4,4,512]{2,1,0:T(4,128)S(1)} %bitcast.213, f32[4,4,512,1024]{3,2,1,0:T(8,128)} %get-tuple-element.65, pred[512,1024]{1,0:T(8,128)(4,1)S(1)} %copy-done.7), kind=kLoop, calls=%fused_computation | loop fusion | flops 50331648 | bytes 84475904 | tf_op jit(solution)/shard_map/convert_element_type | solution.py:99
  1837.0 16.1 add_convert_fusion.1
  1854.4 16.1 fusion.19
  1870.5 17.9 fusion.62
  1937.6 28.5 %all-reduce.1 = (bf16[128]{0:T(256)(128)(2,1)S(1)}, bf16[7,1024]{1,0:T(8,128)(2,1)S(1)}) all-reduce(bf16[128]{0:T(256)(128)(2,1)S(1)} %copy-done.96, bf16[7,1024]{1,0:T(8,128)(2,1)} %bitcast.247), channel_id=1, replica_groups=mesh['dp'=8,'tensor'=4] {'dp'}, use_global_device_ids=true, to_apply=%region_34.35 | all-reduce | flops 7296 | bytes 29184 | tf_op jit(solution)/shard_map/psum | solution.py:310
  1974.1 55.4 %reduce-scatter.20.cloned.1.call-done = bf16[4,256,1024]{2,1,0:T(8,128)(2,1)} async-done(((bf16[4,1024,1024]{2,1,0:T(8,128)(2,1)}), bf16[4,256,1024]{2,1,0:T(8,128)(2,1)}) %reduce-scatter.20.cloned.1.call-update) | async-done | bytes 2097168 | tf_op jit(solution)/shard_map/reduce_scatter | solution.py:257
  (373 shorter events, 568.2 us)
Async XLA Ops:
  7.2 791.1 %copy-start = (bf16[1024,1024]{1,0:T(8,128)(2,1)S(1)}, bf16[1024,1024]{1,0:T(8,128)(2,1)}, u32[]{:S(2)}) copy-start(bf16[1024,1024]{1,0:T(8,128)(2,1)} %param.32) | copy-start | bytes 6291460
  7.2 93.0 %all-gather.7.cloned.1.call-start = ((), (), s32[]{:S(2)}) async-start(), calls=%async_computation.7 | async-start | bytes 10485760 | tf_op jit(solution)/shard_map/all_gather | solution.py:144
  7.9 259.8 %all-gather.9.cloned.1.call-start = ((), (), s32[]{:S(2)}) async-start(), calls=%async_computation.9 | async-start | bytes 10485760 | tf_op jit(solution)/shard_map/all_gather | solution.py:145
  8.7 429.6 %all-reduce.6.cloned.1.call-start = ((), (), s32[]{:S(2)}) async-start(), calls=%async_computation.8 | async-start | bytes 16777216 | tf_op jit(solution)/shard_map/psum | solution.py:169
  10.0 219.6 %copy-start.6 = (pred[512,1024]{1,0:T(8,128)(4,1)}, pred[512,1024]{1,0:T(8,128)(4,1)S(1)}, u32[]{:S(2)}) copy-start(pred[512,1024]{1,0:T(8,128)(4,1)S(1)} %iota_compare_fusion) | copy-start | bytes 1572868
  164.0 65.6 %copy-start.62 = (f32[4,4,512]{2,1,0:T(4,128)}, f32[4,4,512]{2,1,0:T(4,128)S(1)}, u32[]{:S(2)}) copy-start(f32[4,4,512]{2,1,0:T(4,128)S(1)} %get-tuple-element.64) | copy-start | bytes 98308
  179.5 50.2 %copy-start.76 = (f32[4,4,512]{2,1,0:T(4,128)}, f32[4,4,512]{2,1,0:T(4,128)S(1)}, u32[]{:S(2)}) copy-start(f32[4,4,512]{2,1,0:T(4,128)S(1)} %fusion.1) | copy-start | bytes 98308
  195.6 48.6 %copy-start.60 = (f32[4,4,512]{2,1,0:T(4,128)}, f32[4,4,512]{2,1,0:T(4,128)S(1)}, u32[]{:S(2)}) copy-start(f32[4,4,512]{2,1,0:T(4,128)S(1)} %get-tuple-element.66) | copy-start | bytes 98308
  265.8 418.5 %reduce-scatter.10.cloned.1.call-start = ((), (), s32[]{:S(2)}) async-start(), calls=%async_computation.10 | async-start | bytes 10485760 | tf_op jit(solution)/shard_map/reduce_scatter | solution.py:184
  266.5 310.0 %copy-start.53 = (pred[4,1024]{1,0:T(4,128)(4,1)}, pred[4,1024]{1,0:T(4,128)(4,1)S(1)}, u32[]{:S(2)}) copy-start(pred[4,1024]{1,0:T(4,128)(4,1)S(1)} %iota_compare_fusion.2) | copy-start | bytes 12292
  267.2 187.4 %copy-start.78 = (f32[1,1024]{1,0:T(1,128)}, f32[1,1024]{1,0:T(1,128)S(1)}, u32[]{:S(2)}) copy-start(f32[1,1024]{1,0:T(1,128)S(1)} %get-tuple-element.57) | copy-start | bytes 12292
  597.1 182.4 %all-gather.11.cloned.1.call-start = ((), (), s32[]{:S(2)}) async-start(), calls=%async_computation.11 | async-start | bytes 10485760 | tf_op jit(solution)/shard_map/all_gather | solution.py:190
  691.7 220.6 %reduce-scatter.12.cloned.1.call-start = ((), (), s32[]{:S(2)}) async-start(), calls=%async_computation.12 | async-start | bytes 10485760 | tf_op jit(solution)/shard_map/reduce_scatter | solution.py:197
  825.8 185.0 %all-gather.13.cloned.1.call-start = ((), (), s32[]{:S(2)}) async-start(), calls=%async_computation.13 | async-start | bytes 10485760 | tf_op jit(solution)/shard_map/all_gather | solution.py:209
  923.0 227.3 %reduce-scatter.14.cloned.1.call-start = ((), (), s32[]{:S(2)}) async-start(), calls=%async_computation.14 | async-start | bytes 10485760 | tf_op jit(solution)/shard_map/reduce_scatter | solution.py:225
  1063.8 86.5 %copy-start.15 = (bf16[4,256,1024]{2,1,0:T(8,128)(2,1)S(1)}, bf16[4,256,1024]{2,1,0:T(8,128)(2,1)}, u32[]{:S(2)}) copy-start(bf16[4,256,1024]{2,1,0:T(8,128)(2,1)} %param.39) | copy-start | bytes 6291460
  1063.8 86.5 %copy-start.90 = (f32[1,1024]{1,0:T(1,128)S(1)}, f32[1,1024]{1,0:T(1,128)}, u32[]{:S(2)}) copy-start(f32[1,1024]{1,0:T(1,128)} %get-tuple-element.59) | copy-start | bytes 12292
  1063.9 186.4 %all-gather.15.cloned.1.call-start = ((), (), s32[]{:S(2)}) async-start(), calls=%async_computation.15 | async-start | bytes 10485760 | tf_op jit(solution)/shard_map/all_gather | solution.py:234
  1160.3 90.0 %copy-start.42 = (bf16[256,1024]{1,0:T(8,128)(2,1)S(1)}, bf16[256,1024]{1,0:T(8,128)(2,1)}, u32[]{:S(2)}) copy-start(bf16[256,1024]{1,0:T(8,128)(2,1)} %param.30) | copy-start | bytes 1572868
  1162.5 338.4 %reduce-scatter.16.cloned.1.call-start = ((), (), s32[]{:S(2)}) async-start(), calls=%async_computation.16 | async-start | bytes 10485760 | tf_op jit(solution)/shard_map/reduce_scatter | solution.py:251
  1162.7 167.1 %copy-start.64 = (f32[2,8,512]{2,1,0:T(8,128)}, f32[2,8,512]{2,1,0:T(8,128)S(1)}, u32[]{:S(2)}) copy-start(f32[2,8,512]{2,1,0:T(8,128)S(1)} %get-tuple-element.83) | copy-start | bytes 98308
  1162.7 167.1 %copy-start.66 = (f32[2,8,512]{2,1,0:T(8,128)}, f32[2,8,512]{2,1,0:T(8,128)S(1)}, u32[]{:S(2)}) copy-start(f32[2,8,512]{2,1,0:T(8,128)S(1)} %get-tuple-element.82) | copy-start | bytes 98308
  1329.8 54.3 %copy-start.11 = (bf16[4,1024,4,64]{1,3,2,0:T(8,128)(2,1)S(1)}, bf16[4,1024,4,64]{1,3,2,0:T(8,128)(2,1)}, u32[]{:S(2)}) copy-start(bf16[4,1024,4,64]{1,3,2,0:T(8,128)(2,1)} %copy.110) | copy-start | bytes 6291460
  1414.3 86.6 %copy-start.79 = (f32[1,1024]{1,0:T(1,128)S(1)}, f32[1,1024]{1,0:T(1,128)}, u32[]{:S(2)}) copy-start(f32[1,1024]{1,0:T(1,128)} %copy-done.78) | copy-start | bytes 12292
  1414.3 187.8 %all-gather.17.cloned.1.call-start = ((), (), s32[]{:S(2)}) async-start(), calls=%async_computation.17 | async-start | bytes 10485760 | tf_op jit(solution)/shard_map/all_gather | solution.py:267
  1415.1 93.4 %copy-start.83 = (f32[4,256]{1,0:T(4,128)}, f32[4,256]{1,0:T(4,128)S(1)}, u32[]{:S(2)}) copy-start(f32[4,256]{1,0:T(4,128)S(1)} %constant_dynamic-slice_fusion) | copy-start | bytes 12292
  1514.4 419.7 %all-reduce.8.cloned.1.call-start = ((), (), s32[]{:S(2)}) async-start(), calls=%async_computation.21 | async-start | bytes 1048576 | tf_op jit(solution)/shard_map/psum | solution.py:308
  1522.2 79.9 %copy-start.46 = (bf16[256,1024]{1,0:T(8,128)(2,1)S(1)}, bf16[256,1024]{1,0:T(8,128)(2,1)}, u32[]{:S(2)}) copy-start(bf16[256,1024]{1,0:T(8,128)(2,1)} %param.26) | copy-start | bytes 1572868
  1529.4 408.2 %reduce-scatter.22.cloned.1.call-start = ((), (), s32[]{:S(2)}) async-start(), calls=%async_computation.20 | async-start | bytes 81920
  1530.3 437.6 %reduce-scatter.18.cloned.1.call-start = ((), (), s32[]{:S(2)}) async-start(), calls=%async_computation.18 | async-start | bytes 10485760 | tf_op jit(solution)/shard_map/reduce_scatter | solution.py:295
  1853.2 176.3 %reduce-scatter.20.cloned.1.call-start = ((), (), s32[]{:S(2)}) async-start(), calls=%async_computation.19 | async-start | bytes 10485760 | tf_op jit(solution)/shard_map/reduce_scatter | solution.py:257
  1967.2 62.2 %copy-start.1 = (bf16[1024,1024]{1,0:T(8,128)(2,1)S(1)}, bf16[1024,1024]{1,0:T(8,128)(2,1)}, u32[]{:S(2)}) copy-start(bf16[1024,1024]{1,0:T(8,128)(2,1)} %param.32) | copy-start | bytes 6291460
  (88 other events, 944.8 us)
Sparse Core Ops, SparseCore 0:
  9.9 90.2 all-gather.6
  102.1 87.5 all-gather.8
  266.0 172.2 all-reduce.5
  597.2 87.1 reduce-scatter.9
  691.9 87.5 all-gather.10
  825.9 86.4 reduce-scatter.11
  923.1 87.5 all-gather.12
  1064.0 86.3 reduce-scatter.13
  1162.7 87.5 all-gather.14
  1414.4 86.4 reduce-scatter.15
  1514.5 87.5 all-gather.16
  1604.4 56.2 all-reduce.7
  1663.5 22.7 reduce-scatter.21
  1853.3 86.2 reduce-scatter.17
  1943.0 86.4 reduce-scatter.19
where the time goes:
time: 2040 us
  waiting for transfers between devices  955 us (47%)
  matrix products  628 us (31%)
  other arithmetic  247 us (12%)
  local copies, waits for them, and re-layouts  163 us (8%)
  blocking collectives  28.5 us (1%)
    psum x1, waiting for transfers between devices, local(): lax.psum(self_partial.astype(jnp.bfloat16), 'tensor').astype(jnp.float32)  127 us
    dot_general x11, matrix products, multiply_by_transpose(): lax.dot_general(left, right, (((1,), (1,)), ((), ())), preferred_element_...  124 us
    convert_element_type x3, other arithmetic, attend_back(): score_grad = (probs * (prob_grad - along)).astype(jnp.bfloat16)  111 us
    dot_general x4, matrix products, attend_back(): jnp.einsum('sqhe,skhe->shqk', grad_part, value_low, preferred_element_typ...  110 us
    dot_general x12, matrix products, multiply(): return jnp.dot(left, right, preferred_element_type=jnp.float32)  98.2 us
    all_gather x1, waiting for transfers between devices, local(): lax.all_gather(inputs, 'tensor', axis=1, tiled=True)  90.2 us
    all_gather x1, waiting for transfers between devices, local(): lax.all_gather(grad_three.astype(jnp.bfloat16), 'tensor', axis=1, tiled=T...  87.7 us
    all_gather x1, waiting for transfers between devices, local(): lax.all_gather(second_share.astype(jnp.bfloat16), 'tensor', axis=1, tiled...  87.7 us
  transfers between devices with their start and end apart: 15, of which 11 were waited for; matrix products, arithmetic and copies ran while one was open for 28% of the time, Pallas kernels for 0%

commit v1 on v0

--- a/solution.py
+++ b/solution.py
@@ -1,9 +1,691 @@
+import functools
 import jax
 import jax.numpy as jnp
 from jax import lax
+from jax.experimental import pallas as pl
+from jax.experimental.pallas import tpu as pltpu
 from jax.sharding import PartitionSpec as P
 
 HEAD = 64
+F32 = jnp.float32
+BF16 = jnp.bfloat16
+LOG2E = 1.4426950408889634
+LN2 = 0.6931471805599453
+VMEM_LIMIT = 60 * 2**20
+ROWS = 256
+
+
+def nn(left, right):
+    return lax.dot_general(left, right, (((1,), (0,)), ((), ())), preferred_element_type=F32)
+
+
+def nt(left, right):
+    return lax.dot_general(left, right, (((1,), (1,)), ((), ())), preferred_element_type=F32)
+
+
+def tn(left, right):
+    return lax.dot_general(left, right, (((0,), (0,)), ((), ())), preferred_element_type=F32)
+
+
+def norm_rows(values):
+    center = values - jnp.mean(values, axis=-1, keepdims=True)
+    scale = lax.rsqrt(jnp.mean(center * center, axis=-1, keepdims=True) + 1e-05)
+    return center * scale, scale
+
+
+def norm_back_rows(grad, normed, scale, gain):
+    inner = grad * gain
+    middle = jnp.mean(inner, axis=-1, keepdims=True)
+    along = jnp.mean(inner * normed, axis=-1, keepdims=True)
+    return scale * (inner - middle - normed * along)
+
+
+def gelu_and_slope(v):
+    root = 0.7978845608028654
+    square = v * v
+    t = jnp.tanh(v * (root + (root * 0.044715) * square))
+    half = 0.5 + 0.5 * t
+    slope = half + (v * half) * (1.0 - t) * (root + (3.0 * root * 0.044715) * square)
+    return v * half, slope
+
+
+def attend_kernel(causal, first, *refs):
+    refs = list(refs)
+    length_ref = None if causal else refs.pop(0)
+    xq_ref = refs.pop(0)
+    xkv_ref = xq_ref if causal else refs.pop(0)
+    pieces = [refs.pop(0) for _ in range(4)]
+    if not first:
+        refs = refs[5:]
+    e_ref, hd_ref, il_ref, ctx_ref, wf_ref, qkv = refs
+    step = pl.program_id(0)
+    span = xq_ref.shape[0]
+    sources = xkv_ref.shape[0]
+    part = pieces[0].shape[2]
+
+    @pl.when(step == 0)
+    def _():
+        for t in range(4):
+            for m in range(4):
+                wf_ref[m, t * part : (t + 1) * part, :] = pieces[t][0, m]
+        qkv[0] = (nt(wf_ref[0], xq_ref[...]) * (LOG2E * HEAD**-0.5)).astype(BF16)
+        qkv[1] = nt(wf_ref[1], xkv_ref[...]).astype(BF16)
+        qkv[2] = nt(wf_ref[2], xkv_ref[...]).astype(BF16)
+
+    pair = pl.ds(pl.multiple_of(step * 128, 128), 128)
+    q2, k2, v2 = qkv[0, pair, :], qkv[1, pair, :], qkv[2, pair, :]
+    hd_ref[0], hd_ref[1], hd_ref[2] = q2, k2, v2
+    block = min(512, span)
+    for i in range(span // block):
+        n = (i + 1) * block if causal else sources
+        cols = slice(i * block, (i + 1) * block)
+        scores = [
+            tn(k2[h * 64 : h * 64 + 64, :n], q2[h * 64 : h * 64 + 64, cols]) for h in range(2)
+        ]
+        contexts = []
+        for h in range(2):
+            s = scores[h]
+            if causal:
+                key = lax.broadcasted_iota(jnp.int32, (block, block), 0)
+                query = lax.broadcasted_iota(jnp.int32, (block, block), 1)
+                tail = jnp.where(key <= query, s[n - block :], -1e9)
+                s = jnp.concatenate([s[: n - block], tail], axis=0) if n > block else tail
+            else:
+                key = lax.broadcasted_iota(jnp.int32, (n, block), 0)
+                s = jnp.where(key < length_ref[0], s, -1e9)
+            e = jnp.exp2(s - jnp.max(s, axis=0, keepdims=True))
+            inverse = 1.0 / jnp.sum(e, axis=0, keepdims=True)
+            low = e.astype(BF16)
+            e_ref[h, :n, cols] = low
+            il_ref[h, :, cols] = inverse
+            contexts.append((nn(v2[h * 64 : h * 64 + 64, :n], low) * inverse).astype(BF16))
+        joined = jnp.concatenate(contexts, axis=0)
+        hd_ref[3, :, cols] = joined
+        ctx_ref[cols, :] = joined.T
+
+
+def attend_slot(slot, length, xq, xkv, pieces, before):
+    causal = xkv is None
+    span, width = xq.shape
+    sources = span if causal else xkv.shape[0]
+    heads = width // HEAD
+    part = pieces[0][0].shape[2]
+    first = before is None
+    whole = lambda shape: pl.BlockSpec(shape, lambda j: (0,) * len(shape), pipeline_mode=pl.Buffered(1))
+    operands, specs = [], []
+    if not causal:
+        operands.append(length)
+        specs.append(pl.BlockSpec(memory_space=pltpu.SMEM))
+    operands.append(xq)
+    specs.append(whole((span, width)))
+    if not causal:
+        operands.append(xkv)
+        specs.append(whole((sources, width)))
+    for array, index in pieces:
+        operands.append(array)
+        specs.append(
+            pl.BlockSpec(
+                (1, 4, part, width), lambda j, index=index: (index, 0, 0, 0), pipeline_mode=pl.Buffered(1)
+            )
+        )
+    aliases = {}
+    if not first:
+        for n, buffer in enumerate(before):
+            aliases[len(operands)] = n
+            operands.append(buffer)
+            specs.append(pl.BlockSpec(memory_space=pl.ANY))
+    out_shape = (
+        jax.ShapeDtypeStruct((heads, sources, span), BF16),
+        jax.ShapeDtypeStruct((4, width, span), BF16),
+        jax.ShapeDtypeStruct((heads, 1, span), F32),
+        jax.ShapeDtypeStruct((span, width), BF16),
+        jax.ShapeDtypeStruct((4, width, width), BF16),
+    )
+    out_specs = (
+        pl.BlockSpec((2, sources, span), lambda j: (2 * slot + j, 0, 0)),
+        pl.BlockSpec((4, 128, span), lambda j: (0, 2 * slot + j, 0)),
+        pl.BlockSpec((2, 1, span), lambda j: (2 * slot + j, 0, 0)),
+        pl.BlockSpec((span, 128), lambda j: (0, 2 * slot + j)),
+        pl.BlockSpec((4, 4 * part, width), lambda j: (0, slot, 0)),
+    )
+    return pl.pallas_call(
+        functools.partial(attend_kernel, causal, first),
+        grid=(2,),
+        in_specs=specs,
+        out_specs=out_specs,
+        out_shape=out_shape,
+        scratch_shapes=[pltpu.VMEM((3, 4 * part, max(span, sources)), BF16)],
+        input_output_aliases=aliases,
+        compiler_params=pltpu.CompilerParams(vmem_limit_bytes=VMEM_LIMIT),
+        cost_estimate=pl.CostEstimate(
+            flops=12 * 10**9, bytes_accessed=16 * 2**20, transcendentals=4 * span * sources
+        ),
+        name="self_attend" if causal else "cross_attend",
+    )(*operands)
+
+
+def out_norm_kernel(ctx_ref, wo_ref, x_ref, gain_ref, shift_ref, low_ref, n_ref, r_ref):
+    total = nn(ctx_ref[...], wo_ref[0]) + x_ref[...].astype(F32)
+    normed, scale = norm_rows(total)
+    low_ref[...] = (normed * gain_ref[...] + shift_ref[...]).astype(BF16)
+    n_ref[...] = normed.astype(BF16)
+    r_ref[...] = scale
+
+
+def out_norm(ctx, weights, residual, gain, shift):
+    span, width = ctx.shape
+    rows = lambda w: pl.BlockSpec((ROWS, w), lambda i: (i, 0))
+    line = pl.BlockSpec((1, width), lambda i: (0, 0))
+    return pl.pallas_call(
+        out_norm_kernel,
+        grid=(span // ROWS,),
+        in_specs=[
+            rows(width),
+            pl.BlockSpec((1, width, width), lambda i: (3, 0, 0), pipeline_mode=pl.Buffered(1)),
+            rows(width),
+            line,
+            line,
+        ],
+        out_specs=(rows(width), rows(width), rows(1)),
+        out_shape=(
+            jax.ShapeDtypeStruct((span, width), BF16),
+            jax.ShapeDtypeStruct((span, width), BF16),
+            jax.ShapeDtypeStruct((span, 1), F32),
+        ),
+        compiler_params=pltpu.CompilerParams(vmem_limit_bytes=VMEM_LIMIT),
+        cost_estimate=pl.CostEstimate(
+            flops=2 * span * width * width, bytes_accessed=10 * 2**20, transcendentals=0
+        ),
+        name="out_norm",
+    )(ctx, weights, residual, gain, shift)
+
+
+def feed_kernel(first, units, extra, *refs):
+    refs = list(refs)
+    x_ref, bias_ref = refs[:2]
+    pieces = refs[2:6]
+    refs = refs[6:]
+    acc_in = None
+    if not first:
+        acc_in = refs[0]
+        refs = refs[8:]
+    acc_ref, gp_ref, gpa_ref, alow_ref, up_ref, down_ref, ain_ref, aout_ref = refs
+
+    @pl.when(pl.program_id(0) == 0)
+    def _():
+        for t in range(4):
+            piece = pieces[t]
+            up_ref[t * units : (t + 1) * units, :] = piece[0, :units]
+            down_ref[t * units : (t + 1) * units, :] = piece[0, units : 2 * units]
+            ain_ref[t * extra : (t + 1) * extra, :] = piece[0, 2 * units : 2 * units + extra]
+            aout_ref[t * extra : (t + 1) * extra, :] = piece[0, 2 * units + extra :]
+
+    x = x_ref[...]
+    a, slope = gelu_and_slope(nt(x, ain_ref[...]) + bias_ref[...])
+    a_low = a.astype(BF16)
+    alow_ref[...] = a_low
+    gpa_ref[...] = slope.astype(BF16)
+    total = 4.0 * nn(a_low, aout_ref[...])
+    if not first:
+        total = total + acc_in[...]
+    for t in range(4):
+        part = slice(t * units, (t + 1) * units)
+        h, slope = gelu_and_slope(nt(x, up_ref[part, :]))
+        gp_ref[:, part] = slope.astype(BF16)
+        total = total + nn(h.astype(BF16), down_ref[part, :])
+    acc_ref[...] = total
+
+
+def feed_slot(slot, x, bias, pieces, before, units, extra):
+    span, width = x.shape
+    first = before is None
+    rows = lambda w: pl.BlockSpec((ROWS, w), lambda i: (i, 0))
+    operands = [x, bias]
+    specs = [rows(width), pl.BlockSpec((1, 4 * extra), lambda i: (0, 0))]
+    tall = 2 * units + 2 * extra
+    for array, index in pieces:
+        operands.append(array)
+        specs.append(
+            pl.BlockSpec((1, tall, width), lambda i, index=index: (index, 0, 0), pipeline_mode=pl.Buffered(1))
+        )
+    aliases = {}
+    if not first:
+        for n, buffer in enumerate(before):
+            aliases[len(operands)] = n
+            operands.append(buffer)
+            specs.append(rows(width) if n == 0 else pl.BlockSpec(memory_space=pl.ANY))
+    out_shape = (
+        jax.ShapeDtypeStruct((span, width), F32),
+        jax.ShapeDtypeStruct((span, 16 * units), BF16),
+        jax.ShapeDtypeStruct((span, 16 * extra), BF16),
+        jax.ShapeDtypeStruct((span, 16 * extra), BF16),
+        jax.ShapeDtypeStruct((16 * units, width), BF16),
+        jax.ShapeDtypeStruct((16 * units, width), BF16),
+        jax.ShapeDtypeStruct((16 * extra, width), BF16),
+        jax.ShapeDtypeStruct((16 * extra, width), BF16),
+    )
+    out_specs = (
+        rows(width),
+        pl.BlockSpec((ROWS, 4 * units), lambda i: (i, slot)),
+        pl.BlockSpec((ROWS, 4 * extra), lambda i: (i, slot)),
+        pl.BlockSpec((ROWS, 4 * extra), lambda i: (i, slot)),
+        pl.BlockSpec((4 * units, width), lambda i: (slot, 0)),
+        pl.BlockSpec((4 * units, width), lambda i: (slot, 0)),
+        pl.BlockSpec((4 * extra, width), lambda i: (slot, 0)),
+        pl.BlockSpec((4 * extra, width), lambda i: (slot, 0)),
+    )
+    return pl.pallas_call(
+        functools.partial(feed_kernel, first, units, extra),
+        grid=(span // ROWS,),
+        in_specs=specs,
+        out_specs=out_specs,
+        out_shape=out_shape,
+        input_output_aliases=aliases,
+        compiler_params=pltpu.CompilerParams(vmem_limit_bytes=VMEM_LIMIT),
+        cost_estimate=pl.CostEstimate(
+            flops=7 * 10**9, bytes_accessed=20 * 2**20, transcendentals=4 * span * units
+        ),
+        name="feed",
+    )(*operands)
+
+
+def last_norm_kernel(acc_ref, x_ref, extra_ref, gain_ref, shift_ref, grad_ref, out_ref, low_ref, sum_ref):
+    total = acc_ref[...] + x_ref[...].astype(F32) + 4.0 * extra_ref[...]
+    normed, scale = norm_rows(total)
+    out_ref[...] = (normed * gain_ref[...] + shift_ref[...]).astype(BF16)
+    grad = grad_ref[...].astype(F32)
+    back = norm_back_rows(grad, normed, scale, gain_ref[...])
+    low_ref[...] = back.astype(BF16)
+
+    @pl.when(pl.program_id(0) == 0)
+    def _():
+        sum_ref[...] = jnp.zeros_like(sum_ref)
+
+    sum_ref[0:1, :] += jnp.sum(grad * normed, axis=0, keepdims=True)
+    sum_ref[1:2, :] += jnp.sum(grad, axis=0, keepdims=True)
+    sum_ref[2:3, :] += 4.0 * jnp.sum(back, axis=0, keepdims=True)
+
+
+def last_norm(acc, second, extra_shift, gain, shift, grad):
+    span, width = acc.shape
+    rows = pl.BlockSpec((ROWS, width), lambda i: (i, 0))
+    line = pl.BlockSpec((1, width), lambda i: (0, 0))
+    return pl.pallas_call(
+        last_norm_kernel,
+        grid=(span // ROWS,),
+        in_specs=[rows, rows, line, line, line, rows],
+        out_specs=(rows, rows, pl.BlockSpec((8, width), lambda i: (0, 0))),
+        out_shape=(
+            jax.ShapeDtypeStruct((span, width), BF16),
+            jax.ShapeDtypeStruct((span, width), BF16),
+            jax.ShapeDtypeStruct((8, width), F32),
+        ),
+        compiler_params=pltpu.CompilerParams(vmem_limit_bytes=VMEM_LIMIT),
+        cost_estimate=pl.CostEstimate(flops=30 * 2**20, bytes_accessed=12 * 2**20, transcendentals=0),
+        name="last_norm",
+    )(acc, second, extra_shift, gain, shift, grad)
+
+
+def feed_back_kernel(
+    g_ref, up_ref, down_ref, gp_ref, ain_ref, aout_ref, gpa_ref, alow_ref, x_ref, n_ref, r_ref, gain_ref,
+    low_ref, ing_ref, outg_ref, bias_ref, sum_ref, acc,
+):
+    step = pl.program_id(0)
+    span = g_ref.shape[0]
+
+    @pl.when(step == 0)
+    def _():
+        g = g_ref[...]
+        a = 4.0 * nt(g, aout_ref[...]) * gpa_ref[...].astype(F32)
+        bias_ref[...] = jnp.sum(a, axis=0, keepdims=True)
+        a_low = a.astype(BF16)
+        ing_ref[...] = tn(a_low, x_ref[...]).astype(BF16)
+        outg_ref[...] = (4.0 * tn(alow_ref[...], g)).astype(BF16)
+        acc[...] = nn(a_low, ain_ref[...]) + g.astype(F32)
+
+    for i in range(span // ROWS):
+        rows = slice(i * ROWS, (i + 1) * ROWS)
+        h = (nt(g_ref[rows, :], down_ref[...]) * gp_ref[rows, :].astype(F32)).astype(BF16)
+        acc[rows, :] += nn(h, up_ref[...])
+
+    @pl.when(step == pl.num_programs(0) - 1)
+    def _():
+        sum_ref[...] = jnp.zeros_like(sum_ref)
+        for i in range(span // ROWS):
+            rows = slice(i * ROWS, (i + 1) * ROWS)
+            grad = acc[rows, :]
+            normed = n_ref[rows, :].astype(F32)
+            back = norm_back_rows(grad, normed, r_ref[rows, :], gain_ref[...])
+            low_ref[rows, :] = back.astype(BF16)
+            sum_ref[0:1, :] += jnp.sum(grad * normed, axis=0, keepdims=True)
+            sum_ref[1:2, :] += jnp.sum(grad, axis=0, keepdims=True)
+
+
+def feed_back(g, kept, x, normed, scale, gain):
+    _, gp, gpa, alow, up, down, ain, aout = kept
+    span, width = g.shape
+    units, extra = up.shape[0], ain.shape[0]
+    chunk = min(512, units)
+    whole = lambda a: pl.BlockSpec(a.shape, lambda j: (0,) * a.ndim, pipeline_mode=pl.Buffered(1))
+    out_shape = (
+        jax.ShapeDtypeStruct((span, width), BF16),
+        jax.ShapeDtypeStruct((extra, width), BF16),
+        jax.ShapeDtypeStruct((extra, width), BF16),
+        jax.ShapeDtypeStruct((1, extra), F32),
+        jax.ShapeDtypeStruct((8, width), F32),
+    )
+    return pl.pallas_call(
+        feed_back_kernel,
+        grid=(units // chunk,),
+        in_specs=[
+            whole(g),
+            pl.BlockSpec((chunk, width), lambda j: (j, 0)),
+            pl.BlockSpec((chunk, width), lambda j: (j, 0)),
+            pl.BlockSpec((span, chunk), lambda j: (0, j)),
+            whole(ain),
+            whole(aout),
+            whole(gpa),
+            whole(alow),
+            whole(x),
+            whole(normed),
+            whole(scale),
+            whole(gain),
+        ],
+        out_specs=tuple(pl.BlockSpec(s.shape, lambda j: (0, 0)) for s in out_shape),
+        out_shape=out_shape,
+        scratch_shapes=[pltpu.VMEM((span, width), F32)],
+        compiler_params=pltpu.CompilerParams(vmem_limit_bytes=VMEM_LIMIT),
+        cost_estimate=pl.CostEstimate(
+            flops=4 * span * width * units + 8 * span * width * extra,
+            bytes_accessed=40 * 2**20,
+            transcendentals=0,
+        ),
+        name="feed_back",
+    )(g, up, down, gp, ain, aout, gpa, alow, x, normed, scale, gain)
+
+
+def attention_back_kernel(causal, *refs):
+    refs = list(refs)
+    g_ref, wf_ref, e_ref, hd_ref, il_ref = refs[:5]
+    refs = refs[5:]
+    if causal:
+        out_ref, ct, dq, dk, dv = refs
+    else:
+        n_ref, r_ref, gain_ref, low_ref, enc_ref, sum_ref, ct, dq, dk, dv = refs
+    step = pl.program_id(0)
+    span = g_ref.shape[0]
+    sources = e_ref.shape[1]
+
+    @pl.when(step == 0)
+    def _():
+        ct[...] = nt(wf_ref[3], g_ref[...]).astype(BF16)
+
+    pair = pl.ds(pl.multiple_of(step * 128, 128), 128)
+    c2 = ct[pair, :]
+    block = min(512, span)
+    heads = [slice(h * 64, h * 64 + 64) for h in range(2)]
+    scaled, dots = [], []
+    for h in range(2):
+        c = c2[heads[h], :].astype(F32) * il_ref[h]
+        dots.append(jnp.sum(c * hd_ref[3, heads[h], :].astype(F32), axis=0, keepdims=True))
+        scaled.append(c.astype(BF16))
+    sums_k, sums_v = [None, None], [None, None]
+    for i in reversed(range(span // block)):
+        n = (i + 1) * block if causal else sources
+        cols = slice(i * block, (i + 1) * block)
+        grads = [tn(hd_ref[2, heads[h], :n], scaled[h][:, cols]) for h in range(2)]
+        queries = []
+        for h in range(2):
+            e = e_ref[h, :n, cols]
+            ds = (e.astype(F32) * (grads[h] - dots[h][:, cols])).astype(BF16)
+            queries.append((nn(hd_ref[1, heads[h], :n], ds) * HEAD**-0.5).astype(BF16))
+            gk = nn(ds, hd_ref[0, heads[h], cols].T)
+            gv = nn(e, scaled[h][:, cols].T)
+            if sums_k[h] is None:
+                sums_k[h], sums_v[h] = gk, gv
+            elif n == sums_k[h].shape[0]:
+                sums_k[h], sums_v[h] = sums_k[h] + gk, sums_v[h] + gv
+            else:
+                sums_k[h] = jnp.concatenate([sums_k[h][:n] + gk, sums_k[h][n:]], axis=0)
+                sums_v[h] = jnp.concatenate([sums_v[h][:n] + gv, sums_v[h][n:]], axis=0)
+        dq[cols, pair] = jnp.concatenate(queries, axis=0).T
+    dk[:, pair] = (jnp.concatenate(sums_k, axis=1) * LN2).astype(BF16)
+    dv[:, pair] = jnp.concatenate(sums_v, axis=1).astype(BF16)
+
+    @pl.when(step == pl.num_programs(0) - 1)
+    def _():
+        if not causal:
+            sum_ref[...] = jnp.zeros_like(sum_ref)
+        for i in range(span // ROWS):
+            rows = slice(i * ROWS, (i + 1) * ROWS)
+            from_q = nn(dq[rows, :], wf_ref[0]) + g_ref[rows, :].astype(F32)
+            from_kv = nn(dk[rows, :], wf_ref[1]) + nn(dv[rows, :], wf_ref[2])
+            if causal:
+                out_ref[rows, :] = (from_q + from_kv).astype(BF16)
+            else:
+                enc_ref[rows, :] = from_kv.astype(BF16)
+                normed = n_ref[rows, :].astype(F32)
+                back = norm_back_rows(from_q, normed, r_ref[rows, :], gain_ref[...])
+                low_ref[rows, :] = back.astype(BF16)
+                sum_ref[0:1, :] += jnp.sum(from_q * normed, axis=0, keepdims=True)
+                sum_ref[1:2, :] += jnp.sum(from_q, axis=0, keepdims=True)
+
+
+def attention_back(g, kept, norm):
+    e, hd, il, _, wf = kept
+    causal = norm is None
+    span, width = g.shape
+    heads, sources, _ = e.shape
+    whole = lambda a: pl.BlockSpec(a.shape, lambda j: (0,) * a.ndim, pipeline_mode=pl.Buffered(1))
+    operands = [g, wf, e, hd, il]
+    specs = [
+        whole(g),
+        whole(wf),
+        pl.BlockSpec((2, sources, span), lambda j: (j, 0, 0)),
+        pl.BlockSpec((4, 128, span), lambda j: (0, j, 0)),
+        pl.BlockSpec((2, 1, span), lambda j: (j, 0, 0)),
+    ]
+    low = jax.ShapeDtypeStruct((span, width), BF16)
+    if causal:
+        out_shape = (low,)
+    else:
+        operands += list(norm)
+        specs += [whole(a) for a in norm]
+        out_shape = (low, jax.ShapeDtypeStruct((sources, width), BF16), jax.ShapeDtypeStruct((8, width), F32))
+    return pl.pallas_call(
+        functools.partial(attention_back_kernel, causal),
+        grid=(heads // 2,),
+        in_specs=specs,
+        out_specs=tuple(
+            pl.BlockSpec(s.shape, lambda j: (0, 0), pipeline_mode=pl.Buffered(1)) for s in out_shape
+        ),
+        out_shape=out_shape,
+        scratch_shapes=[
+            pltpu.VMEM((width, span), BF16),
+            pltpu.VMEM((span, width), BF16),
+            pltpu.VMEM((sources, width), BF16),
+            pltpu.VMEM((sources, width), BF16),
+        ],
+        compiler_params=pltpu.CompilerParams(vmem_limit_bytes=VMEM_LIMIT),
+        cost_estimate=pl.CostEstimate(
+            flops=40 * 10**9, bytes_accessed=60 * 2**20, transcendentals=0
+        ),
+        name="self_back" if causal else "cross_back",
+    )(*operands)
+
+
+def over(axis, bit):
+    size = lax.axis_size(axis)
+    pairs = [(i, i ^ bit) for i in range(size)]
+    return lambda values: lax.ppermute(values, axis, pairs)
+
+
+def swap_positions(values, place):
+    received = []
+    for k in (1, 2, 3):
+        block = lax.dynamic_index_in_dim(values, place ^ k, 0, keepdims=True)
+        received.append(over("tensor", k)(block))
+    for k in (1, 2, 3):
+        values = lax.dynamic_update_index_in_dim(values, received[k - 1], place ^ k, 0)
+    return values
+
+
+def spread_pieces(own):
+    slots = []
+    for k in (1, 2, 3):
+        here = over("tensor", k)(own)
+        far = over("dp", 2)(here)
+        slots.append([here, over("dp", 1)(here), far, over("dp", 1)(far)])
+    return slots
+
+
+def whole_sequences(
+    inputs,
+    encoded,
+    source_lengths,
+    query_weight,
+    key_weight,
+    value_weight,
+    output_weight,
+    cross_query,
+    cross_key,
+    cross_value,
+    cross_output,
+    up_weight,
+    down_weight,
+    adapter_in,
+    adapter_out,
+    adapter_bias,
+    adapter_shift,
+    norm_gains,
+    norm_shifts,
+    output_grad,
+):
+    place = lax.axis_index("tensor")
+    turn = lax.axis_index("dp") % 4
+    _, share, width = inputs.shape
+    span = 4 * share
+    units, extra = up_weight.shape[1] // 4, adapter_in.shape[1] // 4
+
+    def cut(weight, transpose):
+        return (weight.T if transpose else weight).reshape(4, -1, width)
+
+    x = swap_positions(inputs, place).reshape(span, width)
+    self_own = jnp.stack(
+        [cut(query_weight, True), cut(key_weight, True), cut(value_weight, True), cut(output_weight, False)],
+        axis=1,
+    )
+    cross_own = jnp.stack(
+        [cut(cross_query, True), cut(cross_key, True), cut(cross_value, True), cut(cross_output, False)],
+        axis=1,
+    )
+    feed_own = jnp.concatenate(
+        [cut(up_weight, True), cut(down_weight, False), cut(adapter_in, True), cut(adapter_out, False)],
+        axis=1,
+    )
+    pick = lambda packed: lax.dynamic_index_in_dim(packed, turn, 0, keepdims=True)
+    self_slots = spread_pieces(pick(self_own))
+    source = swap_positions(encoded, place).reshape(span, width)
+    cross_slots = spread_pieces(pick(cross_own))
+    feed_slots = spread_pieces(pick(feed_own))
+    grad = swap_positions(output_grad, place).reshape(span, width)
+
+    def turned(values, axis):
+        for bit in (1, 2):
+            parts = [lax.index_in_dim(values, t ^ bit, axis) for t in range(4)]
+            swapped = lax.concatenate(parts, axis)
+            values = jnp.where((turn & bit) != 0, swapped, values)
+        return values
+
+    bias_own = adapter_bias.reshape(1, -1)
+    biases = [bias_own] + [over("tensor", k)(bias_own) for k in (1, 2, 3)]
+
+    def pieces_of(own, slots, slot):
+        if slot == 0:
+            return [(own, t) for t in range(4)]
+        return [(piece, 0) for piece in slots[slot - 1]]
+
+    gain = lambda j: norm_gains[j : j + 1]
+    shift = lambda j: norm_shifts[j : j + 1]
+    length = lax.dynamic_slice_in_dim(source_lengths, place, 1, 0)
+
+    self_kept = None
+    for slot in range(4):
+        self_kept = attend_slot(slot, None, x, None, pieces_of(self_own, self_slots, slot), self_kept)
+    first, normed_one, scale_one = out_norm(self_kept[3], self_kept[4], x, gain(0), shift(0))
+    cross_kept = None
+    for slot in range(4):
+        cross_kept = attend_slot(
+            slot, length, first, source, pieces_of(cross_own, cross_slots, slot), cross_kept
+        )
+    second, normed_two, scale_two = out_norm(cross_kept[3], cross_kept[4], first, gain(1), shift(1))
+    feed_kept = None
+    for slot in range(4):
+        bias = biases[slot]
+        if slot > 0:
+            bias = turned(bias.reshape(4, extra), 0).reshape(1, -1)
+        feed_kept = feed_slot(
+            slot, second, bias, pieces_of(feed_own, feed_slots, slot), feed_kept, units, extra
+        )
+    outcome, branch_low, sums_three = last_norm(
+        feed_kept[0], second, adapter_shift.reshape(1, -1), gain(2), shift(2), grad
+    )
+    result = swap_positions(outcome.reshape(4, share, width), place)
+    cross_low, in_grad, out_grad, bias_grad, sums_two = feed_back(
+        branch_low, feed_kept, second, normed_two, scale_two, gain(1)
+    )
+
+    def natural(values):
+        slots = values.reshape((4, 4, extra) + values.shape[1:])
+        swapped = turned(slots, 1)
+        return [slots[0]] + [swapped[k] for k in (1, 2, 3)]
+
+    grads = [jnp.stack(pair) for pair in zip(natural(in_grad), natural(out_grad))]
+    sent = [over("tensor", k)(grads[k]) for k in (1, 2, 3)]
+    self_low, encoded_back, sums_one = attention_back(
+        cross_low, cross_kept, (normed_one, scale_one, gain(0))
+    )
+    encoded_result = swap_positions(encoded_back.reshape(4, share, width), place)
+    adapter_sum = grads[0].astype(F32)
+    for part in sent:
+        adapter_sum = adapter_sum + part.astype(F32)
+    adapter_sum = lax.psum(adapter_sum.astype(BF16), "dp").astype(F32)
+    in_total = adapter_sum[0].reshape(4 * extra, width).T
+    out_total = adapter_sum[1].reshape(4 * extra, width)
+
+    bias_parts = natural(bias_grad.reshape(-1))
+    bias_line = jnp.zeros((4, 4 * extra), F32)
+    for k in range(4):
+        bias_line = lax.dynamic_update_index_in_dim(bias_line, bias_parts[k].reshape(-1), place ^ k, 0)
+    bias_line = jnp.pad(bias_line.reshape(-1), (0, width - 16 * extra))
+    small = jnp.stack(
+        [
+            sums_one[0],
+            sums_two[0],
+            sums_three[0],
+            sums_one[1],
+            sums_two[1],
+            sums_three[1],
+            sums_three[2],
+            bias_line,
+        ]
+    )
+    small = lax.psum(small, ("dp", "tensor"))
+    bias_total = lax.dynamic_slice_in_dim(small[7], place * (4 * extra), 4 * extra, 0)
+
+    (input_back,) = attention_back(self_low, self_kept, None)
+    input_result = swap_positions(input_back.reshape(4, share, width), place)
+    return (
+        result,
+        input_result,
+        encoded_result,
+        in_total,
+        out_total,
+        bias_total,
+        small[6],
+        small[0:3],
+        small[3:6],
+    )
 
 
 def gelu_tanh(values):
@@ -346,8 +1028,15 @@
         P(),
         P("dp", "tensor", None),
     )
+    suits = mesh.shape["tensor"] == 4 and mesh.shape["dp"] % 4 == 0
+
+    def layer(*arrays):
+        if suits and arrays[0].shape[:2] == (4, ROWS) and arrays[1].shape[:2] == (4, ROWS):
+            return whole_sequences(*arrays)
+        return local(*arrays)
+
     return jax.shard_map(
-        local,
+        layer,
         mesh=mesh,
         in_specs=placed,
         out_specs=(

time: 2040 us -> 681 us (0.33)
  waiting for transfers between devices: 955 us -> 142 us
  matrix products: 628 us -> 0 us
  Pallas kernels: 0 us -> 324 us
  other arithmetic: 247 us -> 15.7 us
  local copies, waits for them, and re-layouts: 163 us -> 81 us
  starting transfers between devices: 0.62 us -> 58.5 us
    dot_general x49 -> x0, matrix products: 628 us -> none  [the longest x11 124 us: multiply_by_transpose(): lax.dot_general(left, right, (((1,), (1,)), ((), ())), preferred_element_...]
    all_gather x6 -> x0, waiting for transfers between devices: 425 us -> none  [the longest x1 90.2 us: local(): lax.all_gather(inputs, 'tensor', axis=1, tiled=True)]
    reduce_scatter x6 -> x0, waiting for transfers between devices: 401 us -> none  [the longest x1 87.2 us: local(): lax.psum_scatter(cross_partial.astype(jnp.bfloat16), 'tensor', scatter_di...]
    pallas_call x0 -> x18, Pallas kernels: none -> 324 us  [the longest x8 107 us: attend_slot(): pl.pallas_call(functools.partial(attend_kernel, causal, first), grid=(2,)...]
    convert_element_type x12 -> x1, other arithmetic: 146 us -> 2.2 us  [whole_sequences(): adapter_sum = lax.psum(adapter_sum.astype(BF16), 'dp').astype(F32)]
    ppermute x0 -> x60, waiting for transfers between devices: none -> 109 us  [over(): return lambda values: lax.ppermute(values, axis, pairs)]
    reduce_sum x13 -> x0, other arithmetic: 96.8 us -> none  [the longest x3 55.3 us: attend(): denom = jnp.sum(weights, axis=-1, keepdims=True)]
    psum x2 -> x1, waiting for transfers between devices: 127 us -> 33 us  [whole_sequences(): adapter_sum = lax.psum(adapter_sum.astype(BF16), 'dp').astype(F32)]
  transfers between devices with their start and end apart: 15 -> 61, of which waited for: 11 -> 14; matrix products, arithmetic and copies ran while one was open for 28% -> 11% of each run, Pallas kernels for 0% -> 31%
where the time goes in v1:
time: 681 us; the launch traced here: 676 us
  Pallas kernels  324 us (48%)
  waiting for transfers between devices  142 us (21%)
  local copies, waits for them, and re-layouts  81 us (12%)
  starting transfers between devices  58.5 us (9%)
  blocking collectives  39.7 us (6%)
  other arithmetic  15.7 us (2%)
  between operations  15 us (2%)
    ppermute x60, waiting for transfers between devices, over(): return lambda values: lax.ppermute(values, axis, pairs)  109 us
    pallas_call x8, Pallas kernels, attend_slot(): pl.pallas_call(functools.partial(attend_kernel, causal, first), grid=(2,)...  107 us
    pallas_call x2, Pallas kernels, attention_back(): pl.pallas_call(functools.partial(attention_back_kernel, causal), grid=(he...  96 us
    pallas_call x4, Pallas kernels, feed_slot(): pl.pallas_call(functools.partial(feed_kernel, first, units, extra), grid=...  62 us
    ppermute x60, starting transfers between devices, over(): return lambda values: lax.ppermute(values, axis, pairs)  58.4 us
    psum x1, blocking collectives, whole_sequences(): small = lax.psum(small, ('dp', 'tensor'))  39.7 us
    pallas_call x1, Pallas kernels, feed_back(): pl.pallas_call(feed_back_kernel, grid=(units // chunk,), in_specs=[whole(...  36.7 us
    psum x1, waiting for transfers between devices, whole_sequences(): adapter_sum = lax.psum(adapter_sum.astype(BF16), 'dp').astype(F32)  33 us
  transfers between devices with their start and end apart: 61, of which 14 were waited for; matrix products, arithmetic and copies ran while one was open for 11% of the time, Pallas kernels for 31%

profile of v1, /device:TPU:0, one launch (start us, length us, event | category | flops | bytes accessed | tf_op | source)
XLA Modules:
  0.0 675.8 jit_solution(7039092124484672529)
XLA Ops:
  37.9 4.1 copy.98
  61.6 3.6 collective-permute-done.15
  69.6 7.0 %collective-permute-done.45 = bf16[1,256,1024]{2,1,0:T(8,128)(2,1)} collective-permute-done((bf16[1,256,1024]{2,1,0:T(8,128)(2,1)}, bf16[1,256,1024]{2,1,0:T(8,128)(2,1)}, u32[]{:S(2)}, u32[]{:S(2)}) %collective-permute-start.45) | collective-permute-done | bytes 524320 | tf_op jit(solution)/shard_map/ppermute | solution.py:520
  84.1 5.1 collective-permute-done.2
  93.8 23.7 %collective-permute-done.7.refs_1_ = bf16[1,4,64,1024]{3,2,1,0:T(8,128)(2,1)S(1)} collective-permute-done((bf16[1,4,64,1024]{3,2,1,0:T(8,128)(2,1)}, bf16[1,4,64,1024]{3,2,1,0:T(8,128)(2,1)S(1)}, u32[]{:S(2)}, u32[]{:S(2)}) %collective-permute-start.7) | collective-permute-done | bytes 524320 | tf_op jit(solution)/shard_map/ppermute | solution.py:520
  120.5 19.6 %collective-permute-done.16 = bf16[1,256,1024]{2,1,0:T(8,128)(2,1)} collective-permute-done((bf16[1,256,1024]{2,1,0:T(8,128)(2,1)}, bf16[1,256,1024]{2,1,0:T(8,128)(2,1)}, u32[]{:S(2)}, u32[]{:S(2)}) %collective-permute-start.16) | collective-permute-done | bytes 524320 | tf_op jit(solution)/shard_map/ppermute | solution.py:520
  142.2 6.3 collective-permute-done.46
  148.5 11.2 %self_attend.4 = (bf16[16,1024,1024]{2,1,0:T(8,128)(2,1)}, bf16[4,1024,1024]{2,1,0:T(8,128)(2,1)}, f32[16,1,1024]{2,1,0:T(1,128)}, bf16[1024,1024]{1,0:T(8,128)(2,1)}, bf16[4,1024,1024]{2,1,0:T(8,128)(2,1)}) custom-call(bf16[1024,1024]{1,0:T(8,128)(2,1)} %bitcast.41, bf16[4,4,64,1024]{3,2,1,0:T(8,128)(2,1)} %copy-done.5, bf16[4,4,64,1024]{3,2,1,0:T(8,128)(2,1)} %copy-done.5, ...), custom_call_target="tpu_custom_call" | custom-call | flops 12000000000 | bytes 16777216 | tf_op jit(solution)/shard_map/self_attend/pallas_call | solution.py:151
  172.2 11.3 %self_attend.5 = (bf16[16,1024,1024]{2,1,0:T(8,128)(2,1)}, bf16[4,1024,1024]{2,1,0:T(8,128)(2,1)}, f32[16,1,1024]{2,1,0:T(1,128)}, bf16[1024,1024]{1,0:T(8,128)(2,1)}, bf16[4,1024,1024]{2,1,0:T(8,128)(2,1)}) custom-call(bf16[1024,1024]{1,0:T(8,128)(2,1)} %bitcast.42, ...), custom_call_target="tpu_custom_call", output_to_operand_aliasing={{0}: (5, {}), {1}: (6, {}), {2}: (7, {}), {3}: (8, {}), {4}... | custom-call | flops 12000000000 | bytes 16777216 | tf_op jit(solution)/shard_map/self_attend/pallas_call | solution.py:151
  185.5 11.4 %self_attend.6 = (bf16[16,1024,1024]{2,1,0:T(8,128)(2,1)}, bf16[4,1024,1024]{2,1,0:T(8,128)(2,1)}, f32[16,1,1024]{2,1,0:T(1,128)}, bf16[1024,1024]{1,0:T(8,128)(2,1)}, bf16[4,1024,1024]{2,1,0:T(8,128)(2,1)}) custom-call(bf16[1024,1024]{1,0:T(8,128)(2,1)} %bitcast.43, ...), custom_call_target="tpu_custom_call", output_to_operand_aliasing={{0}: (5, {}), {1}: (6, {}), {2}: (7, {}), {3}: (8, {}), {4}... | custom-call | flops 12000000000 | bytes 16777216 | tf_op jit(solution)/shard_map/self_attend/pallas_call | solution.py:151
  200.1 11.2 %self_attend.7 = (bf16[16,1024,1024]{2,1,0:T(8,128)(2,1)}, bf16[4,1024,1024]{2,1,0:T(8,128)(2,1)}, f32[16,1,1024]{2,1,0:T(1,128)}, bf16[1024,1024]{1,0:T(8,128)(2,1)}, bf16[4,1024,1024]{2,1,0:T(8,128)(2,1)}) custom-call(bf16[1024,1024]{1,0:T(8,128)(2,1)} %bitcast.44, ...), custom_call_target="tpu_custom_call", output_to_operand_aliasing={{0}: (5, {}), {1}: (6, {}), {2}: (7, {}), {3}: (8, {}), {4}... | custom-call | flops 12000000000 | bytes 16777216 | tf_op jit(solution)/shard_map/self_attend/pallas_call | solution.py:151
  211.3 7.8 %out_norm.2 = (bf16[1024,1024]{1,0:T(8,128)(2,1)}, bf16[1024,1024]{1,0:T(8,128)(2,1)}, f32[1024,1]{1,0:T(8,128)}) custom-call(bf16[1024,1024]{1,0:T(8,128)(2,1)} %get-tuple-element.113.ctx_ref, bf16[4,1024,1024]{2,1,0:T(8,128)(2,1)} %get-tuple-element.114.wo_ref.refs_1_, bf16[1024,1024]{1,0:T(8,128)(2,1)} %bitcast.45, ...), custom_call_target="tpu_custom_call" | custom-call | flops 2147483648 | bytes 10485760 | tf_op jit(solution)/shard_map/out_norm/pallas_call | solution.py:179
  219.7 15.7 %cross_attend.4 = (bf16[16,1024,1024]{2,1,0:T(8,128)(2,1)}, bf16[4,1024,1024]{2,1,0:T(8,128)(2,1)}, f32[16,1,1024]{2,1,0:T(1,128)}, bf16[1024,1024]{1,0:T(8,128)(2,1)}, bf16[4,1024,1024]{2,1,0:T(8,128)(2,1)}) custom-call(s32[1]{0:T(128)} %dynamic_slice.74.refs_0_, bf16[1024,1024]{1,0:T(8,128)(2,1)} %get-tuple-element.115.refs_1_.x_ref, ...), custom_call_target="tpu_custom_call" | custom-call | flops 12000000000 | bytes 16777216 | tf_op jit(solution)/shard_map/cross_attend/pallas_call | solution.py:151
  240.4 15.3 %cross_attend.5 = (bf16[16,1024,1024]{2,1,0:T(8,128)(2,1)}, bf16[4,1024,1024]{2,1,0:T(8,128)(2,1)}, f32[16,1,1024]{2,1,0:T(1,128)}, bf16[1024,1024]{1,0:T(8,128)(2,1)}, bf16[4,1024,1024]{2,1,0:T(8,128)(2,1)}) custom-call(s32[1]{0:T(128)} %dynamic_slice.74.refs_0_, ...), custom_call_target="tpu_custom_call", output_to_operand_aliasing={{0}: (7, {}), {1}: (8, {}), {2}: (9, {}), {3}: (10, {}), {4... | custom-call | flops 12000000000 | bytes 16777216 | tf_op jit(solution)/shard_map/cross_attend/pallas_call | solution.py:151
  256.3 15.4 %cross_attend.6 = (bf16[16,1024,1024]{2,1,0:T(8,128)(2,1)}, bf16[4,1024,1024]{2,1,0:T(8,128)(2,1)}, f32[16,1,1024]{2,1,0:T(1,128)}, bf16[1024,1024]{1,0:T(8,128)(2,1)}, bf16[4,1024,1024]{2,1,0:T(8,128)(2,1)}) custom-call(s32[1]{0:T(128)} %dynamic_slice.74.refs_0_, ...), custom_call_target="tpu_custom_call", output_to_operand_aliasing={{0}: (7, {}), {1}: (8, {}), {2}: (9, {}), {3}: (10, {}), {4... | custom-call | flops 12000000000 | bytes 16777216 | tf_op jit(solution)/shard_map/cross_attend/pallas_call | solution.py:151
  272.0 17.1 %collective-permute-done.36.refs_2_ = bf16[1,576,1024]{2,1,0:T(8,128)(2,1)S(1)} collective-permute-done((bf16[1,576,1024]{2,1,0:T(8,128)(2,1)}, bf16[1,576,1024]{2,1,0:T(8,128)(2,1)S(1)}, u32[]{:S(2)}, u32[]{:S(2)}) %collective-permute-start.36) | collective-permute-done | bytes 1179680 | tf_op jit(solution)/shard_map/ppermute | solution.py:520
  291.4 15.3 %cross_attend.7 = (bf16[16,1024,1024]{2,1,0:T(8,128)(2,1)}, bf16[4,1024,1024]{2,1,0:T(8,128)(2,1)}, f32[16,1,1024]{2,1,0:T(1,128)}, bf16[1024,1024]{1,0:T(8,128)(2,1)}, bf16[4,1024,1024]{2,1,0:T(8,128)(2,1)}) custom-call(s32[1]{0:T(128)} %dynamic_slice.74.refs_0_, ...), custom_call_target="tpu_custom_call", output_to_operand_aliasing={{0}: (7, {}), {1}: (8, {}), {2}: (9, {}), {3}: (10, {}), {4... | custom-call | flops 12000000000 | bytes 16777216 | tf_op jit(solution)/shard_map/cross_attend/pallas_call | solution.py:151
  306.7 7.8 %out_norm.3 = (bf16[1024,1024]{1,0:T(8,128)(2,1)}, bf16[1024,1024]{1,0:T(8,128)(2,1)}, f32[1024,1]{1,0:T(8,128)}) custom-call(bf16[1024,1024]{1,0:T(8,128)(2,1)} %get-tuple-element.131.ctx_ref, bf16[4,1024,1024]{2,1,0:T(8,128)(2,1)} %get-tuple-element.132.wo_ref.refs_1_, bf16[1024,1024]{1,0:T(8,128)(2,1)} %get-tuple-element.115.refs_1_.x_ref, ...), custom_call_target="tpu_custom_call" | custom-call | flops 2147483648 | bytes 10485760 | tf_op jit(solution)/shard_map/out_norm/pallas_call | solution.py:179
  314.5 3.6 collective-permute-done.38.refs_4_
  318.2 15.4 %feed.4 = (f32[1024,1024]{1,0:T(8,128)}, bf16[1024,4096]{1,0:T(8,128)(2,1)}, bf16[1024,512]{1,0:T(8,128)(2,1)}, bf16[1024,512]{1,0:T(8,128)(2,1)}, bf16[4096,102...) custom-call(bf16[1024,1024]{1,0:T(8,128)(2,1)} %get-tuple-element.133.refs_0_, ...), custom_call_target="tpu_custom_call" | custom-call | flops 7000000000 | bytes 20971520 | tf_op jit(solution)/shard_map/feed/pallas_call | solution.py:277
  334.1 7.8 %collective-permute-done.33.refs_4_ = bf16[1,576,1024]{2,1,0:T(8,128)(2,1)} collective-permute-done((bf16[1,576,1024]{2,1,0:T(8,128)(2,1)S(1)}, bf16[1,576,1024]{2,1,0:T(8,128)(2,1)}, u32[]{:S(2)}, u32[]{:S(2)}) %collective-permute-start.33) | collective-permute-done | bytes 1179680 | tf_op jit(solution)/shard_map/ppermute | solution.py:520
  341.9 15.5 %feed.5 = (f32[1024,1024]{1,0:T(8,128)}, bf16[1024,4096]{1,0:T(8,128)(2,1)}, bf16[1024,512]{1,0:T(8,128)(2,1)}, bf16[1024,512]{1,0:T(8,128)(2,1)}, bf16[4096,102...) custom-call(bf16[1024,1024]{1,0:T(8,128)(2,1)} %get-tuple-element.13, ...), custom_call_target="tpu_custom_call", output_to_operand_aliasing={{0}: (6, {}), {1}: (7, {}), {2}: (8, {}), {3}: (9, {}), {4}... | custom-call | flops 7000000000 | bytes 20971520 | tf_op jit(solution)/shard_map/feed/pallas_call | solution.py:277
  357.5 15.6 %feed.6 = (f32[1024,1024]{1,0:T(8,128)}, bf16[1024,4096]{1,0:T(8,128)(2,1)}, bf16[1024,512]{1,0:T(8,128)(2,1)}, bf16[1024,512]{1,0:T(8,128)(2,1)}, bf16[4096,102...) custom-call(bf16[1024,1024]{1,0:T(8,128)(2,1)} %get-tuple-element.13, ...), custom_call_target="tpu_custom_call", output_to_operand_aliasing={{0}: (6, {}), {1}: (7, {}), {2}: (8, {}), {3}: (9, {}), {4}... | custom-call | flops 7000000000 | bytes 20971520 | tf_op jit(solution)/shard_map/feed/pallas_call | solution.py:277
  374.1 15.5 %feed.7 = (f32[1024,1024]{1,0:T(8,128)}, bf16[1024,4096]{1,0:T(8,128)(2,1)}, bf16[1024,512]{1,0:T(8,128)(2,1)}, bf16[1024,512]{1,0:T(8,128)(2,1)}, bf16[4096,102...) custom-call(bf16[1024,1024]{1,0:T(8,128)(2,1)} %get-tuple-element.13, ...), custom_call_target="tpu_custom_call", output_to_operand_aliasing={{0}: (6, {}), {1}: (7, {}), {2}: (8, {}), {3}: (9, {}), {4}... | custom-call | flops 7000000000 | bytes 20971520 | tf_op jit(solution)/shard_map/feed/pallas_call | solution.py:277
  389.6 7.3 %last_norm.1 = (bf16[1024,1024]{1,0:T(8,128)(2,1)}, bf16[1024,1024]{1,0:T(8,128)(2,1)}, f32[8,1024]{1,0:T(8,128)}) custom-call(f32[1024,1024]{1,0:T(8,128)} %get-tuple-element.158.acc_ref, bf16[1024,1024]{1,0:T(8,128)(2,1)} %get-tuple-element.133.refs_0_.x_ref, f32[1,1024]{1,0:T(1,128)} %bitcast.80, f32[1,1024]{1,0:T(1,128)} %get-tuple-element.245.gain_ref, ...), custom_call_target="tpu_custom_call" | custom-call | flops 31457280 | bytes 12582912 | tf_op jit(solution)/shard_map/last_norm/pallas_call | solution.py:313
  396.9 36.7 %feed_back.1 = (bf16[1024,1024]{1,0:T(8,128)(2,1)}, bf16[512,1024]{1,0:T(8,128)(2,1)}, bf16[512,1024]{1,0:T(8,128)(2,1)}, f32[1,512]{1,0:T(1,128)}, f32[8,1024]{1,0:T(8,128)}) custom-call(bf16[1024,1024]{1,0:T(8,128)(2,1)} %get-tuple-element.160.g_ref, bf16[4096,1024]{1,0:T(8,128)(2,1)} %get-tuple-element.161.up_ref, ...), custom_call_target="tpu_custom_call" | custom-call | flops 21474836480 | bytes 41943040 | tf_op jit(solution)/shard_map/feed_back/pallas_call | solution.py:377
  437.6 53.4 %cross_back.1 = (bf16[1024,1024]{1,0:T(8,128)(2,1)}, bf16[1024,1024]{1,0:T(8,128)(2,1)}, f32[8,1024]{1,0:T(8,128)}) custom-call(bf16[1024,1024]{1,0:T(8,128)(2,1)} %get-tuple-element.170.refs_0_, bf16[4,1024,1024]{2,1,0:T(8,128)(2,1)} %get-tuple-element.132.wo_ref.refs_1_, bf16[16,1024,1024]{2,1,0:T(8,128)(2,1)} %get-tuple-element.171.refs_2_, ...), custom_call_target="tpu_custom_call" | custom-call | flops 40000000000 | bytes 62914560 | tf_op jit(solution)/shard_map/cross_back/pallas_call | solution.py:495
  492.8 39.7 %psum.15 = f32[8,1024]{1,0:T(8,128)S(1)} all-reduce(f32[8,1024]{1,0:T(8,128)S(1)} %stack.32), channel_id=1, replica_groups=mesh['dp'=8,'tensor'=4] {'dp','tensor'}, use_global_device_ids=true, to_apply=%region_1.2 | all-reduce | flops 8192 | bytes 65536 | tf_op jit(solution)/shard_map/psum | solution.py:673
  544.5 42.5 %self_back.1 = bf16[1024,1024]{1,0:T(8,128)(2,1)} custom-call(bf16[1024,1024]{1,0:T(8,128)(2,1)} %get-tuple-element.176.refs_0_, bf16[4,1024,1024]{2,1,0:T(8,128)(2,1)} %get-tuple-element.114.wo_ref.refs_1_, bf16[16,1024,1024]{2,1,0:T(8,128)(2,1)} %get-tuple-element.177.refs_2_, bf16[4,1024,1024]{2,1,0:T(8,128)(2,1)} %get-tuple-element.178.refs_3_, ...), custom_call_target="tpu_custom_call" | custom-call | flops 40000000000 | bytes 62914560 | tf_op jit(solution)/shard_map/self_back/pallas_call | solution.py:495
  600.0 4.7 collective-permute-done.51
  608.8 7.1 %collective-permute-done.48 = bf16[1,256,1024]{2,1,0:T(8,128)(2,1)S(1)} collective-permute-done((bf16[1,256,1024]{2,1,0:T(8,128)(2,1)}, bf16[1,256,1024]{2,1,0:T(8,128)(2,1)S(1)}, u32[]{:S(2)}, u32[]{:S(2)}) %collective-permute-start.48) | collective-permute-done | bytes 524320 | tf_op jit(solution)/shard_map/ppermute | solution.py:520
  618.4 33.0 %all-reduce.3.cloned.1.call-done = bf16[2,4,32,1024]{3,2,1,0:T(8,128)(2,1)} async-done(((bf16[2,4,32,1024]{3,2,1,0:T(8,128)(2,1)}), bf16[2,4,32,1024]{3,2,1,0:T(8,128)(2,1)}) %all-reduce.3.cloned.1.call-update) | async-done | bytes 524304 | tf_op jit(solution)/shard_map/psum | solution.py:652
  (292 shorter events, 154.1 us)
Async XLA Ops:
  7.2 644.3 %all-reduce.3.cloned.1.call-start = ((), (), s32[]{:S(2)}) async-start(), calls=%async_computation | async-start | bytes 1048576 | tf_op jit(solution)/shard_map/psum | solution.py:652
  13.2 37.2 %collective-permute-start.40 = (f32[1,128]{1,0:T(1,128)S(1)}, f32[1,128]{1,0:T(1,128)S(1)}, u32[]{:S(2)}, u32[]{:S(2)}) collective-permute-start(f32[1,128]{1,0:T(1,128)S(1)} %bitcast.83), channel_id=1, source_target_pairs={{0,1},{1,0},{2,3},{3,2},{4,5},{5,4},{6,7},{7,6},{8,9},{9,8},{10,11... | collective-permute-start | bytes 1544 | tf_op jit(solution)/shard_map/ppermute | solution.py:520
  16.1 37.6 %collective-permute-start.35 = (f32[1,128]{1,0:T(1,128)S(1)}, f32[1,128]{1,0:T(1,128)S(1)}, u32[]{:S(2)}, u32[]{:S(2)}) collective-permute-start(f32[1,128]{1,0:T(1,128)S(1)} %bitcast.84), channel_id=1, source_target_pairs={{0,2},{1,3},{2,0},{3,1},{4,6},{5,7},{6,4},{7,5},{8,10},{9,11},{10,... | collective-permute-start | bytes 1544 | tf_op jit(solution)/shard_map/ppermute | solution.py:520
  17.7 37.2 %collective-permute-start.30 = (f32[1,128]{1,0:T(1,128)S(1)}, f32[1,128]{1,0:T(1,128)S(1)}, u32[]{:S(2)}, u32[]{:S(2)}) collective-permute-start(f32[1,128]{1,0:T(1,128)S(1)} %bitcast.85), channel_id=1, source_target_pairs={{0,3},{1,2},{2,1},{3,0},{4,7},{5,6},{6,5},{7,4},{8,11},{9,10},{10,... | collective-permute-start | bytes 1544 | tf_op jit(solution)/shard_map/ppermute | solution.py:520
  18.5 38.0 %collective-permute-start = (bf16[1,256,1024]{2,1,0:T(8,128)(2,1)}, bf16[1,256,1024]{2,1,0:T(8,128)(2,1)}, u32[]{:S(2)}, u32[]{:S(2)}) collective-permute-start(bf16[1,256,1024]{2,1,0:T(8,128)(2,1)} %constant_dynamic-slice_fusion.21), channel_id=1, source_target_pairs={{0,1},{1,0},{2,3},{3,2},{4,5},{5,4},{6,7},{7,6},{8,9},{9,8},{10,11... | collective-permute-start | bytes 1572872 | tf_op jit(solution)/shard_map/ppermute | solution.py:520
  27.6 53.5 %collective-permute-start.11 = (bf16[1,4,64,1024]{3,2,1,0:T(8,128)(2,1)}, bf16[1,4,64,1024]{3,2,1,0:T(8,128)(2,1)}, u32[]{:S(2)}, u32[]{:S(2)}) collective-permute-start(bf16[1,4,64,1024]{3,2,1,0:T(8,128)(2,1)} %constant_dynamic-slice_fusion.18), channel_id=1, source_target_pairs={{0,1},{1,0},{2,3},{3,2},{4,5},{5,4},{6,7},{7,6},{8,9},{9,8},{10,11... | collective-permute-start | bytes 1572872 | tf_op jit(solution)/shard_map/ppermute | solution.py:520
  65.2 52.3 %collective-permute-start.7 = (bf16[1,4,64,1024]{3,2,1,0:T(8,128)(2,1)}, bf16[1,4,64,1024]{3,2,1,0:T(8,128)(2,1)S(1)}, u32[]{:S(2)}, u32[]{:S(2)}) collective-permute-start(bf16[1,4,64,1024]{3,2,1,0:T(8,128)(2,1)} %constant_dynamic-slice_fusion.18), channel_id=1, source_target_pairs={{0,2},{1,3},{2,0},{3,1},{4,6},{5,7},{6,4},{7,5},{8,10},{9,11},{10,... | collective-permute-start | bytes 1572872 | tf_op jit(solution)/shard_map/ppermute | solution.py:520
  76.6 63.5 %collective-permute-start.16 = (bf16[1,256,1024]{2,1,0:T(8,128)(2,1)}, bf16[1,256,1024]{2,1,0:T(8,128)(2,1)}, u32[]{:S(2)}, u32[]{:S(2)}) collective-permute-start(bf16[1,256,1024]{2,1,0:T(8,128)(2,1)} %get-tuple-element.210), channel_id=1, source_target_pairs={{0,2},{1,3},{2,0},{3,1},{4,6},{5,7},{6,4},{7,5},{8,10},{9,11},{10,... | collective-permute-start | bytes 1572872 | tf_op jit(solution)/shard_map/ppermute | solution.py:520
  81.2 58.9 %collective-permute-start.17 = (bf16[1,256,1024]{2,1,0:T(8,128)(2,1)}, bf16[1,256,1024]{2,1,0:T(8,128)(2,1)}, u32[]{:S(2)}, u32[]{:S(2)}) collective-permute-start(bf16[1,256,1024]{2,1,0:T(8,128)(2,1)} %get-tuple-element.208), channel_id=1, source_target_pairs={{0,3},{1,2},{2,1},{3,0},{4,7},{5,6},{6,5},{7,4},{8,11},{9,10},{10,... | collective-permute-start | bytes 1572872 | tf_op jit(solution)/shard_map/ppermute | solution.py:520
  82.6 65.8 %collective-permute-start.46 = (bf16[1,256,1024]{2,1,0:T(8,128)(2,1)}, bf16[1,256,1024]{2,1,0:T(8,128)(2,1)}, u32[]{:S(2)}, u32[]{:S(2)}) collective-permute-start(bf16[1,256,1024]{2,1,0:T(8,128)(2,1)} %get-tuple-element.207), channel_id=1, source_target_pairs={{0,2},{1,3},{2,0},{3,1},{4,6},{5,7},{6,4},{7,5},{8,10},{9,11},{10,... | collective-permute-start | bytes 1572872 | tf_op jit(solution)/shard_map/ppermute | solution.py:520
  117.5 51.5 %collective-permute-start.3 = (bf16[1,4,64,1024]{3,2,1,0:T(8,128)(2,1)}, bf16[1,4,64,1024]{3,2,1,0:T(8,128)(2,1)}, u32[]{:S(2)}, u32[]{:S(2)}) collective-permute-start(bf16[1,4,64,1024]{3,2,1,0:T(8,128)(2,1)} %constant_dynamic-slice_fusion.18), channel_id=1, source_target_pairs={{0,3},{1,2},{2,1},{3,0},{4,7},{5,6},{6,5},{7,4},{8,11},{9,10},{10,... | collective-permute-start | bytes 1572872 | tf_op jit(solution)/shard_map/ppermute | solution.py:520
  120.5 44.9 %collective-permute-start.47 = (bf16[1,256,1024]{2,1,0:T(8,128)(2,1)}, bf16[1,256,1024]{2,1,0:T(8,128)(2,1)}, u32[]{:S(2)}, u32[]{:S(2)}) collective-permute-start(bf16[1,256,1024]{2,1,0:T(8,128)(2,1)} %get-tuple-element.205), channel_id=1, source_target_pairs={{0,3},{1,2},{2,1},{3,0},{4,7},{5,6},{6,5},{7,4},{8,11},{9,10},{10,... | collective-permute-start | bytes 1572872 | tf_op jit(solution)/shard_map/ppermute | solution.py:520
  196.9 42.7 %collective-permute-start.41 = (bf16[1,576,1024]{2,1,0:T(8,128)(2,1)}, bf16[1,576,1024]{2,1,0:T(8,128)(2,1)S(1)}, u32[]{:S(2)}, u32[]{:S(2)}) collective-permute-start(bf16[1,576,1024]{2,1,0:T(8,128)(2,1)} %constant_dynamic-slice_fusion.13), channel_id=1, source_target_pairs={{0,1},{1,0},{2,3},{3,2},{4,5},{5,4},{6,7},{7,6},{8,9},{9,8},{10,11... | collective-permute-start | bytes 3538952 | tf_op jit(solution)/shard_map/ppermute | solution.py:520
  199.2 37.4 %collective-permute-start.24 = (bf16[1,4,64,1024]{3,2,1,0:T(8,128)(2,1)}, bf16[1,4,64,1024]{3,2,1,0:T(8,128)(2,1)}, u32[]{:S(2)}, u32[]{:S(2)}) collective-permute-start(bf16[1,4,64,1024]{3,2,1,0:T(8,128)(2,1)} %collective-permute-done.22.refs_3_), channel_id=1, source_target_pairs={{0,8},{4,12},{8,0},{12,4},{16,24},{20,28},{24,16},{28,20},{1,9},{5... | collective-permute-start | bytes 1572872 | tf_op jit(solution)/shard_map/ppermute | solution.py:520
  235.4 53.8 %collective-permute-start.36 = (bf16[1,576,1024]{2,1,0:T(8,128)(2,1)}, bf16[1,576,1024]{2,1,0:T(8,128)(2,1)S(1)}, u32[]{:S(2)}, u32[]{:S(2)}) collective-permute-start(bf16[1,576,1024]{2,1,0:T(8,128)(2,1)} %constant_dynamic-slice_fusion.13), channel_id=1, source_target_pairs={{0,2},{1,3},{2,0},{3,1},{4,6},{5,7},{6,4},{7,5},{8,10},{9,11},{10,... | collective-permute-start | bytes 3538952 | tf_op jit(solution)/shard_map/ppermute | solution.py:520
  236.6 53.6 %collective-permute-start.31 = (bf16[1,576,1024]{2,1,0:T(8,128)(2,1)}, bf16[1,576,1024]{2,1,0:T(8,128)(2,1)S(1)}, u32[]{:S(2)}, u32[]{:S(2)}) collective-permute-start(bf16[1,576,1024]{2,1,0:T(8,128)(2,1)} %constant_dynamic-slice_fusion.13), channel_id=1, source_target_pairs={{0,3},{1,2},{2,1},{3,0},{4,7},{5,6},{6,5},{7,4},{8,11},{9,10},{10,... | collective-permute-start | bytes 3538952 | tf_op jit(solution)/shard_map/ppermute | solution.py:520
  239.5 51.7 %collective-permute-start.43 = (bf16[1,576,1024]{2,1,0:T(8,128)(2,1)S(1)}, bf16[1,576,1024]{2,1,0:T(8,128)(2,1)}, u32[]{:S(2)}, u32[]{:S(2)}) collective-permute-start(bf16[1,576,1024]{2,1,0:T(8,128)(2,1)S(1)} %collective-permute-done.41.refs_2_), channel_id=1, source_target_pairs={{0,8},{4,12},{8,0},{12,4},{16,24},{20,28},{24,16},{28,20},{1,9},{5... | collective-permute-start | bytes 3538952 | tf_op jit(solution)/shard_map/ppermute | solution.py:520
  271.8 61.8 %collective-permute-start.42 = (bf16[1,576,1024]{2,1,0:T(8,128)(2,1)S(1)}, bf16[1,576,1024]{2,1,0:T(8,128)(2,1)}, u32[]{:S(2)}, u32[]{:S(2)}) collective-permute-start(bf16[1,576,1024]{2,1,0:T(8,128)(2,1)S(1)} %collective-permute-done.41.refs_2_), channel_id=1, source_target_pairs={{0,4},{4,0},{8,12},{12,8},{16,20},{20,16},{24,28},{28,24},{1,5},{5... | collective-permute-start | bytes 3538952 | tf_op jit(solution)/shard_map/ppermute | solution.py:520
  290.2 67.3 %collective-permute-start.37 = (bf16[1,576,1024]{2,1,0:T(8,128)(2,1)S(1)}, bf16[1,576,1024]{2,1,0:T(8,128)(2,1)}, u32[]{:S(2)}, u32[]{:S(2)}) collective-permute-start(bf16[1,576,1024]{2,1,0:T(8,128)(2,1)S(1)} %collective-permute-done.36.refs_2_), channel_id=1, source_target_pairs={{0,4},{4,0},{8,12},{12,8},{16,20},{20,16},{24,28},{28,24},{1,5},{5... | collective-permute-start | bytes 3538952 | tf_op jit(solution)/shard_map/ppermute | solution.py:520
  290.2 51.8 %collective-permute-start.33 = (bf16[1,576,1024]{2,1,0:T(8,128)(2,1)S(1)}, bf16[1,576,1024]{2,1,0:T(8,128)(2,1)}, u32[]{:S(2)}, u32[]{:S(2)}) collective-permute-start(bf16[1,576,1024]{2,1,0:T(8,128)(2,1)S(1)} %collective-permute-done.31.refs_2_), channel_id=1, source_target_pairs={{0,8},{4,12},{8,0},{12,4},{16,24},{20,28},{24,16},{28,20},{1,9},{5... | collective-permute-start | bytes 3538952 | tf_op jit(solution)/shard_map/ppermute | solution.py:520
  291.3 50.7 %collective-permute-start.44 = (bf16[1,576,1024]{2,1,0:T(8,128)(2,1)}, bf16[1,576,1024]{2,1,0:T(8,128)(2,1)}, u32[]{:S(2)}, u32[]{:S(2)}) collective-permute-start(bf16[1,576,1024]{2,1,0:T(8,128)(2,1)} %collective-permute-done.43.refs_4_), channel_id=1, source_target_pairs={{0,4},{4,0},{8,12},{12,8},{16,20},{20,16},{24,28},{28,24},{1,5},{5... | collective-permute-start | bytes 3538952 | tf_op jit(solution)/shard_map/ppermute | solution.py:520
  318.1 39.3 %collective-permute-start.39 = (bf16[1,576,1024]{2,1,0:T(8,128)(2,1)}, bf16[1,576,1024]{2,1,0:T(8,128)(2,1)}, u32[]{:S(2)}, u32[]{:S(2)}) collective-permute-start(bf16[1,576,1024]{2,1,0:T(8,128)(2,1)} %collective-permute-done.38.refs_4_), channel_id=1, source_target_pairs={{0,4},{4,0},{8,12},{12,8},{16,20},{20,16},{24,28},{28,24},{1,5},{5... | collective-permute-start | bytes 3538952 | tf_op jit(solution)/shard_map/ppermute | solution.py:520
  333.6 39.5 %collective-permute-start.32 = (bf16[1,576,1024]{2,1,0:T(8,128)(2,1)S(1)}, bf16[1,576,1024]{2,1,0:T(8,128)(2,1)S(1)}, u32[]{:S(2)}, u32[]{:S(2)}) collective-permute-start(bf16[1,576,1024]{2,1,0:T(8,128)(2,1)S(1)} %collective-permute-done.31.refs_2_), channel_id=1, source_target_pairs={{0,4},{4,0},{8,12},{12,8},{16,20},{20,16},{24,28},{28,24},{1,5},{5... | collective-permute-start | bytes 3538952 | tf_op jit(solution)/shard_map/ppermute | solution.py:520
  535.1 56.9 %collective-permute-start.57 = (bf16[2,4,32,1024]{3,2,1,0:T(8,128)(2,1)}, bf16[2,4,32,1024]{3,2,1,0:T(8,128)(2,1)S(1)}, u32[]{:S(2)}, u32[]{:S(2)}) collective-permute-start(bf16[2,4,32,1024]{3,2,1,0:T(8,128)(2,1)} %pad_maximum_fusion.3), channel_id=1, source_target_pairs={{0,1},{1,0},{2,3},{3,2},{4,5},{5,4},{6,7},{7,6},{8,9},{9,8},{10,11... | collective-permute-start | bytes 1572872 | tf_op jit(solution)/shard_map/ppermute | solution.py:520
  538.2 55.7 %collective-permute-start.58 = (bf16[2,4,32,1024]{3,2,1,0:T(8,128)(2,1)}, bf16[2,4,32,1024]{3,2,1,0:T(8,128)(2,1)S(1)}, u32[]{:S(2)}, u32[]{:S(2)}) collective-permute-start(bf16[2,4,32,1024]{3,2,1,0:T(8,128)(2,1)} %pad_maximum_fusion.4), channel_id=1, source_target_pairs={{0,2},{1,3},{2,0},{3,1},{4,6},{5,7},{6,4},{7,5},{8,10},{9,11},{10,... | collective-permute-start | bytes 1572872 | tf_op jit(solution)/shard_map/ppermute | solution.py:520
  540.5 53.5 %collective-permute-start.59 = (bf16[2,4,32,1024]{3,2,1,0:T(8,128)(2,1)}, bf16[2,4,32,1024]{3,2,1,0:T(8,128)(2,1)}, u32[]{:S(2)}, u32[]{:S(2)}) collective-permute-start(bf16[2,4,32,1024]{3,2,1,0:T(8,128)(2,1)} %pad_maximum_fusion.5), channel_id=1, source_target_pairs={{0,3},{1,2},{2,1},{3,0},{4,7},{5,6},{6,5},{7,4},{8,11},{9,10},{10,... | collective-permute-start | bytes 1572872 | tf_op jit(solution)/shard_map/ppermute | solution.py:520
  542.5 53.8 %collective-permute-start.54 = (bf16[1,256,1024]{2,1,0:T(8,128)(2,1)}, bf16[1,256,1024]{2,1,0:T(8,128)(2,1)S(1)}, u32[]{:S(2)}, u32[]{:S(2)}) collective-permute-start(bf16[1,256,1024]{2,1,0:T(8,128)(2,1)} %constant_dynamic-slice_fusion.3), channel_id=1, source_target_pairs={{0,1},{1,0},{2,3},{3,2},{4,5},{5,4},{6,7},{7,6},{8,9},{9,8},{10,11... | collective-permute-start | bytes 1572872 | tf_op jit(solution)/shard_map/ppermute | solution.py:520
  598.6 55.8 %collective-permute-start.55 = (bf16[1,256,1024]{2,1,0:T(8,128)(2,1)}, bf16[1,256,1024]{2,1,0:T(8,128)(2,1)}, u32[]{:S(2)}, u32[]{:S(2)}) collective-permute-start(bf16[1,256,1024]{2,1,0:T(8,128)(2,1)} %get-tuple-element.197), channel_id=1, source_target_pairs={{0,2},{1,3},{2,0},{3,1},{4,6},{5,7},{6,4},{7,5},{8,10},{9,11},{10,... | collective-permute-start | bytes 1572872 | tf_op jit(solution)/shard_map/ppermute | solution.py:520
  600.0 58.6 %collective-permute-start.56 = (bf16[1,256,1024]{2,1,0:T(8,128)(2,1)S(1)}, bf16[1,256,1024]{2,1,0:T(8,128)(2,1)}, u32[]{:S(2)}, u32[]{:S(2)}) collective-permute-start(bf16[1,256,1024]{2,1,0:T(8,128)(2,1)S(1)} %get-tuple-element.196), channel_id=1, source_target_pairs={{0,3},{1,2},{2,1},{3,0},{4,7},{5,6},{6,5},{7,4},{8,11},{9,10},{10,... | collective-permute-start | bytes 1572872 | tf_op jit(solution)/shard_map/ppermute | solution.py:520
  607.3 53.2 %collective-permute-start.52 = (bf16[1,256,1024]{2,1,0:T(8,128)(2,1)}, bf16[1,256,1024]{2,1,0:T(8,128)(2,1)}, u32[]{:S(2)}, u32[]{:S(2)}) collective-permute-start(bf16[1,256,1024]{2,1,0:T(8,128)(2,1)} %get-tuple-element.200), channel_id=1, source_target_pairs={{0,2},{1,3},{2,0},{3,1},{4,6},{5,7},{6,4},{7,5},{8,10},{9,11},{10,... | collective-permute-start | bytes 1572872 | tf_op jit(solution)/shard_map/ppermute | solution.py:520
  608.7 53.6 %collective-permute-start.53 = (bf16[1,256,1024]{2,1,0:T(8,128)(2,1)}, bf16[1,256,1024]{2,1,0:T(8,128)(2,1)}, u32[]{:S(2)}, u32[]{:S(2)}) collective-permute-start(bf16[1,256,1024]{2,1,0:T(8,128)(2,1)} %get-tuple-element.199), channel_id=1, source_target_pairs={{0,3},{1,2},{2,1},{3,0},{4,7},{5,6},{6,5},{7,4},{8,11},{9,10},{10,... | collective-permute-start | bytes 1572872 | tf_op jit(solution)/shard_map/ppermute | solution.py:520
  617.0 47.3 %collective-permute-start.49 = (bf16[1,256,1024]{2,1,0:T(8,128)(2,1)}, bf16[1,256,1024]{2,1,0:T(8,128)(2,1)}, u32[]{:S(2)}, u32[]{:S(2)}) collective-permute-start(bf16[1,256,1024]{2,1,0:T(8,128)(2,1)} %get-tuple-element.203), channel_id=1, source_target_pairs={{0,2},{1,3},{2,0},{3,1},{4,6},{5,7},{6,4},{7,5},{8,10},{9,11},{10,... | collective-permute-start | bytes 1572872 | tf_op jit(solution)/shard_map/ppermute | solution.py:520
  (63 other events, 1197.8 us)
Sparse Core Ops, SparseCore 0:
  596.3 55.0 all-reduce.2

commit v2 on v0

--- a/solution.py
+++ b/solution.py
@@ -1,9 +1,1065 @@
+import functools
 import jax
 import jax.numpy as jnp
 from jax import lax
+from jax.experimental import pallas as pl
+from jax.experimental.pallas import tpu as pltpu
 from jax.sharding import PartitionSpec as P
 
 HEAD = 64
+F32 = jnp.float32
+BF16 = jnp.bfloat16
+LOG2E = 1.4426950408889634
+LN2 = 0.6931471805599453
+VMEM_LIMIT = 60 * 2**20
+ROWS = 256
+BLOCK = 256
+ANY = pl.BlockSpec(memory_space=pl.ANY)
+SMEM = pl.BlockSpec(memory_space=pltpu.SMEM)
+
+
+def cost(flops, moved):
+    return pl.CostEstimate(flops=int(flops * SHARE), bytes_accessed=int(moved * SHARE), transcendentals=0)
+
+
+SHARE = 1.0
+
+
+def nn(left, right):
+    return lax.dot_general(left, right, (((1,), (0,)), ((), ())), preferred_element_type=F32)
+
+
+def nt(left, right):
+    return lax.dot_general(left, right, (((1,), (1,)), ((), ())), preferred_element_type=F32)
+
+
+def tn(left, right):
+    return lax.dot_general(left, right, (((0,), (0,)), ((), ())), preferred_element_type=F32)
+
+
+def norm_rows(values):
+    center = values - jnp.mean(values, axis=-1, keepdims=True)
+    scale = lax.rsqrt(jnp.mean(center * center, axis=-1, keepdims=True) + 1e-05)
+    return center * scale, scale
+
+
+def norm_back_rows(grad, normed, scale, gain):
+    inner = grad * gain
+    middle = jnp.mean(inner, axis=-1, keepdims=True)
+    along = jnp.mean(inner * normed, axis=-1, keepdims=True)
+    return scale * (inner - middle - normed * along)
+
+
+def gelu_and_slope(v):
+    root = 0.7978845608028654
+    square = v * v
+    t = jnp.tanh(v * (root + (root * 0.044715) * square))
+    half = 0.5 + 0.5 * t
+    slope = half + (v * half) * (1.0 - t) * (root + (3.0 * root * 0.044715) * square)
+    return v * half, slope
+
+
+def head_rows(h):
+    return slice(h * HEAD, (h + 1) * HEAD)
+
+
+def natural(turn, p):
+    slot, t = p // 4, p % 4
+    return t ^ turn if slot == 3 else t
+
+
+def sum_rows(values):
+    return jnp.sum(values, axis=0, keepdims=True)
+
+
+def pack_heads_kernel(ids_ref, q_ref, k_ref, v_ref, o_ref, own_ref, piece_ref, *half_refs):
+    part = own_ref.shape[2]
+    turn = ids_ref[1]
+    for m, ref in enumerate((q_ref, k_ref, v_ref, o_ref)):
+        values = ref[...] if m == 3 else ref[...].T
+        for t in range(4):
+            own_ref[t, m] = values[t * part : (t + 1) * part]
+    piece_ref[0] = own_ref[turn]
+    for half_ref in half_refs:
+        for t in range(2):
+            half_ref[t] = own_ref[2 * (turn // 2) + t]
+
+
+def pack_units_kernel(ids_ref, up_ref, down_ref, ain_ref, aout_ref, bias_ref, own_ref, piece_ref):
+    units, extra = down_ref.shape[0] // 4, aout_ref.shape[0] // 4
+    turn = ids_ref[1]
+    turned = ain_ref[...].T
+    bias = bias_ref[...]
+    begin = 2 * units + 2 * extra
+    for t in range(4):
+        cols = slice(t * units, (t + 1) * units)
+        own_ref[t, :units] = up_ref[:, cols].T
+        own_ref[t, units : 2 * units] = down_ref[cols, :]
+        own_ref[t, 2 * units : 2 * units + extra] = turned[t * extra : (t + 1) * extra]
+        own_ref[t, 2 * units + extra : begin] = aout_ref[t * extra : (t + 1) * extra, :]
+        own_ref[t, begin:, : 4 * extra] = split_lines(bias)
+    piece_ref[0] = own_ref[turn]
+
+
+def split_lines(values):
+    rows, rest = [], values
+    for _ in range(3):
+        low = rest.astype(BF16)
+        rows.append(low)
+        rest = rest - low.astype(F32)
+    rows.append(jnp.zeros((13,) + values.shape[1:], BF16))
+    return jnp.concatenate(rows, axis=0)
+
+
+def pack(kernel, name, ids, own_shape, parts, *weights):
+    vmem = pl.BlockSpec(memory_space=pltpu.VMEM)
+    return pl.pallas_call(
+        kernel,
+        in_specs=[SMEM] + [vmem] * len(weights),
+        out_specs=[vmem] * len(parts),
+        out_shape=[jax.ShapeDtypeStruct((n,) + own_shape, BF16) for n in parts],
+        compiler_params=pltpu.CompilerParams(vmem_limit_bytes=VMEM_LIMIT),
+        cost_estimate=cost(0, 8 * 2**20),
+        name=name,
+    )(ids, *weights)
+
+
+def attend_kernel(causal, count, first, homes, ids_ref, *refs):
+    refs = list(refs)
+    xq_hbm = refs.pop(0)
+    xkv_hbm = xq_hbm if causal else refs.pop(0)
+    sources_of = [refs.pop(0) for _ in range(len(set(n for n, _ in homes)))]
+    if not first:
+        refs = refs[4:]
+    e_ref, hd_ref, il_ref, ctx_ref, xq, xkv, weights, qkv, x_sems, w_sems = refs
+    if causal:
+        xkv = xq
+    step = pl.program_id(0)
+    span, sources = xq.shape[0], xkv.shape[0]
+    part = weights.shape[2] // 4
+
+    def weight_copy(s, t):
+        n, index = homes[4 * s + t]
+        return pltpu.make_async_copy(
+            sources_of[n].at[index, pl.ds(0, 3)],
+            weights.at[s, :, pl.ds(t * part, part), :],
+            w_sems.at[4 * s + t],
+        )
+
+    x_copies = [pltpu.make_async_copy(xq_hbm, xq, x_sems.at[0])]
+    if not causal:
+        x_copies.append(pltpu.make_async_copy(xkv_hbm, xkv, x_sems.at[1]))
+
+    @pl.when(step == 0)
+    def _():
+        for t in range(4):
+            weight_copy(0, t).start()
+        for copy in x_copies:
+            copy.start()
+        for s in range(1, count):
+            for t in range(4):
+                weight_copy(s, t).start()
+        for copy in x_copies:
+            copy.wait()
+
+    for s in range(count):
+
+        @pl.when(step == 2 * s)
+        def _():
+            for t in range(4):
+                weight_copy(s, t).wait()
+            qkv[0] = (nt(weights[s, 0], xq[...]) * (LOG2E * HEAD**-0.5)).astype(BF16)
+            qkv[1] = nt(weights[s, 1], xkv[...]).astype(BF16)
+            qkv[2] = nt(weights[s, 2], xkv[...]).astype(BF16)
+
+    pair = pl.ds(pl.multiple_of((step % 2) * 128, 128), 128)
+    q2, k2, v2 = qkv[0, pair, :], qkv[1, pair, :], qkv[2, pair, :]
+    hd_ref[0], hd_ref[1], hd_ref[2] = q2, k2, v2
+    block = min(BLOCK, span)
+    work = [(i, h) for i in range(span // block) for h in range(2)]
+
+    def reach(i):
+        return (i + 1) * block if causal else sources
+
+    def score(i, h):
+        return tn(k2[head_rows(h), : reach(i)], q2[head_rows(h), i * block : (i + 1) * block])
+
+    ahead = 2 if causal else 4
+    waiting = [score(i, h) for i, h in work[:ahead]]
+    for number, (i, h) in enumerate(work):
+        n, cols = reach(i), slice(i * block, (i + 1) * block)
+        s = waiting.pop(0)
+        if number + ahead < len(work):
+            waiting.append(score(*work[number + ahead]))
+        if causal:
+            key = lax.broadcasted_iota(jnp.int32, (block, block), 0)
+            query = lax.broadcasted_iota(jnp.int32, (block, block), 1)
+            tail = jnp.where(key <= query, s[n - block :], -1e9)
+            s = jnp.concatenate([s[: n - block], tail], axis=0) if n > block else tail
+        else:
+            key = lax.broadcasted_iota(jnp.int32, (n, block), 0)
+            s = jnp.where(key < ids_ref[2], s, -1e9)
+        e = jnp.exp2(s - jnp.max(s, axis=0, keepdims=True))
+        inverse = 1.0 / jnp.sum(e, axis=0, keepdims=True)
+        low = e.astype(BF16)
+        e_ref[h, :n, cols] = low
+        il_ref[h, :, cols] = inverse
+        context = (nn(v2[head_rows(h), :n], low) * inverse).astype(BF16)
+        hd_ref[3, head_rows(h), cols] = context
+        contexts = [context] if h == 0 else contexts + [context]
+        if h == 1:
+            ctx_ref[cols, :] = jnp.concatenate(contexts, axis=0).T
+
+
+def gather_homes(pieces):
+    arrays, homes = [], []
+    for array, index in pieces:
+        where = [n for n, known in enumerate(arrays) if known is array]
+        if not where:
+            arrays.append(array)
+            where = [len(arrays) - 1]
+        homes.append((where[0], index))
+    return arrays, tuple(homes)
+
+
+def attend_slots(ids, slots, xq, xkv, pieces, before):
+    causal = xkv is None
+    span, width = xq.shape
+    sources = span if causal else xkv.shape[0]
+    heads = width // HEAD
+    count, base = len(slots), 2 * slots[0]
+    arrays, homes = gather_homes([pieces[4 * s + t] for s in slots for t in range(4)])
+    part = arrays[0].shape[2]
+    first = before is None
+    operands = [ids, xq] + ([] if causal else [xkv]) + arrays
+    specs = [SMEM] + [ANY] * (len(operands) - 1)
+    aliases = {}
+    if not first:
+        aliases = {len(operands) + n: n for n in range(4)}
+        operands += list(before)
+        specs += [ANY] * 4
+    return pl.pallas_call(
+        functools.partial(attend_kernel, causal, count, first, homes),
+        grid=(2 * count,),
+        in_specs=specs,
+        out_specs=(
+            pl.BlockSpec((2, sources, span), lambda j: (base + j, 0, 0)),
+            pl.BlockSpec((4, 128, span), lambda j: (0, base + j, 0)),
+            pl.BlockSpec((2, 1, span), lambda j: (base + j, 0, 0)),
+            pl.BlockSpec((span, 128), lambda j: (0, base + j)),
+        ),
+        out_shape=(
+            jax.ShapeDtypeStruct((heads, sources, span), BF16),
+            jax.ShapeDtypeStruct((4, width, span), BF16),
+            jax.ShapeDtypeStruct((heads, 1, span), F32),
+            jax.ShapeDtypeStruct((span, width), BF16),
+        ),
+        scratch_shapes=[
+            pltpu.VMEM((span, width), BF16),
+            pltpu.VMEM((16, 128) if causal else (sources, width), BF16),
+            pltpu.VMEM((count, 3, 4 * part, width), BF16),
+            pltpu.VMEM((3, 4 * part, max(span, sources)), BF16),
+            pltpu.SemaphoreType.DMA((2,)),
+            pltpu.SemaphoreType.DMA((4 * count,)),
+        ],
+        input_output_aliases=aliases,
+        compiler_params=pltpu.CompilerParams(vmem_limit_bytes=VMEM_LIMIT),
+        cost_estimate=cost(count * 10 * 10**9, count * 12 * 2**20),
+        name="self_attend" if causal else "cross_attend",
+    )(*operands)
+
+
+def out_norm_kernel(homes, *refs):
+    refs = list(refs)
+    ctx_ref, x_ref, gain_ref, shift_ref = refs[:4]
+    sources = refs[4:-5]
+    low_ref, n_ref, r_ref, wo, sems = refs[-5:]
+    part = wo.shape[0] // len(homes)
+    copies = [
+        pltpu.make_async_copy(sources[n].at[index, 3], wo.at[pl.ds(p * part, part), :], sems.at[p])
+        for p, (n, index) in enumerate(homes)
+    ]
+
+    @pl.when(pl.program_id(0) == 0)
+    def _():
+        for copy in copies:
+            copy.start()
+        for copy in copies:
+            copy.wait()
+
+    rows_here = ctx_ref.shape[0]
+    for i in range(rows_here // ROWS):
+        rows = slice(i * ROWS, (i + 1) * ROWS)
+        total = nn(ctx_ref[rows, :], wo[...]) + x_ref[rows, :].astype(F32)
+        normed, scale = norm_rows(total)
+        low_ref[rows, :] = (normed * gain_ref[...] + shift_ref[...]).astype(BF16)
+        n_ref[rows, :] = normed.astype(BF16)
+        r_ref[rows, :] = scale
+
+
+def out_norm(ctx, pieces, residual, gain, shift):
+    span, width = ctx.shape
+    arrays, homes = gather_homes(pieces)
+    block = min(512, span)
+    rows = lambda w: pl.BlockSpec((block, w), lambda i: (i, 0))
+    line = pl.BlockSpec((1, width), lambda i: (0, 0))
+    return pl.pallas_call(
+        functools.partial(out_norm_kernel, homes),
+        grid=(span // block,),
+        in_specs=[rows(width), rows(width), line, line] + [ANY] * len(arrays),
+        out_specs=(rows(width), rows(width), rows(1)),
+        out_shape=(
+            jax.ShapeDtypeStruct((span, width), BF16),
+            jax.ShapeDtypeStruct((span, width), BF16),
+            jax.ShapeDtypeStruct((span, 1), F32),
+        ),
+        scratch_shapes=[pltpu.VMEM((width, width), BF16), pltpu.SemaphoreType.DMA((len(homes),))],
+        compiler_params=pltpu.CompilerParams(vmem_limit_bytes=VMEM_LIMIT),
+        cost_estimate=cost(2 * span * width * width, 10 * 2**20),
+        name="out_norm",
+    )(ctx, residual, gain, shift, *arrays)
+
+
+def feed_kernel(slots, first, last, units, extra, homes, ids_ref, *refs):
+    count = len(slots)
+    refs = list(refs)
+    x_ref = refs.pop(0)
+    sources = [refs.pop(0) for _ in range(len(set(n for n, _ in homes)))]
+    if last:
+        shift_a_ref, gain_ref, shift_ref, grad_ref = [refs.pop(0) for _ in range(4)]
+    if not first:
+        acc_hbm = refs.pop(0)
+        refs = refs[3:]
+    gp_ref, gpa_ref, alow_ref = [refs.pop(0) for _ in range(3)]
+    if last:
+        out_ref, low_ref, sum_ref = [refs.pop(0) for _ in range(3)]
+    acc, up, down, ain, aout, bias, w_sems, b_sems, acc_sem = refs
+    step = pl.program_id(0)
+    span = x_ref.shape[0]
+
+    def piece_copies(p):
+        n, index = homes[p]
+        there = 4 * (p // 4) + natural(ids_ref[1], 4 * slots[0] + p)
+        parts = (
+            (0, units, up, p),
+            (units, units, down, p),
+            (2 * units, extra, ain, there),
+            (2 * units + extra, extra, aout, there),
+        )
+        found = [
+            pltpu.make_async_copy(
+                sources[n].at[index, pl.ds(begin, size), :],
+                held.at[pl.ds(to * size, size), :],
+                w_sems.at[p, m],
+            )
+            for m, (begin, size, held, to) in enumerate(parts)
+        ]
+        if p % 4 == 0:
+            found.append(
+                pltpu.make_async_copy(
+                    sources[n].at[index, pl.ds(2 * units + 2 * extra, 16), pl.ds(0, 4 * extra)],
+                    bias.at[p // 4],
+                    b_sems.at[p // 4],
+                )
+            )
+        return found
+
+    def acc_copy():
+        return pltpu.make_async_copy(acc_hbm, acc, acc_sem)
+
+    @pl.when(step == 0)
+    def _():
+        for p in range(4 * count):
+            for copy in piece_copies(p):
+                copy.start()
+        if first:
+            acc[...] = jnp.zeros_like(acc)
+        else:
+            acc_copy().start()
+            acc_copy().wait()
+
+    for s in range(count):
+
+        @pl.when(step == 2 * s)
+        def _():
+            for p in range(4 * s, 4 * s + 4):
+                for copy in piece_copies(p):
+                    copy.wait()
+            rows = slice(4 * extra * s, 4 * extra * (s + 1))
+            a, slope = gelu_and_slope(nt(x_ref[...], ain[rows, :]) + sum_rows(bias[s].astype(F32)))
+            a_low = a.astype(BF16)
+            alow_ref[...] = a_low
+            gpa_ref[...] = slope.astype(BF16)
+            acc[...] += 4.0 * nn(a_low, aout[rows, :])
+
+    chunk = pl.ds(pl.multiple_of(step * (2 * units), 2 * units), 2 * units)
+    half = min(512, span)
+    for i in range(span // half):
+        rows = slice(i * half, (i + 1) * half)
+        h, slope = gelu_and_slope(nt(x_ref[rows, :], up[chunk, :]))
+        gp_ref[rows, :] = slope.astype(BF16)
+        acc[rows, :] += nn(h.astype(BF16), down[chunk, :])
+
+    if last:
+
+        @pl.when(step == pl.num_programs(0) - 1)
+        def _():
+            sum_ref[...] = jnp.zeros_like(sum_ref)
+            for i in range(span // ROWS):
+                rows = slice(i * ROWS, (i + 1) * ROWS)
+                total = acc[rows, :] + x_ref[rows, :].astype(F32) + 4.0 * shift_a_ref[...]
+                normed, scale = norm_rows(total)
+                out_ref[rows, :] = (normed * gain_ref[...] + shift_ref[...]).astype(BF16)
+                grad = grad_ref[rows, :].astype(F32)
+                back = norm_back_rows(grad, normed, scale, gain_ref[...])
+                low_ref[rows, :] = back.astype(BF16)
+                sum_ref[0:1, :] += sum_rows(grad * normed)
+                sum_ref[1:2, :] += sum_rows(grad)
+                sum_ref[2:3, :] += 4.0 * sum_rows(back)
+
+
+def feed_slots(ids, slots, x, pieces, before, norm, units, extra):
+    span, width = x.shape
+    first, last = before is None, norm is not None
+    count = len(slots)
+    whole = lambda a: pl.BlockSpec(a.shape, lambda j: (0,) * a.ndim, pipeline_mode=pl.Buffered(1))
+    arrays, homes = gather_homes([pieces[4 * s + t] for s in slots for t in range(4)])
+    operands = [ids, x] + arrays
+    specs = [SMEM, whole(x)] + [ANY] * len(arrays)
+    if last:
+        operands += list(norm)
+        specs += [whole(a) for a in norm]
+    kept_shape = [
+        jax.ShapeDtypeStruct((span, 16 * units), BF16),
+        jax.ShapeDtypeStruct((span, 16 * extra), BF16),
+        jax.ShapeDtypeStruct((span, 16 * extra), BF16),
+    ]
+    kept_specs = [
+        pl.BlockSpec((span, 2 * units), lambda j: (0, 2 * slots[0] + j)),
+        pl.BlockSpec((span, 4 * extra), lambda j: (0, slots[0] + j // 2)),
+        pl.BlockSpec((span, 4 * extra), lambda j: (0, slots[0] + j // 2)),
+    ]
+    aliases = {}
+    if not first:
+        aliases = {len(operands) + 1 + n: n for n in range(3)}
+        operands += list(before)
+        specs += [ANY] * 4
+    total = jax.ShapeDtypeStruct((span, width), F32)
+    once = lambda s: pl.BlockSpec(s.shape, lambda j: (0,) * len(s.shape), pipeline_mode=pl.Buffered(1))
+    if last:
+        low = jax.ShapeDtypeStruct((span, width), BF16)
+        more = [low, low, jax.ShapeDtypeStruct((8, width), F32)]
+        scratch = [pltpu.VMEM((span, width), F32)]
+    else:
+        more, scratch = [total], []
+    outs = pl.pallas_call(
+        functools.partial(feed_kernel, slots, first, last, units, extra, homes),
+        grid=(2 * count,),
+        in_specs=specs,
+        out_specs=kept_specs + [once(s) for s in more],
+        out_shape=kept_shape + more,
+        scratch_shapes=scratch
+        + [
+            pltpu.VMEM((count * 4 * units, width), BF16),
+            pltpu.VMEM((count * 4 * units, width), BF16),
+            pltpu.VMEM((count * 4 * extra, width), BF16),
+            pltpu.VMEM((count * 4 * extra, width), BF16),
+            pltpu.VMEM((count, 16, 4 * extra), BF16),
+            pltpu.SemaphoreType.DMA((4 * count, 4)),
+            pltpu.SemaphoreType.DMA((count,)),
+            pltpu.SemaphoreType.DMA,
+        ],
+        input_output_aliases=aliases,
+        compiler_params=pltpu.CompilerParams(vmem_limit_bytes=VMEM_LIMIT),
+        cost_estimate=cost(count * 6 * 10**9, count * 14 * 2**20),
+        name="feed",
+    )(*operands)
+    kept, rest = list(outs[:3]), list(outs[3:])
+    return kept, rest
+
+
+def adapter_back_kernel(extra, units, homes, ids_ref, *refs):
+    refs = list(refs)
+    g_ref, x_ref, gpa_ref, alow_ref = refs[:4]
+    low_ref, *slot_refs, aout, sems = refs[-7:]
+    sources = refs[4:-7]
+    begin = 2 * units + extra
+    copies = []
+    for p, (n, index) in enumerate(homes):
+        there = 4 * (p // 4) + natural(ids_ref[1], p)
+        copies.append(
+            pltpu.make_async_copy(
+                sources[n].at[index, pl.ds(begin, extra), :],
+                aout.at[pl.ds(there * extra, extra), :],
+                sems.at[p],
+            )
+        )
+    for copy in copies:
+        copy.start()
+    for copy in copies:
+        copy.wait()
+    g = g_ref[...]
+    a = 4.0 * nt(g, aout[...]) * gpa_ref[...].astype(F32)
+    bias = sum_rows(a)
+    a_low = a.astype(BF16)
+    low_ref[...] = a_low
+    in_grad = tn(a_low, x_ref[...]).astype(BF16)
+    out_grad = (4.0 * tn(alow_ref[...], g)).astype(BF16)
+    size = 4 * extra
+    for k in range(4):
+        rows = slice(k * size, (k + 1) * size)
+        slot_refs[k][:size] = in_grad[rows]
+        slot_refs[k][size : 2 * size] = out_grad[rows]
+        slot_refs[k][2 * size :] = jnp.zeros((16, g.shape[1]), BF16)
+        slot_refs[k][2 * size :, :size] = split_lines(bias[:, rows])
+
+
+def adapter_back(ids, g, x, gpa, alow, pieces, units, extra):
+    span, width = g.shape
+    arrays, homes = gather_homes(pieces)
+    vmem = pl.BlockSpec(memory_space=pltpu.VMEM)
+    outs = pl.pallas_call(
+        functools.partial(adapter_back_kernel, extra, units, homes),
+        in_specs=[SMEM] + [vmem] * 4 + [ANY] * len(arrays),
+        out_specs=[vmem] * 5,
+        out_shape=[jax.ShapeDtypeStruct((span, 16 * extra), BF16)]
+        + [jax.ShapeDtypeStruct((8 * extra + 16, width), BF16)] * 4,
+        scratch_shapes=[pltpu.VMEM((16 * extra, width), BF16), pltpu.SemaphoreType.DMA((16,))],
+        compiler_params=pltpu.CompilerParams(vmem_limit_bytes=VMEM_LIMIT),
+        cost_estimate=cost(6 * span * width * 16 * extra, 12 * 2**20),
+        name="adapter_back",
+    )(ids, g, x, gpa, alow, *arrays)
+    return outs[0], list(outs[1:])
+
+
+def feed_back_kernel(units, extra, homes, ids_ref, *refs):
+    refs = list(refs)
+    g_ref, gp_ref, alow_ref, n_ref, r_ref, gain_ref = refs[:6]
+    low_ref, sum_ref, acc, up, down, ain, w_sems, a_sems = refs[-8:]
+    sources = refs[6:-8]
+    step = pl.program_id(0)
+    steps = len(homes) // 2
+    span = g_ref.shape[0]
+
+    def chunk_copies(j, home):
+        copies = []
+        for t in range(2):
+            n, index = homes[2 * home + t]
+            for m, held in enumerate((up, down)):
+                copies.append(
+                    pltpu.make_async_copy(
+                        sources[n].at[index, pl.ds(m * units, units), :],
+                        held.at[j % 2, pl.ds(t * units, units), :],
+                        w_sems.at[j % 2, t, m],
+                    )
+                )
+        return copies
+
+    def ain_copies():
+        return [
+            pltpu.make_async_copy(
+                sources[n].at[index, pl.ds(2 * units, extra), :],
+                ain.at[pl.ds((4 * (p // 4) + natural(ids_ref[1], p)) * extra, extra), :],
+                a_sems.at[p],
+            )
+            for p, (n, index) in enumerate(homes)
+        ]
+
+    @pl.when(step == 0)
+    def _():
+        for copy in ain_copies():
+            copy.start()
+        for copy in chunk_copies(0, 0):
+            copy.start()
+        for copy in ain_copies():
+            copy.wait()
+        acc[...] = nn(alow_ref[...], ain[...]) + g_ref[...].astype(F32)
+
+    for j in range(1, steps):
+
+        @pl.when(step == j - 1)
+        def _():
+            for copy in chunk_copies(j, j):
+                copy.start()
+
+    for copy in chunk_copies(step, 0):
+        copy.wait()
+    half = min(512, span)
+    side = step % 2
+    for i in range(span // half):
+        rows = slice(i * half, (i + 1) * half)
+        h = (nt(g_ref[rows, :], down[side]) * gp_ref[rows, :].astype(F32)).astype(BF16)
+        acc[rows, :] += nn(h, up[side])
+
+    @pl.when(step == pl.num_programs(0) - 1)
+    def _():
+        sum_ref[...] = jnp.zeros_like(sum_ref)
+        for i in range(span // ROWS):
+            rows = slice(i * ROWS, (i + 1) * ROWS)
+            grad = acc[rows, :]
+            normed = n_ref[rows, :].astype(F32)
+            back = norm_back_rows(grad, normed, r_ref[rows, :], gain_ref[...])
+            low_ref[rows, :] = back.astype(BF16)
+            sum_ref[0:1, :] += sum_rows(grad * normed)
+            sum_ref[1:2, :] += sum_rows(grad)
+
+
+def feed_back(ids, g, slopes, a_low, pieces, normed, scale, gain, units, extra):
+    span, width = g.shape
+    arrays, homes = gather_homes(pieces)
+    whole = lambda a: pl.BlockSpec(a.shape, lambda j: (0,) * a.ndim, pipeline_mode=pl.Buffered(1))
+    out_shape = (jax.ShapeDtypeStruct((span, width), BF16), jax.ShapeDtypeStruct((8, width), F32))
+    return pl.pallas_call(
+        functools.partial(feed_back_kernel, units, extra, homes),
+        grid=(8,),
+        in_specs=[
+            SMEM,
+            whole(g),
+            pl.BlockSpec((span, 2 * units), lambda j: (0, j)),
+            whole(a_low),
+            whole(normed),
+            whole(scale),
+            whole(gain),
+        ]
+        + [ANY] * len(arrays),
+        out_specs=tuple(
+            pl.BlockSpec(s.shape, lambda j: (0, 0), pipeline_mode=pl.Buffered(1)) for s in out_shape
+        ),
+        out_shape=out_shape,
+        scratch_shapes=[
+            pltpu.VMEM((span, width), F32),
+            pltpu.VMEM((2, 2 * units, width), BF16),
+            pltpu.VMEM((2, 2 * units, width), BF16),
+            pltpu.VMEM((16 * extra, width), BF16),
+            pltpu.SemaphoreType.DMA((2, 2, 2)),
+            pltpu.SemaphoreType.DMA((16,)),
+        ],
+        compiler_params=pltpu.CompilerParams(vmem_limit_bytes=VMEM_LIMIT),
+        cost_estimate=cost(20 * 10**9, 40 * 2**20),
+        name="feed_back",
+    )(ids, g, slopes, a_low, normed, scale, gain, *arrays)
+
+
+def attention_back_kernel(causal, homes, *refs):
+    refs = list(refs)
+    g_ref, e_ref, hd_ref, il_ref = refs[:4]
+    refs = refs[4:]
+    if not causal:
+        n_ref, r_ref, gain_ref = [refs.pop(0) for _ in range(3)]
+    sources_of = [refs.pop(0) for _ in range(len(set(n for n, _ in homes)))]
+    if causal:
+        passed_hbm = refs.pop(0)
+    out_ref = refs.pop(0)
+    if causal:
+        put_hbm = refs.pop(0)
+    else:
+        low_ref, sum_ref = [refs.pop(0) for _ in range(2)]
+    wf, ct, dq, dk, dv, sems = refs[:6]
+    step = pl.program_id(0)
+    if causal:
+        passing, pass_sems = refs[6:]
+        bring = pltpu.make_async_copy(passed_hbm, passing, pass_sems.at[0])
+        put = pltpu.make_async_copy(passing, put_hbm, pass_sems.at[1])
+
+        @pl.when(step == 1)
+        def _():
+            bring.start()
+
+        @pl.when(step == 3)
+        def _():
+            bring.wait()
+            put.start()
+
+        @pl.when(step == pl.num_programs(0) - 1)
+        def _():
+            put.wait()
+
+    span = g_ref.shape[0]
+    sources = e_ref.shape[1]
+    part = wf.shape[1] // len(homes)
+
+    def copies(wanted):
+        found = []
+        for p, (n, index) in enumerate(homes):
+            begin, size = (3, 1) if wanted else (0, 3)
+            found.append(
+                pltpu.make_async_copy(
+                    sources_of[n].at[index, pl.ds(begin, size)],
+                    wf.at[pl.ds(begin, size), pl.ds(p * part, part), :],
+                    sems.at[wanted, p],
+                )
+            )
+        return found
+
+    @pl.when(step == 0)
+    def _():
+        for copy in copies(1) + copies(0):
+            copy.start()
+        for copy in copies(1):
+            copy.wait()
+        ct[...] = nt(wf[3], g_ref[...]).astype(BF16)
+
+    pair = pl.ds(pl.multiple_of(step * 128, 128), 128)
+    c2 = ct[pair, :]
+    block = min(BLOCK if causal else 512, span)
+    scaled, dots = [], []
+    for h in range(2):
+        c = c2[head_rows(h), :].astype(F32) * il_ref[h]
+        dots.append(jnp.sum(c * hd_ref[3, head_rows(h), :].astype(F32), axis=0, keepdims=True))
+        scaled.append(c.astype(BF16))
+    sums_k, sums_v = [None, None], [None, None]
+    for i in reversed(range(span // block)):
+        n = (i + 1) * block if causal else sources
+        cols = slice(i * block, (i + 1) * block)
+        grads = [tn(hd_ref[2, head_rows(h), :n], scaled[h][:, cols]) for h in range(2)]
+        queries = []
+        for h in range(2):
+            e = e_ref[h, :n, cols]
+            ds = (e.astype(F32) * (grads[h] - dots[h][:, cols])).astype(BF16)
+            queries.append((nn(hd_ref[1, head_rows(h), :n], ds) * HEAD**-0.5).astype(BF16))
+            gk = nn(ds, hd_ref[0, head_rows(h), cols].T)
+            gv = nn(e, scaled[h][:, cols].T)
+            if sums_k[h] is None:
+                sums_k[h], sums_v[h] = gk, gv
+            elif n == sums_k[h].shape[0]:
+                sums_k[h], sums_v[h] = sums_k[h] + gk, sums_v[h] + gv
+            else:
+                sums_k[h] = jnp.concatenate([sums_k[h][:n] + gk, sums_k[h][n:]], axis=0)
+                sums_v[h] = jnp.concatenate([sums_v[h][:n] + gv, sums_v[h][n:]], axis=0)
+        dq[cols, pair] = jnp.concatenate(queries, axis=0).T
+    dk[:, pair] = (jnp.concatenate(sums_k, axis=1) * LN2).astype(BF16)
+    dv[:, pair] = jnp.concatenate(sums_v, axis=1).astype(BF16)
+
+    @pl.when(step == pl.num_programs(0) - 1)
+    def _():
+        for copy in copies(0):
+            copy.wait()
+        for i in range(sources // ROWS):
+            rows = slice(i * ROWS, (i + 1) * ROWS)
+            total = nn(dk[rows, :], wf[1]) + nn(dv[rows, :], wf[2])
+            if causal:
+                total = total + nn(dq[rows, :], wf[0]) + g_ref[rows, :].astype(F32)
+            out_ref[rows, :] = total.astype(BF16)
+        if not causal:
+            sum_ref[...] = jnp.zeros_like(sum_ref)
+            for i in range(span // ROWS):
+                rows = slice(i * ROWS, (i + 1) * ROWS)
+                grad = nn(dq[rows, :], wf[0]) + g_ref[rows, :].astype(F32)
+                normed = n_ref[rows, :].astype(F32)
+                back = norm_back_rows(grad, normed, r_ref[rows, :], gain_ref[...])
+                low_ref[rows, :] = back.astype(BF16)
+                sum_ref[0:1, :] += sum_rows(grad * normed)
+                sum_ref[1:2, :] += sum_rows(grad)
+
+
+def attention_back(g, kept, pieces, norm, passed=None):
+    e, hd, il, _ = kept
+    causal = norm is None
+    span, width = g.shape
+    heads, sources, _ = e.shape
+    arrays, homes = gather_homes(pieces)
+    whole = lambda a: pl.BlockSpec(a.shape, lambda j: (0,) * a.ndim, pipeline_mode=pl.Buffered(1))
+    operands = [g, e, hd, il]
+    specs = [
+        whole(g),
+        pl.BlockSpec((2, sources, span), lambda j: (j, 0, 0)),
+        pl.BlockSpec((4, 128, span), lambda j: (0, j, 0)),
+        pl.BlockSpec((2, 1, span), lambda j: (j, 0, 0)),
+    ]
+    out_shape = [jax.ShapeDtypeStruct((sources, width), BF16)]
+    if not causal:
+        operands += list(norm)
+        specs += [whole(a) for a in norm]
+        out_shape += [jax.ShapeDtypeStruct((span, width), BF16), jax.ShapeDtypeStruct((8, width), F32)]
+    out_specs = [pl.BlockSpec(s.shape, lambda j: (0, 0), pipeline_mode=pl.Buffered(1)) for s in out_shape]
+    scratch = []
+    if causal:
+        arrays = arrays + [passed]
+        out_shape.append(jax.ShapeDtypeStruct(passed.shape, passed.dtype))
+        out_specs.append(ANY)
+        scratch = [pltpu.VMEM(passed.shape, passed.dtype), pltpu.SemaphoreType.DMA((2,))]
+    return pl.pallas_call(
+        functools.partial(attention_back_kernel, causal, homes),
+        grid=(heads // 2,),
+        in_specs=specs + [ANY] * len(arrays),
+        out_specs=out_specs,
+        out_shape=out_shape,
+        scratch_shapes=[
+            pltpu.VMEM((4, width, width), BF16),
+            pltpu.VMEM((width, span), BF16),
+            pltpu.VMEM((span, width), BF16),
+            pltpu.VMEM((sources, width), BF16),
+            pltpu.VMEM((sources, width), BF16),
+            pltpu.SemaphoreType.DMA((2, len(homes))),
+        ]
+        + scratch,
+        compiler_params=pltpu.CompilerParams(vmem_limit_bytes=VMEM_LIMIT),
+        cost_estimate=cost(40 * 10**9, 60 * 2**20),
+        name="self_back" if causal else "cross_back",
+    )(*operands, *arrays)
+
+
+def copy_kernel(from_ref, to_ref):
+    to_ref[...] = from_ref[...]
+
+
+def copied(values):
+    spec = pl.BlockSpec((1,) + values.shape[1:], lambda i: (i, 0, 0))
+    return pl.pallas_call(
+        copy_kernel,
+        grid=(values.shape[0],),
+        in_specs=[spec],
+        out_specs=spec,
+        out_shape=jax.ShapeDtypeStruct(values.shape, values.dtype),
+        cost_estimate=cost(0, 4 * 2**20),
+        name="copied",
+    )(values)
+
+
+def swap(values, name, bit):
+    size = lax.axis_size(name)
+    return lax.ppermute(values, name, [(i, i ^ bit) for i in range(size)])
+
+
+def cross_swap(values, even, odd):
+    size = lax.axis_size("tensor")
+    pairs = []
+    for d in range(lax.axis_size("dp")):
+        for i in range(size):
+            pairs.append((d * size + i, d * size + (i ^ (odd if d % 2 else even))))
+    return lax.ppermute(values, ("dp", "tensor"), pairs)
+
+
+def turn_over(values):
+    return lax.all_to_all(values, "tensor", 0, 0, tiled=True)
+
+
+def add_low(left, right):
+    return (left.astype(F32) + right.astype(F32)).astype(BF16)
+
+
+def after(values, *earlier):
+    return lax.optimization_barrier((values, earlier))[0]
+
+
+def send_near(what, half, piece):
+    with jax.named_scope(what + "_near"):
+        return cross_swap(half, 1, 2), swap(piece, "tensor", 3)
+
+
+def all_pieces(*arrays):
+    return [(array, t) for array in arrays for t in range(array.shape[0])]
+
+
+def whole_sequences(
+    inputs,
+    encoded,
+    source_lengths,
+    query_weight,
+    key_weight,
+    value_weight,
+    output_weight,
+    cross_query,
+    cross_key,
+    cross_value,
+    cross_output,
+    up_weight,
+    down_weight,
+    adapter_in,
+    adapter_out,
+    adapter_bias,
+    adapter_shift,
+    norm_gains,
+    norm_shifts,
+    output_grad,
+):
+    place = lax.axis_index("tensor")
+    turn = lax.axis_index("dp") % 4
+    _, share, width = inputs.shape
+    span = 4 * share
+    units, extra = up_weight.shape[1] // 4, adapter_in.shape[1] // 4
+    length = lax.dynamic_index_in_dim(source_lengths, place, 0, keepdims=False)
+    ids = jnp.stack([place, turn, length]).astype(jnp.int32)
+    gain = lambda j: norm_gains[j : j + 1]
+    shift = lambda j: norm_shifts[j : j + 1]
+    heads_shape = (4, output_weight.shape[0] // 4, width)
+    units_shape = (2 * units + 2 * extra + 16, width)
+
+    x = turn_over(inputs).reshape(span, width)
+    self_own, self_piece, self_half = pack(
+        pack_heads_kernel, "pack_self", ids, heads_shape, (4, 1, 2), query_weight, key_weight, value_weight, output_weight
+    )
+    self_near = send_near("self", self_half, self_piece)
+    cross_own, cross_piece = pack(
+        pack_heads_kernel,
+        "pack_cross",
+        after(ids, self_half),
+        heads_shape,
+        (4, 1),
+        cross_query,
+        cross_key,
+        cross_value,
+        cross_output,
+    )
+    feed_own, feed_piece = pack(
+        pack_units_kernel,
+        "pack_feed",
+        after(ids, cross_piece),
+        units_shape,
+        (4, 1),
+        up_weight,
+        down_weight,
+        adapter_in,
+        adapter_out,
+        adapter_bias.reshape(1, -1),
+    )
+    x = after(x, feed_piece)
+    source = turn_over(after(encoded, x)).reshape(span, width)
+    cross_near = send_near("cross", cross_own, cross_piece)
+    self_kept = attend_slots(ids, (0,), x, None, all_pieces(self_own), None)
+
+    half, piece = after(self_near, self_kept[0])
+    with jax.named_scope("self_far"):
+        far_half, far_piece = swap(half, "dp", 2), swap(piece, "dp", 2)
+    with jax.named_scope("self_core"):
+        core_half, core_piece = swap(half, "dp", 1), swap(piece, "dp", 1)
+        core_far_half = swap(far_half, "dp", 1)
+    shard = after(cross_near[0], far_half)
+    self_pieces = all_pieces(self_own, half, far_half, core_half, core_far_half)
+    self_kept = attend_slots(ids, (1, 2), after(x, piece, shard), None, self_pieces, self_kept)
+    with jax.named_scope("self_core"):
+        core_far_piece = swap(after(far_piece, self_kept[0]), "dp", 1)
+    self_pieces += all_pieces(piece, core_piece, far_piece, core_far_piece)
+    feed_near = send_near("feed", after(feed_own, self_kept[0]), after(feed_piece, self_kept[0]))
+    shard, piece = after(shard, self_kept[0]), after(cross_near[1], self_kept[0])
+    with jax.named_scope("cross_far"):
+        far_piece = swap(piece, "dp", 2)
+    with jax.named_scope("cross_core"):
+        core_shard, core_piece = swap(shard, "dp", 1), swap(piece, "dp", 1)
+    self_kept = attend_slots(ids, (3,), after(x, piece), None, self_pieces, self_kept)
+    first, normed_one, scale_one = out_norm(self_kept[3], self_pieces, x, gain(0), shift(0))
+
+    with jax.named_scope("cross_core"):
+        core_far_piece = swap(after(far_piece, first), "dp", 1)
+    cross_pieces = all_pieces(cross_own, shard)
+    cross_kept = attend_slots(
+        ids, (0, 1), after(first, core_shard, core_piece, core_far_piece), source, cross_pieces, None
+    )
+    cross_pieces += all_pieces(core_shard, piece, core_piece, far_piece, core_far_piece)
+    cross_kept = attend_slots(ids, (2, 3), first, source, cross_pieces, cross_kept)
+    shard = after(feed_near[0], cross_kept[0])
+    grad = turn_over(after(output_grad, cross_kept[0])).reshape(span, width)
+    second, normed_two, scale_two = out_norm(
+        cross_kept[3], cross_pieces, after(first, shard), gain(1), shift(1)
+    )
+
+    with jax.named_scope("feed_core"):
+        core_shard = swap(after(shard, cross_kept[0]), "dp", 1)
+    kept, rest = feed_slots(
+        ids, (0,), after(second, core_shard), all_pieces(feed_own), None, None, units, extra
+    )
+    piece = after(feed_near[1], rest[0])
+    with jax.named_scope("feed_far"):
+        far_piece = swap(piece, "dp", 2)
+    with jax.named_scope("feed_core"):
+        core_piece = swap(piece, "dp", 1)
+    feed_pieces = all_pieces(feed_own, shard, core_shard)
+    kept, rest = feed_slots(
+        ids, (1, 2), after(second, piece), feed_pieces, rest + kept, None, units, extra
+    )
+    with jax.named_scope("feed_core"):
+        core_far_piece = swap(after(far_piece, rest[0]), "dp", 1)
+    feed_pieces += all_pieces(piece, core_piece, far_piece, core_far_piece)
+    norm = (adapter_shift.reshape(1, -1), gain(2), shift(2), grad)
+    kept, rest = feed_slots(
+        ids, (3,), after(second, core_piece), feed_pieces, rest + kept, norm, units, extra
+    )
+    outcome, branch_low, sums_three = rest
+    slopes, adapter_slopes, adapted_low = kept
+    result = turn_over(outcome.reshape(4, share, width))
+    a_low, grads = adapter_back(
+        ids, branch_low, second, adapter_slopes, adapted_low, feed_pieces, units, extra
+    )
+    with jax.named_scope("adapter"):
+        grads_there = [
+            cross_swap(grads[1], 1, 2),
+            cross_swap(grads[2], 2, 1),
+            swap(grads[3], "tensor", 3),
+        ]
+    cross_low, sums_two = feed_back(
+        ids,
+        after(branch_low, a_low),
+        slopes,
+        a_low,
+        feed_pieces,
+        normed_two,
+        scale_two,
+        gain(1),
+        units,
+        extra,
+    )
+    adapter_sum = grads[0].astype(F32)
+    for part in grads_there:
+        adapter_sum = adapter_sum + part.astype(F32)
+    adapter_sum = adapter_sum.astype(BF16)
+    with jax.named_scope("adapter"):
+        adapter_there = swap(adapter_sum, "dp", 1)
+    encoded_back, self_low, sums_one = attention_back(
+        after(cross_low, adapter_sum), cross_kept, cross_pieces, (normed_one, scale_one, gain(0))
+    )
+    adapter_sum = add_low(adapter_sum, after(adapter_there, self_low))
+    encoded_result = turn_over(encoded_back.reshape(4, share, width))
+    small = jnp.concatenate(
+        [
+            sums_one[0:1],
+            sums_two[0:1],
+            sums_three[0:1],
+            sums_one[1:2],
+            sums_two[1:2],
+            sums_three[1:2],
+            sums_three[2:3],
+            jnp.zeros((1, width), F32),
+        ],
+        axis=0,
+    )
+    with jax.named_scope("small"):
+        small_there = [swap(small, "tensor", k) for k in (1, 2, 3)]
+    with jax.named_scope("adapter"):
+        adapter_there = swap(adapter_sum, "dp", 2)
+    input_back, result = attention_back(
+        after(self_low, small, adapter_sum), self_kept, self_pieces, None, result
+    )
+    input_back, small_there, adapter_there, encoded_result = lax.optimization_barrier(
+        (input_back, small_there, adapter_there, encoded_result)
+    )
+    input_result = turn_over(input_back.reshape(4, share, width))
+    for part in small_there:
+        small = small + part
+    adapter_sum = add_low(adapter_sum, adapter_there)
+    bit = 4
+    while bit < lax.axis_size("dp"):
+        with jax.named_scope("adapter"):
+            adapter_sum = add_low(adapter_sum, swap(adapter_sum, "dp", bit))
+        bit *= 2
+    bit = 1
+    while bit < lax.axis_size("dp"):
+        with jax.named_scope("small"):
+            small = small + swap(small, "dp", bit)
+        bit *= 2
+    encoded_result = copied(encoded_result)
+    adapter_sum = adapter_sum.astype(F32)
+    size = 4 * extra
+    return (
+        result,
+        input_result,
+        encoded_result,
+        adapter_sum[:size].T,
+        adapter_sum[size : 2 * size],
+        jnp.sum(adapter_sum[2 * size :, :size], axis=0),
+        small[6],
+        small[0:3],
+        small[3:6],
+    )
 
 
 def gelu_tanh(values):
@@ -346,8 +1402,15 @@
         P(),
         P("dp", "tensor", None),
     )
+    suits = mesh.shape["tensor"] == 4 and mesh.shape["dp"] in (4, 8, 16, 32)
+
+    def layer(*arrays):
+        if suits and arrays[0].shape[:2] == (4, ROWS) and arrays[1].shape[:2] == (4, ROWS):
+            return whole_sequences(*arrays)
+        return local(*arrays)
+
     return jax.shard_map(
-        local,
+        layer,
         mesh=mesh,
         in_specs=placed,
         out_specs=(

time: 2040 us -> 481 us (0.24)
  waiting for transfers between devices: 955 us -> 71.4 us
  matrix products: 628 us -> 0 us
  Pallas kernels: 0 us -> 314 us
  other arithmetic: 247 us -> 6.08 us
  local copies, waits for them, and re-layouts: 163 us -> 19 us
  starting transfers between devices: 0.62 us -> 59.8 us
  blocking collectives: 28.5 us -> 0 us
    dot_general x49 -> x0, matrix products: 628 us -> none  [the longest x11 124 us: multiply_by_transpose(): lax.dot_general(left, right, (((1,), (1,)), ((), ())), preferred_element_...]
    all_gather x6 -> x0, waiting for transfers between devices: 425 us -> none  [the longest x1 90.2 us: local(): lax.all_gather(inputs, 'tensor', axis=1, tiled=True)]
    reduce_scatter x6 -> x0, waiting for transfers between devices: 401 us -> none  [the longest x1 87.2 us: local(): lax.psum_scatter(cross_partial.astype(jnp.bfloat16), 'tensor', scatter_di...]
    pallas_call x0 -> x18, Pallas kernels: none -> 314 us  [the longest x2 93.2 us: attention_back(): pl.pallas_call(functools.partial(attention_back_kernel, causal, homes), g...]
    convert_element_type x12 -> x4, other arithmetic: 146 us -> 4.3 us  [the longest x2 2.51 us: add_low(): return (left.astype(F32) + right.astype(F32)).astype(BF16)]
    psum x2 -> x0, waiting for transfers between devices: 127 us -> none  [the longest x1 127 us: local(): lax.psum(self_partial.astype(jnp.bfloat16), 'tensor').astype(jnp.float32)]
    reduce_sum x13 -> x1, other arithmetic: 96.8 us -> 0.53 us  [whole_sequences(): jnp.sum(adapter_sum[2 * size:, :size], axis=0)]
    reshape x12 -> x0, local copies, waits for them, and re-layouts: 78 us -> none  [the longest x10 71.2 us: split_heads(): return values.astype(jnp.bfloat16).reshape(sequences, count, heads, HEAD)]
  transfers between devices with their start and end apart: 15 -> 38, of which waited for: 11 -> 12; matrix products, arithmetic and copies ran while one was open for 28% -> 3% of each run, Pallas kernels for 0% -> 60%
where the time goes in v2:
time: 481 us; the launch traced here: 472 us
  Pallas kernels  314 us (65%)
  waiting for transfers between devices  71.4 us (15%)
  starting transfers between devices  59.8 us (12%)
  local copies, waits for them, and re-layouts  19 us (4%)
  other arithmetic  6.08 us (1%)
    pallas_call x2, Pallas kernels, attention_back(): pl.pallas_call(functools.partial(attention_back_kernel, causal, homes), g...  93.2 us
    pallas_call x5, Pallas kernels, attend_slots(): pl.pallas_call(functools.partial(attend_kernel, causal, count, first, hom...  86.6 us
    pallas_call x3, Pallas kernels, feed_slots(): pl.pallas_call(functools.partial(feed_kernel, slots, first, last, units,...  61.6 us
    ppermute x27, waiting for transfers between devices, swap(): return lax.ppermute(values, name, [(i, i ^ bit) for i in range(size)])  56.3 us
    pallas_call x1, Pallas kernels, feed_back(): pl.pallas_call(functools.partial(feed_back_kernel, units, extra, homes),...  29.6 us
    all_to_all x6, starting transfers between devices, turn_over(): return lax.all_to_all(values, 'tensor', 0, 0, tiled=True)  25.8 us
    ppermute x27, starting transfers between devices, swap(): return lax.ppermute(values, name, [(i, i ^ bit) for i in range(size)])  25.3 us
    pallas_call x2, Pallas kernels, out_norm(): pl.pallas_call(functools.partial(out_norm_kernel, homes), grid=(span // b...  16.7 us
  transfers between devices with their start and end apart: 38, of which 12 were waited for; matrix products, arithmetic and copies ran while one was open for 3% of the time, Pallas kernels for 60%

profile of v2, /device:TPU:0, one launch (start us, length us, event | category | flops | bytes accessed | tf_op | source)
XLA Modules:
  0.0 471.5 jit_solution(11537364084940309643)
XLA Ops:
  0.7 5.2 %all-to-all-start = ((bf16[4,256,1024]{2,1,0:T(8,128)(2,1)}), bf16[4,256,1024]{2,1,0:T(8,128)(2,1)S(1)}, u32[]{:S(2)}, u32[]{:S(2)}) async-start(bf16[4,256,1024]{2,1,0:T(8,128)(2,1)} %param.20), calls=%async_computation | async-start | bytes 4194304 | tf_op jit(solution)/shard_map/all_to_all | solution.py:834
  7.6 3.9 pack_self.1
  15.0 3.5 pack_cross.1
  20.0 5.8 %pack_feed.1 = (bf16[4,592,1024]{2,1,0:T(8,128)(2,1)}, bf16[1,592,1024]{2,1,0:T(8,128)(2,1)}) custom-call(s32[3]{0:T(128)} %pad_add_fusion.ids_ref, bf16[1024,1024]{1,0:T(8,128)(2,1)} %up_ref.1, bf16[1024,1024]{1,0:T(8,128)(2,1)} %down_ref.1, bf16[1024,128]{1,0:T(8,128)(2,1)} %ain_ref.1, bf16[128,1024]{1,0:T(8,128)(2,1)} %aout_ref.1, f32[1,128]{1,0:T(1,128)} %bitcast.22), custom_call_target="tpu_custom_call" | custom-call | bytes 8388608 | tf_op jit(solution)/shard_map/pack_feed/pallas_call | solution.py:116
  25.8 7.5 %all-to-all-done = bf16[4,256,1024]{2,1,0:T(8,128)(2,1)S(1)} async-done(((bf16[4,256,1024]{2,1,0:T(8,128)(2,1)}), bf16[4,256,1024]{2,1,0:T(8,128)(2,1)S(1)}, u32[]{:S(2)}, u32[]{:S(2)}) %all-to-all-start) | async-done | bytes 2097184 | tf_op jit(solution)/shard_map/all_to_all | solution.py:834
  34.5 10.6 %self_attend.3 = (bf16[16,1024,1024]{2,1,0:T(8,128)(2,1)}, bf16[4,1024,1024]{2,1,0:T(8,128)(2,1)}, f32[16,1,1024]{2,1,0:T(1,128)}, bf16[1024,1024]{1,0:T(8,128)(2,1)}) custom-call(s32[3]{0:T(128)} %pad_add_fusion.ids_ref, bf16[1024,1024]{1,0:T(8,128)(2,1)} %bitcast.13, bf16[4,4,64,1024]{3,2,1,0:T(8,128)(2,1)} %get-tuple-element.110.refs_1_.refs_4_), custom_call_target="tpu_custom_call" | custom-call | flops 10000000000 | bytes 12582912 | tf_op jit(solution)/shard_map/self_attend/pallas_call | solution.py:241
  45.1 9.1 %collective-permute-done.2.refs_1_.refs_9_ = bf16[1,4,64,1024]{3,2,1,0:T(8,128)(2,1)S(1)} collective-permute-done((bf16[1,4,64,1024]{3,2,1,0:T(8,128)(2,1)}, bf16[1,4,64,1024]{3,2,1,0:T(8,128)(2,1)S(1)}, u32[]{:S(2)}, u32[]{:S(2)}) %collective-permute-start.2) | collective-permute-done | bytes 524320 | tf_op jit(solution)/shard_map/self_near/ppermute | solution.py:821
  55.9 17.1 %collective-permute-done.4.refs_2_.refs_6_ = bf16[2,4,64,1024]{3,2,1,0:T(8,128)(2,1)S(1)} collective-permute-done((bf16[2,4,64,1024]{3,2,1,0:T(8,128)(2,1)}, bf16[2,4,64,1024]{3,2,1,0:T(8,128)(2,1)S(1)}, u32[]{:S(2)}, u32[]{:S(2)}) %collective-permute-start.4) | collective-permute-done | bytes 1048608 | tf_op jit(solution)/shard_map/self_far/ppermute | solution.py:821
  73.0 6.8 %collective-permute-start = (bf16[1,4,64,1024]{3,2,1,0:T(8,128)(2,1)}, bf16[1,4,64,1024]{3,2,1,0:T(8,128)(2,1)}, u32[]{:S(2)}, u32[]{:S(2)}) collective-permute-start(bf16[1,4,64,1024]{3,2,1,0:T(8,128)(2,1)} %get-tuple-element.105), channel_id=1, source_target_pairs={{0,3},{1,2},{2,1},{3,0},{4,7},{5,6},{6,5},{7,4},{8,11},{9,10},{10,... | collective-permute-start | bytes 1572872 | tf_op jit(solution)/shard_map/cross_near/ppermute | solution.py:821
  83.5 17.0 %self_attend.4 = (bf16[16,1024,1024]{2,1,0:T(8,128)(2,1)}, bf16[4,1024,1024]{2,1,0:T(8,128)(2,1)}, f32[16,1,1024]{2,1,0:T(1,128)}, bf16[1024,1024]{1,0:T(8,128)(2,1)}) custom-call(s32[3]{0:T(128)} %pad_add_fusion.ids_ref, bf16[1024,1024]{1,0:T(8,128)(2,1)} %bitcast.14, ...), custom_call_target="tpu_custom_call", output_to_operand_aliasing={{0}: (6, {}), {1}: (7, {}), {2}: (8, {}), {3}: (9, {})} | custom-call | flops 20000000000 | bytes 25165824 | tf_op jit(solution)/shard_map/self_attend/pallas_call | solution.py:241
  101.8 4.7 all-to-all-start.1
  109.7 10.6 %self_attend.5 = (bf16[16,1024,1024]{2,1,0:T(8,128)(2,1)}, bf16[4,1024,1024]{2,1,0:T(8,128)(2,1)}, f32[16,1,1024]{2,1,0:T(1,128)}, bf16[1024,1024]{1,0:T(8,128)(2,1)}) custom-call(s32[3]{0:T(128)} %pad_add_fusion.ids_ref, bf16[1024,1024]{1,0:T(8,128)(2,1)} %bitcast.15, ...), custom_call_target="tpu_custom_call", output_to_operand_aliasing={{0}: (6, {}), {1}: (7, {}), {2}: (8, {}), {3}: (9, {})} | custom-call | flops 10000000000 | bytes 12582912 | tf_op jit(solution)/shard_map/self_attend/pallas_call | solution.py:241
  120.3 8.4 %out_norm.2 = (bf16[1024,1024]{1,0:T(8,128)(2,1)}, bf16[1024,1024]{1,0:T(8,128)(2,1)}, f32[1024,1]{1,0:T(8,128)}) custom-call(bf16[1024,1024]{1,0:T(8,128)(2,1)} %get-tuple-element.127.refs_0_, bf16[1024,1024]{1,0:T(8,128)(2,1)} %bitcast.16, f32[1,1024]{1,0:T(1,128)} %get-tuple-element.221.refs_2_.refs_6_, f32[1,1024]{1,0:T(1,128)} %get-tuple-element.215.refs_3_, ...), custom_call_target="tpu_custom_call" | custom-call | flops 2147483648 | bytes 10485760 | tf_op jit(solution)/shard_map/out_norm/pallas_call | solution.py:306
  132.7 24.0 %cross_attend.2 = (bf16[16,1024,1024]{2,1,0:T(8,128)(2,1)}, bf16[4,1024,1024]{2,1,0:T(8,128)(2,1)}, f32[16,1,1024]{2,1,0:T(1,128)}, bf16[1024,1024]{1,0:T(8,128)(2,1)}) custom-call(s32[3]{0:T(128)} %pad_add_fusion.ids_ref, bf16[1024,1024]{1,0:T(8,128)(2,1)} %get-tuple-element.142.refs_0_.refs_1_, bf16[1024,1024]{1,0:T(8,128)(2,1)} %bitcast.4.refs_1_, ...), custom_call_target="tpu_custom_call" | custom-call | flops 20000000000 | bytes 25165824 | tf_op jit(solution)/shard_map/cross_attend/pallas_call | solution.py:241
  156.8 24.5 %cross_attend.3 = (bf16[16,1024,1024]{2,1,0:T(8,128)(2,1)}, bf16[4,1024,1024]{2,1,0:T(8,128)(2,1)}, f32[16,1,1024]{2,1,0:T(1,128)}, bf16[1024,1024]{1,0:T(8,128)(2,1)}) custom-call(s32[3]{0:T(128)} %pad_add_fusion.ids_ref, ...), custom_call_target="tpu_custom_call", output_to_operand_aliasing={{0}: (8, {}), {1}: (9, {}), {2}: (10, {}), {3}: (11, {})} | custom-call | flops 20000000000 | bytes 25165824 | tf_op jit(solution)/shard_map/cross_attend/pallas_call | solution.py:241
  185.8 8.3 %out_norm.3 = (bf16[1024,1024]{1,0:T(8,128)(2,1)}, bf16[1024,1024]{1,0:T(8,128)(2,1)}, f32[1024,1]{1,0:T(8,128)}) custom-call(bf16[1024,1024]{1,0:T(8,128)(2,1)} %get-tuple-element.137.refs_0_, bf16[1024,1024]{1,0:T(8,128)(2,1)} %get-tuple-element.142.refs_0_.refs_1_, f32[1,1024]{1,0:T(1,128)} %get-tuple-element.220.refs_2_.refs_5_, ...), custom_call_target="tpu_custom_call" | custom-call | flops 2147483648 | bytes 10485760 | tf_op jit(solution)/shard_map/out_norm/pallas_call | solution.py:306
  194.1 14.5 %feed.3 = (bf16[1024,4096]{1,0:T(8,128)(2,1)}, bf16[1024,512]{1,0:T(8,128)(2,1)}, bf16[1024,512]{1,0:T(8,128)(2,1)}, f32[1024,1024]{1,0:T(8,128)}) custom-call(s32[3]{0:T(128)} %pad_add_fusion.ids_ref, bf16[1024,1024]{1,0:T(8,128)(2,1)} %get-tuple-element.150.refs_0_.refs_1_, bf16[4,592,1024]{2,1,0:T(8,128)(2,1)} %get-tuple-element.139.refs_1_.refs_4_.refs_6_), custom_call_target="tpu_custom_call" | custom-call | flops 6000000000 | bytes 14680064 | tf_op jit(solution)/shard_map/feed/pallas_call | solution.py:455
  208.7 5.6 %collective-permute-done.15.refs_1_.refs_7_.refs_9_ = bf16[1,592,1024]{2,1,0:T(8,128)(2,1)S(1)} collective-permute-done((bf16[1,592,1024]{2,1,0:T(8,128)(2,1)S(1)}, bf16[1,592,1024]{2,1,0:T(8,128)(2,1)S(1)}, u32[]{:S(2)}, u32[]{:S(2)}) %collective-permute-start.15) | collective-permute-done | bytes 1212448 | tf_op jit(solution)/shard_map/feed_near/ppermute | solution.py:821
  214.5 3.6 all-to-all-start.2
  218.3 25.8 %feed.4 = (bf16[1024,4096]{1,0:T(8,128)(2,1)}, bf16[1024,512]{1,0:T(8,128)(2,1)}, bf16[1024,512]{1,0:T(8,128)(2,1)}, f32[1024,1024]{1,0:T(8,128)}) custom-call(s32[3]{0:T(128)} %pad_add_fusion.ids_ref, bf16[1024,1024]{1,0:T(8,128)(2,1)} %get-tuple-element.150.refs_0_.refs_1_, ...), custom_call_target="tpu_custom_call", output_to_operand_aliasing={{0}: (5, {}), {1}: (6, {}), {2}: (7, {})} | custom-call | flops 12000000000 | bytes 29360128 | tf_op jit(solution)/shard_map/feed/pallas_call | solution.py:455
  247.4 21.3 %feed.5 = (bf16[1024,4096]{1,0:T(8,128)(2,1)}, bf16[1024,512]{1,0:T(8,128)(2,1)}, bf16[1024,512]{1,0:T(8,128)(2,1)}, bf16[1024,1024]{1,0:T(8,128)(2,1)}, bf16[1024,1024]{1,0:T(8,128)(2,1)}, /*index=5*/f32[8,1024]{1,0:T(8,128)}) custom-call(s32[3]{0:T(128)} %pad_add_fusion.ids_ref, ...), custom_call_target="tpu_custom_call", output_to_operand_aliasing={{0}: (11, {}), {1}: (12, {}), {2}: (13, {})} | custom-call | flops 6000000000 | bytes 14680064 | tf_op jit(solution)/shard_map/feed/pallas_call | solution.py:455
  270.2 9.0 %adapter_back.1 = (bf16[1024,512]{1,0:T(8,128)(2,1)}, bf16[272,1024]{1,0:T(8,128)(2,1)}, bf16[272,1024]{1,0:T(8,128)(2,1)}, bf16[272,1024]{1,0:T(8,128)(2,1)}, bf16[272,1024]{1,0:T(8,128)(2,1)}) custom-call(s32[3]{0:T(128)} %pad_add_fusion.ids_ref, bf16[1024,1024]{1,0:T(8,128)(2,1)} %get-tuple-element.164.refs_0_, ...), custom_call_target="tpu_custom_call" | custom-call | flops 3221225472 | bytes 12582912 | tf_op jit(solution)/shard_map/adapter_back/pallas_call | solution.py:521
  282.8 4.3 all-to-all-start.3
  287.1 29.6 %feed_back.1 = (bf16[1024,1024]{1,0:T(8,128)(2,1)}, f32[8,1024]{1,0:T(8,128)}) custom-call(s32[3]{0:T(128)} %pad_add_fusion.ids_ref, bf16[1024,1024]{1,0:T(8,128)(2,1)} %get-tuple-element.164.refs_0_, bf16[1024,4096]{1,0:T(8,128)(2,1)} %get-tuple-element.165.refs_1_, bf16[1024,512]{1,0:T(8,128)(2,1)} %get-tuple-element.163.refs_2_, ...), custom_call_target="tpu_custom_call" | custom-call | flops 20000000000 | bytes 41943040 | tf_op jit(solution)/shard_map/feed_back/pallas_call | solution.py:612
  322.7 53.2 %cross_back.1 = (bf16[1024,1024]{1,0:T(8,128)(2,1)}, bf16[1024,1024]{1,0:T(8,128)(2,1)}, f32[8,1024]{1,0:T(8,128)}) custom-call(bf16[1024,1024]{1,0:T(8,128)(2,1)} %get-tuple-element.173.refs_0_, bf16[16,1024,1024]{2,1,0:T(8,128)(2,1)} %get-tuple-element.140.refs_1_, bf16[4,1024,1024]{2,1,0:T(8,128)(2,1)} %get-tuple-element.174.refs_2_, ...), custom_call_target="tpu_custom_call" | custom-call | flops 40000000000 | bytes 62914560 | tf_op jit(solution)/shard_map/cross_back/pallas_call | solution.py:781
  385.6 3.6 all-to-all-start.4
  389.2 40.0 %self_back.1 = (bf16[1024,1024]{1,0:T(8,128)(2,1)}, bf16[4,256,1024]{2,1,0:T(8,128)(2,1)}) custom-call(bf16[1024,1024]{1,0:T(8,128)(2,1)} %get-tuple-element.183.refs_0_, bf16[16,1024,1024]{2,1,0:T(8,128)(2,1)} %get-tuple-element.184.refs_1_, bf16[4,1024,1024]{2,1,0:T(8,128)(2,1)} %get-tuple-element.185.refs_2_, f32[16,1,1024]{2,1,0:T(1,128)} %get-tuple-element.186.refs_3_, ...), custom_call_target="tpu_custom_call" | custom-call | flops 40000000000 | bytes 62914560 | tf_op jit(solution)/shard_map/self_back/pallas_call | solution.py:781
  430.5 4.5 all-to-all-start.5
  440.6 10.5 %collective-permute-done.30 = f32[8,1024]{1,0:T(8,128)S(1)} collective-permute-done((f32[8,1024]{1,0:T(8,128)S(1)}, f32[8,1024]{1,0:T(8,128)S(1)}, u32[]{:S(2)}, u32[]{:S(2)}) %collective-permute-start.30) | collective-permute-done | bytes 32800 | tf_op jit(solution)/shard_map/small/ppermute | solution.py:821
  452.2 3.8 copied.1
  456.0 8.3 %collective-permute-done.31 = f32[8,1024]{1,0:T(8,128)S(1)} collective-permute-done((f32[8,1024]{1,0:T(8,128)S(1)}, f32[8,1024]{1,0:T(8,128)S(1)}, u32[]{:S(2)}, u32[]{:S(2)}) %collective-permute-start.31) | collective-permute-done | bytes 32800 | tf_op jit(solution)/shard_map/small/ppermute | solution.py:821
  468.1 3.1 copy.67
  (129 shorter events, 62.7 us)
Async XLA Ops:
  0.7 32.6 %all-to-all-start = ((bf16[4,256,1024]{2,1,0:T(8,128)(2,1)}), bf16[4,256,1024]{2,1,0:T(8,128)(2,1)S(1)}, u32[]{:S(2)}, u32[]{:S(2)}) async-start(bf16[4,256,1024]{2,1,0:T(8,128)(2,1)} %param.20), calls=%async_computation | async-start | bytes 4194304 | tf_op jit(solution)/shard_map/all_to_all | solution.py:834
  11.5 42.7 %collective-permute-start.1 = (bf16[2,4,64,1024]{3,2,1,0:T(8,128)(2,1)}, bf16[2,4,64,1024]{3,2,1,0:T(8,128)(2,1)}, u32[]{:S(2)}, u32[]{:S(2)}) collective-permute-start(bf16[2,4,64,1024]{3,2,1,0:T(8,128)(2,1)} %get-tuple-element.103), channel_id=1, source_target_pairs={{0,1},{1,0},{2,3},{3,2},{4,6},{5,7},{6,4},{7,5},{8,9},{9,8},{10,11... | collective-permute-start | bytes 3145736 | tf_op jit(solution)/shard_map/self_near/ppermute | solution.py:830
  13.5 40.6 %collective-permute-start.2 = (bf16[1,4,64,1024]{3,2,1,0:T(8,128)(2,1)}, bf16[1,4,64,1024]{3,2,1,0:T(8,128)(2,1)S(1)}, u32[]{:S(2)}, u32[]{:S(2)}) collective-permute-start(bf16[1,4,64,1024]{3,2,1,0:T(8,128)(2,1)} %get-tuple-element.109), channel_id=1, source_target_pairs={{0,3},{1,2},{2,1},{3,0},{4,7},{5,6},{6,5},{7,4},{8,11},{9,10},{10,... | collective-permute-start | bytes 1572872 | tf_op jit(solution)/shard_map/self_near/ppermute | solution.py:821
  18.5 63.0 %collective-permute-start.3 = (bf16[4,4,64,1024]{3,2,1,0:T(8,128)(2,1)}, bf16[4,4,64,1024]{3,2,1,0:T(8,128)(2,1)}, u32[]{:S(2)}, u32[]{:S(2)}) collective-permute-start(bf16[4,4,64,1024]{3,2,1,0:T(8,128)(2,1)} %get-tuple-element.113.refs_2_.refs_4_.refs_7_), channel_id=1, source_target_pairs={{0,1},{1,0},{2,3},{3,2},{4,6},{5,7},{6,4},{7,5},{8,9},{9,8},{10,11... | collective-permute-start | bytes 6291464 | tf_op jit(solution)/shard_map/cross_near/ppermute | solution.py:830
  54.2 18.8 %collective-permute-start.4 = (bf16[2,4,64,1024]{3,2,1,0:T(8,128)(2,1)}, bf16[2,4,64,1024]{3,2,1,0:T(8,128)(2,1)S(1)}, u32[]{:S(2)}, u32[]{:S(2)}) collective-permute-start(bf16[2,4,64,1024]{3,2,1,0:T(8,128)(2,1)} %collective-permute-done.1.refs_1_.refs_5_), channel_id=1, source_target_pairs={{0,8},{4,12},{8,0},{12,4},{16,24},{20,28},{24,16},{28,20},{1,9},{5... | collective-permute-start | bytes 3145736 | tf_op jit(solution)/shard_map/self_far/ppermute | solution.py:821
  55.9 25.6 %collective-permute-start.5 = (bf16[2,4,64,1024]{3,2,1,0:T(8,128)(2,1)}, bf16[2,4,64,1024]{3,2,1,0:T(8,128)(2,1)S(1)}, u32[]{:S(2)}, u32[]{:S(2)}) collective-permute-start(bf16[2,4,64,1024]{3,2,1,0:T(8,128)(2,1)} %collective-permute-done.1.refs_1_.refs_5_), channel_id=1, source_target_pairs={{0,4},{4,0},{8,12},{12,8},{16,20},{20,16},{24,28},{28,24},{1,5},{5... | collective-permute-start | bytes 3145736 | tf_op jit(solution)/shard_map/self_core/ppermute | solution.py:821
  73.0 33.5 %collective-permute-start = (bf16[1,4,64,1024]{3,2,1,0:T(8,128)(2,1)}, bf16[1,4,64,1024]{3,2,1,0:T(8,128)(2,1)}, u32[]{:S(2)}, u32[]{:S(2)}) collective-permute-start(bf16[1,4,64,1024]{3,2,1,0:T(8,128)(2,1)} %get-tuple-element.105), channel_id=1, source_target_pairs={{0,3},{1,2},{2,1},{3,0},{4,7},{5,6},{6,5},{7,4},{8,11},{9,10},{10,... | collective-permute-start | bytes 1572872 | tf_op jit(solution)/shard_map/cross_near/ppermute | solution.py:821
  79.8 20.7 %collective-permute-start.8 = (bf16[1,4,64,1024]{3,2,1,0:T(8,128)(2,1)S(1)}, bf16[1,4,64,1024]{3,2,1,0:T(8,128)(2,1)S(1)}, u32[]{:S(2)}, u32[]{:S(2)}) collective-permute-start(bf16[1,4,64,1024]{3,2,1,0:T(8,128)(2,1)S(1)} %collective-permute-done.2.refs_1_.refs_9_), channel_id=1, source_target_pairs={{0,8},{4,12},{8,0},{12,4},{16,24},{20,28},{24,16},{28,20},{1,9},{5... | collective-permute-start | bytes 1572872 | tf_op jit(solution)/shard_map/self_far/ppermute | solution.py:821
  81.5 25.5 %collective-permute-start.7 = (bf16[1,4,64,1024]{3,2,1,0:T(8,128)(2,1)S(1)}, bf16[1,4,64,1024]{3,2,1,0:T(8,128)(2,1)S(1)}, u32[]{:S(2)}, u32[]{:S(2)}) collective-permute-start(bf16[1,4,64,1024]{3,2,1,0:T(8,128)(2,1)S(1)} %collective-permute-done.2.refs_1_.refs_9_), channel_id=1, source_target_pairs={{0,4},{4,0},{8,12},{12,8},{16,20},{20,16},{24,28},{28,24},{1,5},{5... | collective-permute-start | bytes 1572872 | tf_op jit(solution)/shard_map/self_core/ppermute | solution.py:821
  101.1 29.7 %collective-permute-start.10 = (bf16[4,4,64,1024]{3,2,1,0:T(8,128)(2,1)}, bf16[4,4,64,1024]{3,2,1,0:T(8,128)(2,1)}, u32[]{:S(2)}, u32[]{:S(2)}) collective-permute-start(bf16[4,4,64,1024]{3,2,1,0:T(8,128)(2,1)} %collective-permute-done.3.refs_3_.refs_5_.refs_8_), channel_id=1, source_target_pairs={{0,4},{4,0},{8,12},{12,8},{16,20},{20,16},{24,28},{28,24},{1,5},{5... | collective-permute-start | bytes 6291464 | tf_op jit(solution)/shard_map/cross_core/ppermute | solution.py:821
  101.8 30.9 %all-to-all-start.1 = ((bf16[4,256,1024]{2,1,0:T(8,128)(2,1)}), bf16[4,256,1024]{2,1,0:T(8,128)(2,1)}, u32[]{:S(2)}, u32[]{:S(2)}) async-start(bf16[4,256,1024]{2,1,0:T(8,128)(2,1)} %param.21), calls=%async_computation.1 | async-start | bytes 4194304 | tf_op jit(solution)/shard_map/all_to_all | solution.py:834
  106.5 22.3 %collective-permute-start.12 = (bf16[1,4,64,1024]{3,2,1,0:T(8,128)(2,1)}, bf16[1,4,64,1024]{3,2,1,0:T(8,128)(2,1)S(1)}, u32[]{:S(2)}, u32[]{:S(2)}) collective-permute-start(bf16[1,4,64,1024]{3,2,1,0:T(8,128)(2,1)} %collective-permute-done.refs_3_.refs_7_.refs_10_), channel_id=1, source_target_pairs={{0,8},{4,12},{8,0},{12,4},{16,24},{20,28},{24,16},{28,20},{1,9},{5... | collective-permute-start | bytes 1572872 | tf_op jit(solution)/shard_map/cross_far/ppermute | solution.py:821
  106.8 22.1 %collective-permute-start.11 = (bf16[1,4,64,1024]{3,2,1,0:T(8,128)(2,1)}, bf16[1,4,64,1024]{3,2,1,0:T(8,128)(2,1)S(1)}, u32[]{:S(2)}, u32[]{:S(2)}) collective-permute-start(bf16[1,4,64,1024]{3,2,1,0:T(8,128)(2,1)} %collective-permute-done.refs_3_.refs_7_.refs_10_), channel_id=1, source_target_pairs={{0,4},{4,0},{8,12},{12,8},{16,20},{20,16},{24,28},{28,24},{1,5},{5... | collective-permute-start | bytes 1572872 | tf_op jit(solution)/shard_map/cross_core/ppermute | solution.py:821
  107.1 77.2 %collective-permute-start.14 = (bf16[4,592,1024]{2,1,0:T(8,128)(2,1)}, bf16[4,592,1024]{2,1,0:T(8,128)(2,1)}, u32[]{:S(2)}, u32[]{:S(2)}) collective-permute-start(bf16[4,592,1024]{2,1,0:T(8,128)(2,1)} %get-tuple-element.139.refs_1_.refs_4_.refs_6_), channel_id=1, source_target_pairs={{0,1},{1,0},{2,3},{3,2},{4,6},{5,7},{6,4},{7,5},{8,9},{9,8},{10,11... | collective-permute-start | bytes 14549000 | tf_op jit(solution)/shard_map/feed_near/ppermute | solution.py:830
  184.3 29.9 %collective-permute-start.15 = (bf16[1,592,1024]{2,1,0:T(8,128)(2,1)S(1)}, bf16[1,592,1024]{2,1,0:T(8,128)(2,1)S(1)}, u32[]{:S(2)}, u32[]{:S(2)}) collective-permute-start(bf16[1,592,1024]{2,1,0:T(8,128)(2,1)S(1)} %copy-done.20), channel_id=1, source_target_pairs={{0,3},{1,2},{2,1},{3,0},{4,7},{5,6},{6,5},{7,4},{8,11},{9,10},{10,... | collective-permute-start | bytes 3637256 | tf_op jit(solution)/shard_map/feed_near/ppermute | solution.py:821
  214.2 29.8 %collective-permute-start.18 = (bf16[1,592,1024]{2,1,0:T(8,128)(2,1)S(1)}, bf16[1,592,1024]{2,1,0:T(8,128)(2,1)}, u32[]{:S(2)}, u32[]{:S(2)}) collective-permute-start(bf16[1,592,1024]{2,1,0:T(8,128)(2,1)S(1)} %collective-permute-done.15.refs_1_.refs_7_.refs_9_), channel_id=1, source_target_pairs={{0,8},{4,12},{8,0},{12,4},{16,24},{20,28},{24,16},{28,20},{1,9},{5... | collective-permute-start | bytes 3637256 | tf_op jit(solution)/shard_map/feed_far/ppermute | solution.py:821
  214.5 30.0 %all-to-all-start.2 = ((bf16[4,256,1024]{2,1,0:T(8,128)(2,1)}), bf16[4,256,1024]{2,1,0:T(8,128)(2,1)S(1)}, u32[]{:S(2)}, u32[]{:S(2)}) async-start(bf16[4,256,1024]{2,1,0:T(8,128)(2,1)} %param.39), calls=%async_computation.2 | async-start | bytes 4194304 | tf_op jit(solution)/shard_map/all_to_all | solution.py:834
  218.2 26.3 %collective-permute-start.17 = (bf16[1,592,1024]{2,1,0:T(8,128)(2,1)S(1)}, bf16[1,592,1024]{2,1,0:T(8,128)(2,1)}, u32[]{:S(2)}, u32[]{:S(2)}) collective-permute-start(bf16[1,592,1024]{2,1,0:T(8,128)(2,1)S(1)} %collective-permute-done.15.refs_1_.refs_7_.refs_9_), channel_id=1, source_target_pairs={{0,4},{4,0},{8,12},{12,8},{16,20},{20,16},{24,28},{28,24},{1,5},{5... | collective-permute-start | bytes 3637256 | tf_op jit(solution)/shard_map/feed_core/ppermute | solution.py:821
  279.2 38.3 %collective-permute-start.20 = (bf16[272,1024]{1,0:T(8,128)(2,1)}, bf16[272,1024]{1,0:T(8,128)(2,1)S(1)}, u32[]{:S(2)}, u32[]{:S(2)}) collective-permute-start(bf16[272,1024]{1,0:T(8,128)(2,1)} %get-tuple-element.170), channel_id=1, source_target_pairs={{0,1},{1,0},{2,3},{3,2},{4,6},{5,7},{6,4},{7,5},{8,9},{9,8},{10,11... | collective-permute-start | bytes 1671176 | tf_op jit(solution)/shard_map/adapter/ppermute | solution.py:830
  281.2 38.9 %collective-permute-start.21 = (bf16[272,1024]{1,0:T(8,128)(2,1)}, bf16[272,1024]{1,0:T(8,128)(2,1)S(1)}, u32[]{:S(2)}, u32[]{:S(2)}) collective-permute-start(bf16[272,1024]{1,0:T(8,128)(2,1)} %get-tuple-element.171), channel_id=1, source_target_pairs={{0,2},{1,3},{2,0},{3,1},{4,5},{5,4},{6,7},{7,6},{8,10},{9,11},{10,... | collective-permute-start | bytes 1671176 | tf_op jit(solution)/shard_map/adapter/ppermute | solution.py:830
  282.7 37.5 %collective-permute-start.22 = (bf16[272,1024]{1,0:T(8,128)(2,1)}, bf16[272,1024]{1,0:T(8,128)(2,1)}, u32[]{:S(2)}, u32[]{:S(2)}) collective-permute-start(bf16[272,1024]{1,0:T(8,128)(2,1)} %get-tuple-element.172), channel_id=1, source_target_pairs={{0,3},{1,2},{2,1},{3,0},{4,7},{5,6},{6,5},{7,4},{8,11},{9,10},{10,... | collective-permute-start | bytes 1671176 | tf_op jit(solution)/shard_map/adapter/ppermute | solution.py:821
  282.8 101.5 %all-to-all-start.3 = ((bf16[4,256,1024]{2,1,0:T(8,128)(2,1)}), bf16[4,256,1024]{2,1,0:T(8,128)(2,1)S(1)}, u32[]{:S(2)}, u32[]{:S(2)}) async-start(bf16[4,256,1024]{2,1,0:T(8,128)(2,1)} %bitcast.7), calls=%async_computation.3 | async-start | bytes 4194304 | tf_op jit(solution)/shard_map/all_to_all | solution.py:834
  322.6 57.8 %collective-permute-start.23 = (bf16[272,1024]{1,0:T(8,128)(2,1)S(1)}, bf16[272,1024]{1,0:T(8,128)(2,1)S(1)}, u32[]{:S(2)}, u32[]{:S(2)}) collective-permute-start(bf16[272,1024]{1,0:T(8,128)(2,1)S(1)} %add_convert_fusion.3), channel_id=1, source_target_pairs={{0,4},{4,0},{8,12},{12,8},{16,20},{20,16},{24,28},{28,24},{1,5},{5... | collective-permute-start | bytes 1671176 | tf_op jit(solution)/shard_map/adapter/ppermute | solution.py:821
  376.8 52.3 %collective-permute-start.24 = (f32[8,1024]{1,0:T(8,128)S(1)}, f32[8,1024]{1,0:T(8,128)S(1)}, u32[]{:S(2)}, u32[]{:S(2)}) collective-permute-start(f32[8,1024]{1,0:T(8,128)S(1)} %concatenate.4), channel_id=1, source_target_pairs={{0,1},{1,0},{2,3},{3,2},{4,5},{5,4},{6,7},{7,6},{8,9},{9,8},{10,11... | collective-permute-start | bytes 98312 | tf_op jit(solution)/shard_map/small/ppermute | solution.py:821
  376.9 52.3 %collective-permute-start.25 = (f32[8,1024]{1,0:T(8,128)S(1)}, f32[8,1024]{1,0:T(8,128)S(1)}, u32[]{:S(2)}, u32[]{:S(2)}) collective-permute-start(f32[8,1024]{1,0:T(8,128)S(1)} %concatenate.4), channel_id=1, source_target_pairs={{0,2},{1,3},{2,0},{3,1},{4,6},{5,7},{6,4},{7,5},{8,10},{9,11},{10,... | collective-permute-start | bytes 98312 | tf_op jit(solution)/shard_map/small/ppermute | solution.py:821
  378.4 50.8 %collective-permute-start.26 = (f32[8,1024]{1,0:T(8,128)S(1)}, f32[8,1024]{1,0:T(8,128)S(1)}, u32[]{:S(2)}, u32[]{:S(2)}) collective-permute-start(f32[8,1024]{1,0:T(8,128)S(1)} %concatenate.4), channel_id=1, source_target_pairs={{0,3},{1,2},{2,1},{3,0},{4,7},{5,6},{6,5},{7,4},{8,11},{9,10},{10,... | collective-permute-start | bytes 98312 | tf_op jit(solution)/shard_map/small/ppermute | solution.py:821
  382.4 46.7 %collective-permute-start.27 = (bf16[272,1024]{1,0:T(8,128)(2,1)S(1)}, bf16[272,1024]{1,0:T(8,128)(2,1)}, u32[]{:S(2)}, u32[]{:S(2)}) collective-permute-start(bf16[272,1024]{1,0:T(8,128)(2,1)S(1)} %add_convert_fusion.2), channel_id=1, source_target_pairs={{0,8},{4,12},{8,0},{12,4},{16,24},{20,28},{24,16},{28,20},{1,9},{5... | collective-permute-start | bytes 1671176 | tf_op jit(solution)/shard_map/adapter/ppermute | solution.py:821
  385.6 43.6 %all-to-all-start.4 = ((bf16[4,256,1024]{2,1,0:T(8,128)(2,1)}), bf16[4,256,1024]{2,1,0:T(8,128)(2,1)S(1)}, u32[]{:S(2)}, u32[]{:S(2)}) async-start(bf16[4,256,1024]{2,1,0:T(8,128)(2,1)} %bitcast.19), calls=%async_computation.4 | async-start | bytes 4194304 | tf_op jit(solution)/shard_map/all_to_all | solution.py:834
  430.5 37.5 %all-to-all-start.5 = ((bf16[4,256,1024]{2,1,0:T(8,128)(2,1)}), bf16[4,256,1024]{2,1,0:T(8,128)(2,1)}, u32[]{:S(2)}, u32[]{:S(2)}) async-start(bf16[4,256,1024]{2,1,0:T(8,128)(2,1)} %bitcast.18), calls=%async_computation.5 | async-start | bytes 4194304 | tf_op jit(solution)/shard_map/all_to_all | solution.py:834
  436.3 29.2 %collective-permute-start.28 = (bf16[272,1024]{1,0:T(8,128)(2,1)S(1)}, bf16[272,1024]{1,0:T(8,128)(2,1)S(1)}, u32[]{:S(2)}, u32[]{:S(2)}) collective-permute-start(bf16[272,1024]{1,0:T(8,128)(2,1)S(1)} %add_convert_fusion.1), channel_id=1, source_target_pairs={{0,16},{4,20},{8,24},{12,28},{16,0},{20,4},{24,8},{28,12},{1,17},{... | collective-permute-start | bytes 1671176 | tf_op jit(solution)/shard_map/adapter/ppermute | solution.py:821
  440.2 10.9 %collective-permute-start.30 = (f32[8,1024]{1,0:T(8,128)S(1)}, f32[8,1024]{1,0:T(8,128)S(1)}, u32[]{:S(2)}, u32[]{:S(2)}) collective-permute-start(f32[8,1024]{1,0:T(8,128)S(1)} %add.55), channel_id=1, source_target_pairs={{0,8},{4,12},{8,0},{12,4},{16,24},{20,28},{24,16},{28,20},{1,9},{5... | collective-permute-start | bytes 98312 | tf_op jit(solution)/shard_map/small/ppermute | solution.py:821
  451.2 13.1 %collective-permute-start.31 = (f32[8,1024]{1,0:T(8,128)S(1)}, f32[8,1024]{1,0:T(8,128)S(1)}, u32[]{:S(2)}, u32[]{:S(2)}) collective-permute-start(f32[8,1024]{1,0:T(8,128)S(1)} %add.56), channel_id=1, source_target_pairs={{0,16},{4,20},{8,24},{12,28},{16,0},{20,4},{24,8},{28,12},{1,17},{... | collective-permute-start | bytes 98312 | tf_op jit(solution)/shard_map/small/ppermute | solution.py:821
  (28 other events, 292.2 us)

commit v3 on v2

--- a/solution.py
+++ b/solution.py
@@ -72,22 +72,16 @@
     return jnp.sum(values, axis=0, keepdims=True)
 
 
-def pack_heads_kernel(ids_ref, q_ref, k_ref, v_ref, o_ref, own_ref, piece_ref, *half_refs):
+def pack_heads_kernel(ids_ref, q_ref, k_ref, v_ref, o_ref, own_ref):
     part = own_ref.shape[2]
-    turn = ids_ref[1]
     for m, ref in enumerate((q_ref, k_ref, v_ref, o_ref)):
         values = ref[...] if m == 3 else ref[...].T
         for t in range(4):
             own_ref[t, m] = values[t * part : (t + 1) * part]
-    piece_ref[0] = own_ref[turn]
-    for half_ref in half_refs:
-        for t in range(2):
-            half_ref[t] = own_ref[2 * (turn // 2) + t]
-
-
-def pack_units_kernel(ids_ref, up_ref, down_ref, ain_ref, aout_ref, bias_ref, own_ref, piece_ref):
+
+
+def pack_units_kernel(ids_ref, up_ref, down_ref, ain_ref, aout_ref, bias_ref, own_ref):
     units, extra = down_ref.shape[0] // 4, aout_ref.shape[0] // 4
-    turn = ids_ref[1]
     turned = ain_ref[...].T
     bias = bias_ref[...]
     begin = 2 * units + 2 * extra
@@ -98,7 +92,6 @@
         own_ref[t, 2 * units : 2 * units + extra] = turned[t * extra : (t + 1) * extra]
         own_ref[t, 2 * units + extra : begin] = aout_ref[t * extra : (t + 1) * extra, :]
         own_ref[t, begin:, : 4 * extra] = split_lines(bias)
-    piece_ref[0] = own_ref[turn]
 
 
 def split_lines(values):
@@ -111,13 +104,13 @@
     return jnp.concatenate(rows, axis=0)
 
 
-def pack(kernel, name, ids, own_shape, parts, *weights):
+def pack(kernel, name, ids, own_shape, *weights):
     vmem = pl.BlockSpec(memory_space=pltpu.VMEM)
     return pl.pallas_call(
         kernel,
         in_specs=[SMEM] + [vmem] * len(weights),
-        out_specs=[vmem] * len(parts),
-        out_shape=[jax.ShapeDtypeStruct((n,) + own_shape, BF16) for n in parts],
+        out_specs=vmem,
+        out_shape=jax.ShapeDtypeStruct((4,) + own_shape, BF16),
         compiler_params=pltpu.CompilerParams(vmem_limit_bytes=VMEM_LIMIT),
         cost_estimate=cost(0, 8 * 2**20),
         name=name,
@@ -372,33 +365,33 @@
         for p in range(4 * count):
             for copy in piece_copies(p):
                 copy.start()
-        if first:
-            acc[...] = jnp.zeros_like(acc)
-        else:
-            acc_copy().start()
-            acc_copy().wait()
-
+            if p == 3 and not first:
+                acc_copy().start()
+
+    half = min(512, span)
     for s in range(count):
 
-        @pl.when(step == 2 * s)
+        @pl.when(step == s)
         def _():
             for p in range(4 * s, 4 * s + 4):
                 for copy in piece_copies(p):
                     copy.wait()
-            rows = slice(4 * extra * s, 4 * extra * (s + 1))
-            a, slope = gelu_and_slope(nt(x_ref[...], ain[rows, :]) + sum_rows(bias[s].astype(F32)))
-            a_low = a.astype(BF16)
-            alow_ref[...] = a_low
-            gpa_ref[...] = slope.astype(BF16)
-            acc[...] += 4.0 * nn(a_low, aout[rows, :])
-
-    chunk = pl.ds(pl.multiple_of(step * (2 * units), 2 * units), 2 * units)
-    half = min(512, span)
-    for i in range(span // half):
-        rows = slice(i * half, (i + 1) * half)
-        h, slope = gelu_and_slope(nt(x_ref[rows, :], up[chunk, :]))
-        gp_ref[rows, :] = slope.astype(BF16)
-        acc[rows, :] += nn(h.astype(BF16), down[chunk, :])
+            wide = slice(4 * units * s, 4 * units * (s + 1))
+            small = slice(4 * extra * s, 4 * extra * (s + 1))
+            shift_a = sum_rows(bias[s].astype(F32))
+            for i in range(span // half):
+                rows = slice(i * half, (i + 1) * half)
+                x = x_ref[rows, :]
+                a, slope = gelu_and_slope(nt(x, ain[small, :]) + shift_a)
+                a_low = a.astype(BF16)
+                alow_ref[rows, :] = a_low
+                gpa_ref[rows, :] = slope.astype(BF16)
+                h, slope = gelu_and_slope(nt(x, up[wide, :]))
+                gp_ref[rows, :] = slope.astype(BF16)
+                total = nn(h.astype(BF16), down[wide, :]) + 4.0 * nn(a_low, aout[small, :])
+                if s == 0 and i == 0 and not first:
+                    acc_copy().wait()
+                acc[rows, :] = total if first and s == 0 else acc[rows, :] + total
 
     if last:
 
@@ -435,9 +428,9 @@
         jax.ShapeDtypeStruct((span, 16 * extra), BF16),
     ]
     kept_specs = [
-        pl.BlockSpec((span, 2 * units), lambda j: (0, 2 * slots[0] + j)),
-        pl.BlockSpec((span, 4 * extra), lambda j: (0, slots[0] + j // 2)),
-        pl.BlockSpec((span, 4 * extra), lambda j: (0, slots[0] + j // 2)),
+        pl.BlockSpec((span, 4 * units), lambda j: (0, slots[0] + j)),
+        pl.BlockSpec((span, 4 * extra), lambda j: (0, slots[0] + j)),
+        pl.BlockSpec((span, 4 * extra), lambda j: (0, slots[0] + j)),
     ]
     aliases = {}
     if not first:
@@ -454,7 +447,7 @@
         more, scratch = [total], []
     outs = pl.pallas_call(
         functools.partial(feed_kernel, slots, first, last, units, extra, homes),
-        grid=(2 * count,),
+        grid=(count,),
         in_specs=specs,
         out_specs=kept_specs + [once(s) for s in more],
         out_shape=kept_shape + more,
@@ -842,9 +835,22 @@
     return lax.optimization_barrier((values, earlier))[0]
 
 
-def send_near(what, half, piece):
+def near(what, own):
     with jax.named_scope(what + "_near"):
-        return cross_swap(half, 1, 2), swap(piece, "tensor", 3)
+        return cross_swap(own, 1, 2)
+
+
+def onward(what, shard, parts=2):
+    where = lax.axis_index("dp")
+    begin = 2 * (where % 2) + (where // 2 % 2 if parts == 1 else 0)
+    half = lax.dynamic_slice_in_dim(shard, begin, parts, 0)
+    with jax.named_scope(what + "_onward"):
+        return cross_swap(half, 2, 1)
+
+
+def core(what, values):
+    with jax.named_scope(what + "_core"):
+        return swap(values, "dp", 1)
 
 
 def all_pieces(*arrays):
@@ -874,7 +880,7 @@
     output_grad,
 ):
     place = lax.axis_index("tensor")
-    turn = lax.axis_index("dp") % 4
+    turn = 2 * (lax.axis_index("dp") % 2) + lax.axis_index("dp") // 2 % 2
     _, share, width = inputs.shape
     span = 4 * share
     units, extra = up_weight.shape[1] // 4, adapter_in.shape[1] // 4
@@ -886,94 +892,71 @@
     units_shape = (2 * units + 2 * extra + 16, width)
 
     x = turn_over(inputs).reshape(span, width)
-    self_own, self_piece, self_half = pack(
-        pack_heads_kernel, "pack_self", ids, heads_shape, (4, 1, 2), query_weight, key_weight, value_weight, output_weight
-    )
-    self_near = send_near("self", self_half, self_piece)
-    cross_own, cross_piece = pack(
+    self_own = pack(
+        pack_heads_kernel, "pack_self", ids, heads_shape, query_weight, key_weight, value_weight, output_weight
+    )
+    shard = near("self", self_own)
+    cross_own = pack(
         pack_heads_kernel,
         "pack_cross",
-        after(ids, self_half),
+        after(ids, self_own),
         heads_shape,
-        (4, 1),
         cross_query,
         cross_key,
         cross_value,
         cross_output,
     )
-    feed_own, feed_piece = pack(
+    feed_own = pack(
         pack_units_kernel,
         "pack_feed",
-        after(ids, cross_piece),
+        after(ids, cross_own),
         units_shape,
-        (4, 1),
         up_weight,
         down_weight,
         adapter_in,
         adapter_out,
         adapter_bias.reshape(1, -1),
     )
-    x = after(x, feed_piece)
-    source = turn_over(after(encoded, x)).reshape(span, width)
-    cross_near = send_near("cross", cross_own, cross_piece)
+    x = after(x, feed_own)
     self_kept = attend_slots(ids, (0,), x, None, all_pieces(self_own), None)
 
-    half, piece = after(self_near, self_kept[0])
-    with jax.named_scope("self_far"):
-        far_half, far_piece = swap(half, "dp", 2), swap(piece, "dp", 2)
-    with jax.named_scope("self_core"):
-        core_half, core_piece = swap(half, "dp", 1), swap(piece, "dp", 1)
-        core_far_half = swap(far_half, "dp", 1)
-    shard = after(cross_near[0], far_half)
-    self_pieces = all_pieces(self_own, half, far_half, core_half, core_far_half)
-    self_kept = attend_slots(ids, (1, 2), after(x, piece, shard), None, self_pieces, self_kept)
-    with jax.named_scope("self_core"):
-        core_far_piece = swap(after(far_piece, self_kept[0]), "dp", 1)
-    self_pieces += all_pieces(piece, core_piece, far_piece, core_far_piece)
-    feed_near = send_near("feed", after(feed_own, self_kept[0]), after(feed_piece, self_kept[0]))
-    shard, piece = after(shard, self_kept[0]), after(cross_near[1], self_kept[0])
-    with jax.named_scope("cross_far"):
-        far_piece = swap(piece, "dp", 2)
-    with jax.named_scope("cross_core"):
-        core_shard, core_piece = swap(shard, "dp", 1), swap(piece, "dp", 1)
-    self_kept = attend_slots(ids, (3,), after(x, piece), None, self_pieces, self_kept)
+    shard = after(shard, self_kept[0])
+    half, core_shard = onward("self", shard), core("self", shard)
+    source = turn_over(after(encoded, core_shard)).reshape(span, width)
+    self_pieces = all_pieces(self_own, shard, core_shard)
+    self_kept = attend_slots(ids, (1, 2), after(x, core_shard), None, self_pieces, self_kept)
+    half = after(half, self_kept[0])
+    self_pieces += all_pieces(half, core("self", half))
+    cross_shard = near("cross", after(cross_own, source, half))
+    self_kept = attend_slots(ids, (3,), x, None, self_pieces, self_kept)
     first, normed_one, scale_one = out_norm(self_kept[3], self_pieces, x, gain(0), shift(0))
 
-    with jax.named_scope("cross_core"):
-        core_far_piece = swap(after(far_piece, first), "dp", 1)
+    shard = after(cross_shard, first)
+    half, core_shard = onward("cross", shard), core("cross", shard)
+    feed_shard = near("feed", after(feed_own, shard))
     cross_pieces = all_pieces(cross_own, shard)
-    cross_kept = attend_slots(
-        ids, (0, 1), after(first, core_shard, core_piece, core_far_piece), source, cross_pieces, None
-    )
-    cross_pieces += all_pieces(core_shard, piece, core_piece, far_piece, core_far_piece)
+    cross_kept = attend_slots(ids, (0, 1), after(first, shard), source, cross_pieces, None)
+    half = after(half, cross_kept[0])
+    cross_pieces += all_pieces(core_shard, half, core("cross", half))
     cross_kept = attend_slots(ids, (2, 3), first, source, cross_pieces, cross_kept)
-    shard = after(feed_near[0], cross_kept[0])
-    grad = turn_over(after(output_grad, cross_kept[0])).reshape(span, width)
-    second, normed_two, scale_two = out_norm(
-        cross_kept[3], cross_pieces, after(first, shard), gain(1), shift(1)
-    )
-
-    with jax.named_scope("feed_core"):
-        core_shard = swap(after(shard, cross_kept[0]), "dp", 1)
+    second, normed_two, scale_two = out_norm(cross_kept[3], cross_pieces, first, gain(1), shift(1))
+
+    shard = after(feed_shard, second)
+    piece, core_shard = onward("feed", shard, 1), core("feed", shard)
     kept, rest = feed_slots(
-        ids, (0,), after(second, core_shard), all_pieces(feed_own), None, None, units, extra
-    )
-    piece = after(feed_near[1], rest[0])
+        ids, (0,), after(second, shard), all_pieces(feed_own), None, None, units, extra
+    )
+    piece = after(piece, rest[0])
     with jax.named_scope("feed_far"):
         far_piece = swap(piece, "dp", 2)
-    with jax.named_scope("feed_core"):
-        core_piece = swap(piece, "dp", 1)
+    core_piece = core("feed", piece)
     feed_pieces = all_pieces(feed_own, shard, core_shard)
-    kept, rest = feed_slots(
-        ids, (1, 2), after(second, piece), feed_pieces, rest + kept, None, units, extra
-    )
-    with jax.named_scope("feed_core"):
-        core_far_piece = swap(after(far_piece, rest[0]), "dp", 1)
-    feed_pieces += all_pieces(piece, core_piece, far_piece, core_far_piece)
+    grad = turn_over(after(output_grad, rest[0])).reshape(span, width)
+    kept, rest = feed_slots(ids, (1, 2), second, feed_pieces, rest + kept, None, units, extra)
+    far_piece = after(far_piece, rest[0], grad)
+    feed_pieces += all_pieces(piece, far_piece, core_piece, core("feed", far_piece))
     norm = (adapter_shift.reshape(1, -1), gain(2), shift(2), grad)
-    kept, rest = feed_slots(
-        ids, (3,), after(second, core_piece), feed_pieces, rest + kept, norm, units, extra
-    )
+    kept, rest = feed_slots(ids, (3,), second, feed_pieces, rest + kept, norm, units, extra)
     outcome, branch_low, sums_three = rest
     slopes, adapter_slopes, adapted_low = kept
     result = turn_over(outcome.reshape(4, share, width))

time: 481 us -> 464 us (0.965)
  Pallas kernels: 314 us -> 303 us
  starting transfers between devices: 59.8 us -> 49 us
  local copies, waits for them, and re-layouts: 19 us -> 24.5 us
    ppermute x27 -> x18, waiting for transfers between devices: 56.3 us -> 30.1 us  [swap(): return lax.ppermute(values, name, [(i, i ^ bit) for i in range(size)])]
    ppermute x5 -> x8, waiting for transfers between devices: 5.64 us -> 25.6 us  [cross_swap(): return lax.ppermute(values, ('dp', 'tensor'), pairs)]
    ppermute x27 -> x18, starting transfers between devices: 25.3 us -> 12.5 us  [swap(): return lax.ppermute(values, name, [(i, i ^ bit) for i in range(size)])]
    pallas_call x3, Pallas kernels: 61.6 us -> 51 us  [feed_slots(): pl.pallas_call(functools.partial(feed_kernel, slots, first, last, units,...]
    all_to_all x6, waiting for transfers between devices: 9.44 us -> 18.4 us  [turn_over(): return lax.all_to_all(values, 'tensor', 0, 0, tiled=True)]
    dynamic_slice x0 -> x3, local copies, waits for them, and re-layouts: none -> 5.95 us  [onward(): half = lax.dynamic_slice_in_dim(shard, begin, parts, 0)]
    ppermute x5 -> x8, starting transfers between devices: 8.8 us -> 11.2 us  [cross_swap(): return lax.ppermute(values, ('dp', 'tensor'), pairs)]
    unnamed x46 -> x36, local copies, waits for them, and re-layouts: 12.4 us -> 12 us
  transfers between devices with their start and end apart: 38 -> 32, of which waited for: 12 -> 15; matrix products, arithmetic and copies ran while one was open for 3% -> 4% of each run, Pallas kernels for 60% -> 60%
where the time goes in v3:
time: 464 us; the launch traced here: 458 us
  Pallas kernels  303 us (65%)
  waiting for transfers between devices  74.1 us (16%)
  starting transfers between devices  49 us (11%)
  local copies, waits for them, and re-layouts  24.5 us (5%)
  other arithmetic  6.28 us (1%)
    pallas_call x2, Pallas kernels, attention_back(): pl.pallas_call(functools.partial(attention_back_kernel, causal, homes), g...  93.4 us
    pallas_call x5, Pallas kernels, attend_slots(): pl.pallas_call(functools.partial(attend_kernel, causal, count, first, hom...  86.8 us
    pallas_call x3, Pallas kernels, feed_slots(): pl.pallas_call(functools.partial(feed_kernel, slots, first, last, units,...  51 us
    ppermute x18, waiting for transfers between devices, swap(): return lax.ppermute(values, name, [(i, i ^ bit) for i in range(size)])  30.1 us
    pallas_call x1, Pallas kernels, feed_back(): pl.pallas_call(functools.partial(feed_back_kernel, units, extra, homes),...  29.6 us
    ppermute x8, waiting for transfers between devices, cross_swap(): return lax.ppermute(values, ('dp', 'tensor'), pairs)  25.6 us
    all_to_all x6, starting transfers between devices, turn_over(): return lax.all_to_all(values, 'tensor', 0, 0, tiled=True)  25.3 us
    all_to_all x6, waiting for transfers between devices, turn_over(): return lax.all_to_all(values, 'tensor', 0, 0, tiled=True)  18.4 us
  transfers between devices with their start and end apart: 32, of which 15 were waited for; matrix products, arithmetic and copies ran while one was open for 4% of the time, Pallas kernels for 60%

profile of v3, /device:TPU:0, one launch (start us, length us, event | category | flops | bytes accessed | tf_op | source)
XLA Modules:
  0.0 458.5 jit_solution(9540128138219621997)
XLA Ops:
  0.7 5.2 %all-to-all-start = ((bf16[4,256,1024]{2,1,0:T(8,128)(2,1)}), bf16[4,256,1024]{2,1,0:T(8,128)(2,1)S(1)}, u32[]{:S(2)}, u32[]{:S(2)}) async-start(bf16[4,256,1024]{2,1,0:T(8,128)(2,1)} %param.20), calls=%async_computation | async-start | bytes 4194304 | tf_op jit(solution)/shard_map/all_to_all | solution.py:827
  7.7 3.3 pack_self.1.refs_1_.refs_4_
  13.0 3.4 pack_cross.1.refs_2_.refs_4_.refs_7_
  16.4 5.4 %pack_feed.1.refs_1_.refs_4_.refs_6_ = bf16[4,592,1024]{2,1,0:T(8,128)(2,1)} custom-call(s32[3]{0:T(128)} %pad_add_fusion.ids_ref, bf16[1024,1024]{1,0:T(8,128)(2,1)} %up_ref.1, bf16[1024,1024]{1,0:T(8,128)(2,1)} %down_ref.1, bf16[1024,128]{1,0:T(8,128)(2,1)} %ain_ref.1, bf16[128,1024]{1,0:T(8,128)(2,1)} %aout_ref.1, f32[1,128]{1,0:T(1,128)} %bitcast.22), custom_call_target="tpu_custom_call" | custom-call | bytes 8388608 | tf_op jit(solution)/shard_map/pack_feed/pallas_call | solution.py:109
  21.8 9.9 %all-to-all-done = bf16[4,256,1024]{2,1,0:T(8,128)(2,1)S(1)} async-done(((bf16[4,256,1024]{2,1,0:T(8,128)(2,1)}), bf16[4,256,1024]{2,1,0:T(8,128)(2,1)S(1)}, u32[]{:S(2)}, u32[]{:S(2)}) %all-to-all-start) | async-done | bytes 2097184 | tf_op jit(solution)/shard_map/all_to_all | solution.py:827
  33.0 10.6 %self_attend.3 = (bf16[16,1024,1024]{2,1,0:T(8,128)(2,1)}, bf16[4,1024,1024]{2,1,0:T(8,128)(2,1)}, f32[16,1,1024]{2,1,0:T(1,128)}, bf16[1024,1024]{1,0:T(8,128)(2,1)}) custom-call(s32[3]{0:T(128)} %pad_add_fusion.ids_ref, bf16[1024,1024]{1,0:T(8,128)(2,1)} %bitcast.13, bf16[4,4,64,1024]{3,2,1,0:T(8,128)(2,1)} %pack_self.1.refs_1_.refs_4_), custom_call_target="tpu_custom_call" | custom-call | flops 10000000000 | bytes 12582912 | tf_op jit(solution)/shard_map/self_attend/pallas_call | solution.py:234
  43.6 9.7 %collective-permute-done.refs_1_.refs_5_ = bf16[4,4,64,1024]{3,2,1,0:T(8,128)(2,1)} collective-permute-done((bf16[4,4,64,1024]{3,2,1,0:T(8,128)(2,1)}, bf16[4,4,64,1024]{3,2,1,0:T(8,128)(2,1)}, u32[]{:S(2)}, u32[]{:S(2)}) %collective-permute-start) | collective-permute-done | bytes 2097184 | tf_op jit(solution)/shard_map/self_near/ppermute | solution.py:823
  59.0 4.6 %all-to-all-start.1 = ((bf16[4,256,1024]{2,1,0:T(8,128)(2,1)}), bf16[4,256,1024]{2,1,0:T(8,128)(2,1)}, u32[]{:S(2)}, u32[]{:S(2)}) async-start(bf16[4,256,1024]{2,1,0:T(8,128)(2,1)} %param.21), calls=%async_computation.1 | async-start | bytes 4194304 | tf_op jit(solution)/shard_map/all_to_all | solution.py:827
  63.6 17.0 %self_attend.4 = (bf16[16,1024,1024]{2,1,0:T(8,128)(2,1)}, bf16[4,1024,1024]{2,1,0:T(8,128)(2,1)}, f32[16,1,1024]{2,1,0:T(1,128)}, bf16[1024,1024]{1,0:T(8,128)(2,1)}) custom-call(s32[3]{0:T(128)} %pad_add_fusion.ids_ref, bf16[1024,1024]{1,0:T(8,128)(2,1)} %bitcast.14, ...), custom_call_target="tpu_custom_call", output_to_operand_aliasing={{0}: (4, {}), {1}: (5, {}), {2}: (6, {}), {3}: (7, {})} | custom-call | flops 20000000000 | bytes 25165824 | tf_op jit(solution)/shard_map/self_attend/pallas_call | solution.py:234
  80.7 5.3 %collective-permute-done.1.refs_1_.refs_7_ = bf16[2,4,64,1024]{3,2,1,0:T(8,128)(2,1)S(1)} collective-permute-done((bf16[2,4,64,1024]{3,2,1,0:T(8,128)(2,1)}, bf16[2,4,64,1024]{3,2,1,0:T(8,128)(2,1)S(1)}, u32[]{:S(2)}, u32[]{:S(2)}) %collective-permute-start.1) | collective-permute-done | bytes 1048608 | tf_op jit(solution)/shard_map/self_onward/ppermute | solution.py:823
  86.0 7.2 %all-to-all-done.1 = bf16[4,256,1024]{2,1,0:T(8,128)(2,1)} async-done(((bf16[4,256,1024]{2,1,0:T(8,128)(2,1)}), bf16[4,256,1024]{2,1,0:T(8,128)(2,1)}, u32[]{:S(2)}, u32[]{:S(2)}) %all-to-all-start.1) | async-done | bytes 2097184 | tf_op jit(solution)/shard_map/all_to_all | solution.py:827
  95.0 10.7 %self_attend.5 = (bf16[16,1024,1024]{2,1,0:T(8,128)(2,1)}, bf16[4,1024,1024]{2,1,0:T(8,128)(2,1)}, f32[16,1,1024]{2,1,0:T(1,128)}, bf16[1024,1024]{1,0:T(8,128)(2,1)}) custom-call(s32[3]{0:T(128)} %pad_add_fusion.ids_ref, bf16[1024,1024]{1,0:T(8,128)(2,1)} %bitcast.15, ...), custom_call_target="tpu_custom_call", output_to_operand_aliasing={{0}: (4, {}), {1}: (5, {}), {2}: (6, {}), {3}: (7, {})} | custom-call | flops 10000000000 | bytes 12582912 | tf_op jit(solution)/shard_map/self_attend/pallas_call | solution.py:234
  105.7 8.3 %out_norm.2 = (bf16[1024,1024]{1,0:T(8,128)(2,1)}, bf16[1024,1024]{1,0:T(8,128)(2,1)}, f32[1024,1]{1,0:T(8,128)}) custom-call(bf16[1024,1024]{1,0:T(8,128)(2,1)} %get-tuple-element.102.refs_0_, bf16[1024,1024]{1,0:T(8,128)(2,1)} %bitcast.16, f32[1,1024]{1,0:T(1,128)} %get-tuple-element.191.refs_2_.refs_6_, f32[1,1024]{1,0:T(1,128)} %get-tuple-element.185.refs_3_, ...), custom_call_target="tpu_custom_call" | custom-call | flops 2147483648 | bytes 10485760 | tf_op jit(solution)/shard_map/out_norm/pallas_call | solution.py:299
  114.0 5.3 %collective-permute-done.4.refs_3_.refs_5_.refs_8_ = bf16[4,4,64,1024]{3,2,1,0:T(8,128)(2,1)} collective-permute-done((bf16[4,4,64,1024]{3,2,1,0:T(8,128)(2,1)S(1)}, bf16[4,4,64,1024]{3,2,1,0:T(8,128)(2,1)}, u32[]{:S(2)}, u32[]{:S(2)}) %collective-permute-start.4) | collective-permute-done | bytes 2097184 | tf_op jit(solution)/shard_map/cross_near/ppermute | solution.py:823
  122.8 24.3 %cross_attend.2 = (bf16[16,1024,1024]{2,1,0:T(8,128)(2,1)}, bf16[4,1024,1024]{2,1,0:T(8,128)(2,1)}, f32[16,1,1024]{2,1,0:T(1,128)}, bf16[1024,1024]{1,0:T(8,128)(2,1)}) custom-call(s32[3]{0:T(128)} %pad_add_fusion.ids_ref, bf16[1024,1024]{1,0:T(8,128)(2,1)} %get-tuple-element.107.refs_0_.refs_1_, bf16[1024,1024]{1,0:T(8,128)(2,1)} %bitcast.4.refs_1_, ...), custom_call_target="tpu_custom_call" | custom-call | flops 20000000000 | bytes 25165824 | tf_op jit(solution)/shard_map/cross_attend/pallas_call | solution.py:234
  151.7 24.3 %cross_attend.3 = (bf16[16,1024,1024]{2,1,0:T(8,128)(2,1)}, bf16[4,1024,1024]{2,1,0:T(8,128)(2,1)}, f32[16,1,1024]{2,1,0:T(1,128)}, bf16[1024,1024]{1,0:T(8,128)(2,1)}) custom-call(s32[3]{0:T(128)} %pad_add_fusion.ids_ref, ...), custom_call_target="tpu_custom_call", output_to_operand_aliasing={{0}: (6, {}), {1}: (7, {}), {2}: (8, {}), {3}: (9, {})} | custom-call | flops 20000000000 | bytes 25165824 | tf_op jit(solution)/shard_map/cross_attend/pallas_call | solution.py:234
  176.0 8.8 %out_norm.3 = (bf16[1024,1024]{1,0:T(8,128)(2,1)}, bf16[1024,1024]{1,0:T(8,128)(2,1)}, f32[1024,1]{1,0:T(8,128)}) custom-call(bf16[1024,1024]{1,0:T(8,128)(2,1)} %get-tuple-element.113.refs_0_, bf16[1024,1024]{1,0:T(8,128)(2,1)} %get-tuple-element.107.refs_0_.refs_1_, f32[1,1024]{1,0:T(1,128)} %get-tuple-element.190.refs_2_.refs_5_, ...), custom_call_target="tpu_custom_call" | custom-call | flops 2147483648 | bytes 10485760 | tf_op jit(solution)/shard_map/out_norm/pallas_call | solution.py:299
  191.3 12.4 %feed.3 = (bf16[1024,4096]{1,0:T(8,128)(2,1)}, bf16[1024,512]{1,0:T(8,128)(2,1)}, bf16[1024,512]{1,0:T(8,128)(2,1)}, f32[1024,1024]{1,0:T(8,128)}) custom-call(s32[3]{0:T(128)} %pad_add_fusion.ids_ref, bf16[1024,1024]{1,0:T(8,128)(2,1)} %get-tuple-element.117.refs_0_.refs_1_, bf16[4,592,1024]{2,1,0:T(8,128)(2,1)} %pack_feed.1.refs_1_.refs_4_.refs_6_), custom_call_target="tpu_custom_call" | custom-call | flops 6000000000 | bytes 14680064 | tf_op jit(solution)/shard_map/feed/pallas_call | solution.py:448
  203.7 3.6 all-to-all-start.2
  209.1 21.8 %feed.4 = (bf16[1024,4096]{1,0:T(8,128)(2,1)}, bf16[1024,512]{1,0:T(8,128)(2,1)}, bf16[1024,512]{1,0:T(8,128)(2,1)}, f32[1024,1024]{1,0:T(8,128)}) custom-call(s32[3]{0:T(128)} %pad_add_fusion.ids_ref, bf16[1024,1024]{1,0:T(8,128)(2,1)} %get-tuple-element.117.refs_0_.refs_1_, ...), custom_call_target="tpu_custom_call", output_to_operand_aliasing={{0}: (5, {}), {1}: (6, {}), {2}: (7, {})} | custom-call | flops 12000000000 | bytes 29360128 | tf_op jit(solution)/shard_map/feed/pallas_call | solution.py:448
  232.2 3.5 collective-permute-done.10.refs_2_.refs_8_.refs_10_
  239.0 16.8 %feed.5 = (bf16[1024,4096]{1,0:T(8,128)(2,1)}, bf16[1024,512]{1,0:T(8,128)(2,1)}, bf16[1024,512]{1,0:T(8,128)(2,1)}, bf16[1024,1024]{1,0:T(8,128)(2,1)}, bf16[1024,1024]{1,0:T(8,128)(2,1)}, /*index=5*/f32[8,1024]{1,0:T(8,128)}) custom-call(s32[3]{0:T(128)} %pad_add_fusion.ids_ref, ...), custom_call_target="tpu_custom_call", output_to_operand_aliasing={{0}: (11, {}), {1}: (12, {}), {2}: (13, {})} | custom-call | flops 6000000000 | bytes 14680064 | tf_op jit(solution)/shard_map/feed/pallas_call | solution.py:448
  257.3 9.4 %adapter_back.1 = (bf16[1024,512]{1,0:T(8,128)(2,1)}, bf16[272,1024]{1,0:T(8,128)(2,1)}, bf16[272,1024]{1,0:T(8,128)(2,1)}, bf16[272,1024]{1,0:T(8,128)(2,1)}, bf16[272,1024]{1,0:T(8,128)(2,1)}) custom-call(s32[3]{0:T(128)} %pad_add_fusion.ids_ref, bf16[1024,1024]{1,0:T(8,128)(2,1)} %get-tuple-element.133.refs_0_, ...), custom_call_target="tpu_custom_call" | custom-call | flops 3221225472 | bytes 12582912 | tf_op jit(solution)/shard_map/adapter_back/pallas_call | solution.py:514
  270.3 3.8 all-to-all-start.3
  274.1 29.6 %feed_back.1 = (bf16[1024,1024]{1,0:T(8,128)(2,1)}, f32[8,1024]{1,0:T(8,128)}) custom-call(s32[3]{0:T(128)} %pad_add_fusion.ids_ref, bf16[1024,1024]{1,0:T(8,128)(2,1)} %get-tuple-element.133.refs_0_, bf16[1024,4096]{1,0:T(8,128)(2,1)} %get-tuple-element.134.refs_1_, bf16[1024,512]{1,0:T(8,128)(2,1)} %get-tuple-element.132.refs_2_, ...), custom_call_target="tpu_custom_call" | custom-call | flops 20000000000 | bytes 41943040 | tf_op jit(solution)/shard_map/feed_back/pallas_call | solution.py:605
  309.3 53.4 %cross_back.1 = (bf16[1024,1024]{1,0:T(8,128)(2,1)}, bf16[1024,1024]{1,0:T(8,128)(2,1)}, f32[8,1024]{1,0:T(8,128)}) custom-call(bf16[1024,1024]{1,0:T(8,128)(2,1)} %get-tuple-element.142.refs_0_, bf16[16,1024,1024]{2,1,0:T(8,128)(2,1)} %get-tuple-element.143.refs_1_, bf16[4,1024,1024]{2,1,0:T(8,128)(2,1)} %get-tuple-element.144.refs_2_, ...), custom_call_target="tpu_custom_call" | custom-call | flops 40000000000 | bytes 62914560 | tf_op jit(solution)/shard_map/cross_back/pallas_call | solution.py:774
  372.4 3.6 all-to-all-start.4
  376.0 40.0 %self_back.1 = (bf16[1024,1024]{1,0:T(8,128)(2,1)}, bf16[4,256,1024]{2,1,0:T(8,128)(2,1)}) custom-call(bf16[1024,1024]{1,0:T(8,128)(2,1)} %get-tuple-element.153.refs_0_, bf16[16,1024,1024]{2,1,0:T(8,128)(2,1)} %get-tuple-element.154.refs_1_, bf16[4,1024,1024]{2,1,0:T(8,128)(2,1)} %get-tuple-element.155.refs_2_, f32[16,1,1024]{2,1,0:T(1,128)} %get-tuple-element.156.refs_3_, ...), custom_call_target="tpu_custom_call" | custom-call | flops 40000000000 | bytes 62914560 | tf_op jit(solution)/shard_map/self_back/pallas_call | solution.py:774
  417.6 4.5 all-to-all-start.5
  427.7 10.4 %collective-permute-done.24 = f32[8,1024]{1,0:T(8,128)S(1)} collective-permute-done((f32[8,1024]{1,0:T(8,128)S(1)}, f32[8,1024]{1,0:T(8,128)S(1)}, u32[]{:S(2)}, u32[]{:S(2)}) %collective-permute-start.24) | collective-permute-done | bytes 32800 | tf_op jit(solution)/shard_map/small/ppermute | solution.py:814
  439.3 3.8 copied.1
  443.1 8.3 %collective-permute-done.25 = f32[8,1024]{1,0:T(8,128)S(1)} collective-permute-done((f32[8,1024]{1,0:T(8,128)S(1)}, f32[8,1024]{1,0:T(8,128)S(1)}, u32[]{:S(2)}, u32[]{:S(2)}) %collective-permute-start.25) | collective-permute-done | bytes 32800 | tf_op jit(solution)/shard_map/small/ppermute | solution.py:814
  (110 shorter events, 69.1 us)
Async XLA Ops:
  0.7 31.1 %all-to-all-start = ((bf16[4,256,1024]{2,1,0:T(8,128)(2,1)}), bf16[4,256,1024]{2,1,0:T(8,128)(2,1)S(1)}, u32[]{:S(2)}, u32[]{:S(2)}) async-start(bf16[4,256,1024]{2,1,0:T(8,128)(2,1)} %param.20), calls=%async_computation | async-start | bytes 4194304 | tf_op jit(solution)/shard_map/all_to_all | solution.py:827
  11.0 42.3 %collective-permute-start = (bf16[4,4,64,1024]{3,2,1,0:T(8,128)(2,1)}, bf16[4,4,64,1024]{3,2,1,0:T(8,128)(2,1)}, u32[]{:S(2)}, u32[]{:S(2)}) collective-permute-start(bf16[4,4,64,1024]{3,2,1,0:T(8,128)(2,1)} %pack_self.1.refs_1_.refs_4_), channel_id=1, source_target_pairs={{0,1},{1,0},{2,3},{3,2},{4,6},{5,7},{6,4},{7,5},{8,9},{9,8},{10,11... | collective-permute-start | bytes 6291464 | tf_op jit(solution)/shard_map/self_near/ppermute | solution.py:823
  53.3 4.4 collective-permute-start.2
  55.6 30.4 %collective-permute-start.1 = (bf16[2,4,64,1024]{3,2,1,0:T(8,128)(2,1)}, bf16[2,4,64,1024]{3,2,1,0:T(8,128)(2,1)S(1)}, u32[]{:S(2)}, u32[]{:S(2)}) collective-permute-start(bf16[2,4,64,1024]{3,2,1,0:T(8,128)(2,1)} %constant_dynamic-slice_fusion.2), channel_id=1, source_target_pairs={{0,2},{1,3},{2,0},{3,1},{4,5},{5,4},{6,7},{7,6},{8,10},{9,11},{10,... | collective-permute-start | bytes 3145736 | tf_op jit(solution)/shard_map/self_onward/ppermute | solution.py:823
  59.0 34.2 %all-to-all-start.1 = ((bf16[4,256,1024]{2,1,0:T(8,128)(2,1)}), bf16[4,256,1024]{2,1,0:T(8,128)(2,1)}, u32[]{:S(2)}, u32[]{:S(2)}) async-start(bf16[4,256,1024]{2,1,0:T(8,128)(2,1)} %param.21), calls=%async_computation.1 | async-start | bytes 4194304 | tf_op jit(solution)/shard_map/all_to_all | solution.py:827
  86.0 9.0 %collective-permute-start.3 = (bf16[2,4,64,1024]{3,2,1,0:T(8,128)(2,1)S(1)}, bf16[2,4,64,1024]{3,2,1,0:T(8,128)(2,1)}, u32[]{:S(2)}, u32[]{:S(2)}) collective-permute-start(bf16[2,4,64,1024]{3,2,1,0:T(8,128)(2,1)S(1)} %collective-permute-done.1.refs_1_.refs_7_), channel_id=1, source_target_pairs={{0,4},{4,0},{8,12},{12,8},{16,20},{20,16},{24,28},{28,24},{1,5},{5... | collective-permute-start | bytes 3145736 | tf_op jit(solution)/shard_map/self_core/ppermute | solution.py:814
  93.2 26.1 %collective-permute-start.4 = (bf16[4,4,64,1024]{3,2,1,0:T(8,128)(2,1)S(1)}, bf16[4,4,64,1024]{3,2,1,0:T(8,128)(2,1)}, u32[]{:S(2)}, u32[]{:S(2)}) collective-permute-start(bf16[4,4,64,1024]{3,2,1,0:T(8,128)(2,1)S(1)} %copy-done.2), channel_id=1, source_target_pairs={{0,1},{1,0},{2,3},{3,2},{4,6},{5,7},{6,4},{7,5},{8,9},{9,8},{10,11... | collective-permute-start | bytes 6291464 | tf_op jit(solution)/shard_map/cross_near/ppermute | solution.py:823
  120.6 29.4 %collective-permute-start.5 = (bf16[4,4,64,1024]{3,2,1,0:T(8,128)(2,1)}, bf16[4,4,64,1024]{3,2,1,0:T(8,128)(2,1)S(1)}, u32[]{:S(2)}, u32[]{:S(2)}) collective-permute-start(bf16[4,4,64,1024]{3,2,1,0:T(8,128)(2,1)} %collective-permute-done.4.refs_3_.refs_5_.refs_8_), channel_id=1, source_target_pairs={{0,4},{4,0},{8,12},{12,8},{16,20},{20,16},{24,28},{28,24},{1,5},{5... | collective-permute-start | bytes 6291464 | tf_op jit(solution)/shard_map/cross_core/ppermute | solution.py:814
  120.7 26.4 %collective-permute-start.6 = (bf16[2,4,64,1024]{3,2,1,0:T(8,128)(2,1)S(1)}, bf16[2,4,64,1024]{3,2,1,0:T(8,128)(2,1)}, u32[]{:S(2)}, u32[]{:S(2)}) collective-permute-start(bf16[2,4,64,1024]{3,2,1,0:T(8,128)(2,1)S(1)} %constant_dynamic-slice_fusion.1), channel_id=1, source_target_pairs={{0,2},{1,3},{2,0},{3,1},{4,5},{5,4},{6,7},{7,6},{8,10},{9,11},{10,... | collective-permute-start | bytes 3145736 | tf_op jit(solution)/shard_map/cross_onward/ppermute | solution.py:823
  122.2 64.9 %collective-permute-start.8 = (bf16[4,592,1024]{2,1,0:T(8,128)(2,1)}, bf16[4,592,1024]{2,1,0:T(8,128)(2,1)}, u32[]{:S(2)}, u32[]{:S(2)}) collective-permute-start(bf16[4,592,1024]{2,1,0:T(8,128)(2,1)} %pack_feed.1.refs_1_.refs_4_.refs_6_), channel_id=1, source_target_pairs={{0,1},{1,0},{2,3},{3,2},{4,6},{5,7},{6,4},{7,5},{8,9},{9,8},{10,11... | collective-permute-start | bytes 14549000 | tf_op jit(solution)/shard_map/feed_near/ppermute | solution.py:823
  147.1 2.9 collective-permute-start.7
  187.1 22.0 %collective-permute-start.11 = (bf16[4,592,1024]{2,1,0:T(8,128)(2,1)}, bf16[4,592,1024]{2,1,0:T(8,128)(2,1)}, u32[]{:S(2)}, u32[]{:S(2)}) collective-permute-start(bf16[4,592,1024]{2,1,0:T(8,128)(2,1)} %collective-permute-done.8.refs_1_.refs_5_.refs_7_), channel_id=1, source_target_pairs={{0,4},{4,0},{8,12},{12,8},{16,20},{20,16},{24,28},{28,24},{1,5},{5... | collective-permute-start | bytes 14549000 | tf_op jit(solution)/shard_map/feed_core/ppermute | solution.py:814
  189.9 17.4 %collective-permute-start.9 = (bf16[1,592,1024]{2,1,0:T(8,128)(2,1)}, bf16[1,592,1024]{2,1,0:T(8,128)(2,1)S(1)}, u32[]{:S(2)}, u32[]{:S(2)}) collective-permute-start(bf16[1,592,1024]{2,1,0:T(8,128)(2,1)} %constant_dynamic-slice_fusion), channel_id=1, source_target_pairs={{0,2},{1,3},{2,0},{3,1},{4,5},{5,4},{6,7},{7,6},{8,10},{9,11},{10,... | collective-permute-start | bytes 3637256 | tf_op jit(solution)/shard_map/feed_onward/ppermute | solution.py:823
  203.7 28.6 %all-to-all-start.2 = ((bf16[4,256,1024]{2,1,0:T(8,128)(2,1)}), bf16[4,256,1024]{2,1,0:T(8,128)(2,1)S(1)}, u32[]{:S(2)}, u32[]{:S(2)}) async-start(bf16[4,256,1024]{2,1,0:T(8,128)(2,1)} %param.39), calls=%async_computation.2 | async-start | bytes 4194304 | tf_op jit(solution)/shard_map/all_to_all | solution.py:827
  207.3 28.4 %collective-permute-start.10 = (bf16[1,592,1024]{2,1,0:T(8,128)(2,1)S(1)}, bf16[1,592,1024]{2,1,0:T(8,128)(2,1)}, u32[]{:S(2)}, u32[]{:S(2)}) collective-permute-start(bf16[1,592,1024]{2,1,0:T(8,128)(2,1)S(1)} %collective-permute-done.9.refs_1_.refs_7_.refs_9_), channel_id=1, source_target_pairs={{0,8},{4,12},{8,0},{12,4},{16,24},{20,28},{24,16},{28,20},{1,9},{5... | collective-permute-start | bytes 3637256 | tf_op jit(solution)/shard_map/feed_far/ppermute | solution.py:814
  209.1 26.6 %collective-permute-start.12 = (bf16[1,592,1024]{2,1,0:T(8,128)(2,1)S(1)}, bf16[1,592,1024]{2,1,0:T(8,128)(2,1)}, u32[]{:S(2)}, u32[]{:S(2)}) collective-permute-start(bf16[1,592,1024]{2,1,0:T(8,128)(2,1)S(1)} %collective-permute-done.9.refs_1_.refs_7_.refs_9_), channel_id=1, source_target_pairs={{0,4},{4,0},{8,12},{12,8},{16,20},{20,16},{24,28},{28,24},{1,5},{5... | collective-permute-start | bytes 3637256 | tf_op jit(solution)/shard_map/feed_core/ppermute | solution.py:814
  235.7 3.2 collective-permute-start.13
  266.7 37.8 %collective-permute-start.14 = (bf16[272,1024]{1,0:T(8,128)(2,1)}, bf16[272,1024]{1,0:T(8,128)(2,1)S(1)}, u32[]{:S(2)}, u32[]{:S(2)}) collective-permute-start(bf16[272,1024]{1,0:T(8,128)(2,1)} %get-tuple-element.139), channel_id=1, source_target_pairs={{0,1},{1,0},{2,3},{3,2},{4,6},{5,7},{6,4},{7,5},{8,9},{9,8},{10,11... | collective-permute-start | bytes 1671176 | tf_op jit(solution)/shard_map/adapter/ppermute | solution.py:823
  268.4 39.1 %collective-permute-start.15 = (bf16[272,1024]{1,0:T(8,128)(2,1)}, bf16[272,1024]{1,0:T(8,128)(2,1)}, u32[]{:S(2)}, u32[]{:S(2)}) collective-permute-start(bf16[272,1024]{1,0:T(8,128)(2,1)} %get-tuple-element.140), channel_id=1, source_target_pairs={{0,2},{1,3},{2,0},{3,1},{4,5},{5,4},{6,7},{7,6},{8,10},{9,11},{10,... | collective-permute-start | bytes 1671176 | tf_op jit(solution)/shard_map/adapter/ppermute | solution.py:823
  269.9 37.6 %collective-permute-start.16 = (bf16[272,1024]{1,0:T(8,128)(2,1)}, bf16[272,1024]{1,0:T(8,128)(2,1)}, u32[]{:S(2)}, u32[]{:S(2)}) collective-permute-start(bf16[272,1024]{1,0:T(8,128)(2,1)} %get-tuple-element.141), channel_id=1, source_target_pairs={{0,3},{1,2},{2,1},{3,0},{4,7},{5,6},{6,5},{7,4},{8,11},{9,10},{10,... | collective-permute-start | bytes 1671176 | tf_op jit(solution)/shard_map/adapter/ppermute | solution.py:814
  270.3 100.8 %all-to-all-start.3 = ((bf16[4,256,1024]{2,1,0:T(8,128)(2,1)}), bf16[4,256,1024]{2,1,0:T(8,128)(2,1)S(1)}, u32[]{:S(2)}, u32[]{:S(2)}) async-start(bf16[4,256,1024]{2,1,0:T(8,128)(2,1)} %bitcast.7), calls=%async_computation.3 | async-start | bytes 4194304 | tf_op jit(solution)/shard_map/all_to_all | solution.py:827
  309.2 58.0 %collective-permute-start.17 = (bf16[272,1024]{1,0:T(8,128)(2,1)S(1)}, bf16[272,1024]{1,0:T(8,128)(2,1)S(1)}, u32[]{:S(2)}, u32[]{:S(2)}) collective-permute-start(bf16[272,1024]{1,0:T(8,128)(2,1)S(1)} %add_convert_fusion.3), channel_id=1, source_target_pairs={{0,4},{4,0},{8,12},{12,8},{16,20},{20,16},{24,28},{28,24},{1,5},{5... | collective-permute-start | bytes 1671176 | tf_op jit(solution)/shard_map/adapter/ppermute | solution.py:814
  363.7 52.4 %collective-permute-start.18 = (f32[8,1024]{1,0:T(8,128)S(1)}, f32[8,1024]{1,0:T(8,128)S(1)}, u32[]{:S(2)}, u32[]{:S(2)}) collective-permute-start(f32[8,1024]{1,0:T(8,128)S(1)} %concatenate.4), channel_id=1, source_target_pairs={{0,1},{1,0},{2,3},{3,2},{4,5},{5,4},{6,7},{7,6},{8,9},{9,8},{10,11... | collective-permute-start | bytes 98312 | tf_op jit(solution)/shard_map/small/ppermute | solution.py:814
  363.7 52.3 %collective-permute-start.19 = (f32[8,1024]{1,0:T(8,128)S(1)}, f32[8,1024]{1,0:T(8,128)S(1)}, u32[]{:S(2)}, u32[]{:S(2)}) collective-permute-start(f32[8,1024]{1,0:T(8,128)S(1)} %concatenate.4), channel_id=1, source_target_pairs={{0,2},{1,3},{2,0},{3,1},{4,6},{5,7},{6,4},{7,5},{8,10},{9,11},{10,... | collective-permute-start | bytes 98312 | tf_op jit(solution)/shard_map/small/ppermute | solution.py:814
  365.3 50.8 %collective-permute-start.20 = (f32[8,1024]{1,0:T(8,128)S(1)}, f32[8,1024]{1,0:T(8,128)S(1)}, u32[]{:S(2)}, u32[]{:S(2)}) collective-permute-start(f32[8,1024]{1,0:T(8,128)S(1)} %concatenate.4), channel_id=1, source_target_pairs={{0,3},{1,2},{2,1},{3,0},{4,7},{5,6},{6,5},{7,4},{8,11},{9,10},{10,... | collective-permute-start | bytes 98312 | tf_op jit(solution)/shard_map/small/ppermute | solution.py:814
  369.3 46.8 %collective-permute-start.21 = (bf16[272,1024]{1,0:T(8,128)(2,1)S(1)}, bf16[272,1024]{1,0:T(8,128)(2,1)S(1)}, u32[]{:S(2)}, u32[]{:S(2)}) collective-permute-start(bf16[272,1024]{1,0:T(8,128)(2,1)S(1)} %add_convert_fusion.2), channel_id=1, source_target_pairs={{0,8},{4,12},{8,0},{12,4},{16,24},{20,28},{24,16},{28,20},{1,9},{5... | collective-permute-start | bytes 1671176 | tf_op jit(solution)/shard_map/adapter/ppermute | solution.py:814
  372.4 43.7 %all-to-all-start.4 = ((bf16[4,256,1024]{2,1,0:T(8,128)(2,1)}), bf16[4,256,1024]{2,1,0:T(8,128)(2,1)S(1)}, u32[]{:S(2)}, u32[]{:S(2)}) async-start(bf16[4,256,1024]{2,1,0:T(8,128)(2,1)} %bitcast.19), calls=%async_computation.4 | async-start | bytes 4194304 | tf_op jit(solution)/shard_map/all_to_all | solution.py:827
  417.6 37.6 %all-to-all-start.5 = ((bf16[4,256,1024]{2,1,0:T(8,128)(2,1)}), bf16[4,256,1024]{2,1,0:T(8,128)(2,1)}, u32[]{:S(2)}, u32[]{:S(2)}) async-start(bf16[4,256,1024]{2,1,0:T(8,128)(2,1)} %bitcast.18), calls=%async_computation.5 | async-start | bytes 4194304 | tf_op jit(solution)/shard_map/all_to_all | solution.py:827
  423.3 29.2 %collective-permute-start.22 = (bf16[272,1024]{1,0:T(8,128)(2,1)S(1)}, bf16[272,1024]{1,0:T(8,128)(2,1)S(1)}, u32[]{:S(2)}, u32[]{:S(2)}) collective-permute-start(bf16[272,1024]{1,0:T(8,128)(2,1)S(1)} %add_convert_fusion.1), channel_id=1, source_target_pairs={{0,16},{4,20},{8,24},{12,28},{16,0},{20,4},{24,8},{28,12},{1,17},{... | collective-permute-start | bytes 1671176 | tf_op jit(solution)/shard_map/adapter/ppermute | solution.py:814
  426.0 1.3 collective-permute-start.23
  427.2 10.9 %collective-permute-start.24 = (f32[8,1024]{1,0:T(8,128)S(1)}, f32[8,1024]{1,0:T(8,128)S(1)}, u32[]{:S(2)}, u32[]{:S(2)}) collective-permute-start(f32[8,1024]{1,0:T(8,128)S(1)} %add.78), channel_id=1, source_target_pairs={{0,8},{4,12},{8,0},{12,4},{16,24},{20,28},{24,16},{28,20},{1,9},{5... | collective-permute-start | bytes 98312 | tf_op jit(solution)/shard_map/small/ppermute | solution.py:814
  438.1 13.2 %collective-permute-start.25 = (f32[8,1024]{1,0:T(8,128)S(1)}, f32[8,1024]{1,0:T(8,128)S(1)}, u32[]{:S(2)}, u32[]{:S(2)}) collective-permute-start(f32[8,1024]{1,0:T(8,128)S(1)} %add.79), channel_id=1, source_target_pairs={{0,16},{4,20},{8,24},{12,28},{16,0},{20,4},{24,8},{28,12},{1,17},{... | collective-permute-start | bytes 98312 | tf_op jit(solution)/shard_map/small/ppermute | solution.py:814
  (17 other events, 181.7 us)

commit v4 on v3

--- a/solution.py
+++ b/solution.py
@@ -951,7 +951,7 @@
         far_piece = swap(piece, "dp", 2)
     core_piece = core("feed", piece)
     feed_pieces = all_pieces(feed_own, shard, core_shard)
-    grad = turn_over(after(output_grad, rest[0])).reshape(span, width)
+    grad = turn_over(after(output_grad, core_piece)).reshape(span, width)
     kept, rest = feed_slots(ids, (1, 2), second, feed_pieces, rest + kept, None, units, extra)
     far_piece = after(far_piece, rest[0], grad)
     feed_pieces += all_pieces(piece, far_piece, core_piece, core("feed", far_piece))

time: 464 us -> 471 us (1.015)
  waiting for transfers between devices: 74.1 us -> 80.2 us
    unnamed x36 -> x38, local copies, waits for them, and re-layouts: 12 us -> 13.1 us
  transfers between devices with their start and end apart: 32 -> 32, of which waited for: 15 -> 16; matrix products, arithmetic and copies ran while one was open for 4% -> 3% of each run, Pallas kernels for 60% -> 60%
where the time goes in v4:
time: 471 us; the launch traced here: 465 us
  Pallas kernels  303 us (64%)
  waiting for transfers between devices  80.2 us (17%)
  starting transfers between devices  49.1 us (10%)
  local copies, waits for them, and re-layouts  24.6 us (5%)
  other arithmetic  6.25 us (1%)
    pallas_call x2, Pallas kernels, attention_back(): pl.pallas_call(functools.partial(attention_back_kernel, causal, homes), g...  93.4 us
    pallas_call x5, Pallas kernels, attend_slots(): pl.pallas_call(functools.partial(attend_kernel, causal, count, first, hom...  86.8 us
    pallas_call x3, Pallas kernels, feed_slots(): pl.pallas_call(functools.partial(feed_kernel, slots, first, last, units,...  51 us
    ppermute x18, waiting for transfers between devices, swap(): return lax.ppermute(values, name, [(i, i ^ bit) for i in range(size)])  34.8 us
    pallas_call x1, Pallas kernels, feed_back(): pl.pallas_call(functools.partial(feed_back_kernel, units, extra, homes),...  29.6 us
    ppermute x8, waiting for transfers between devices, cross_swap(): return lax.ppermute(values, ('dp', 'tensor'), pairs)  28.3 us
    all_to_all x6, starting transfers between devices, turn_over(): return lax.all_to_all(values, 'tensor', 0, 0, tiled=True)  25.3 us
    all_to_all x6, waiting for transfers between devices, turn_over(): return lax.all_to_all(values, 'tensor', 0, 0, tiled=True)  17.1 us
  transfers between devices with their start and end apart: 32, of which 16 were waited for; matrix products, arithmetic and copies ran while one was open for 3% of the time, Pallas kernels for 60%

profile of v4, /device:TPU:0, one launch (start us, length us, event | category | flops | bytes accessed | tf_op | source)
XLA Modules:
  0.0 464.6 jit_solution(12852224823921803917)
XLA Ops:
  0.7 5.2 %all-to-all-start = ((bf16[4,256,1024]{2,1,0:T(8,128)(2,1)}), bf16[4,256,1024]{2,1,0:T(8,128)(2,1)S(1)}, u32[]{:S(2)}, u32[]{:S(2)}) async-start(bf16[4,256,1024]{2,1,0:T(8,128)(2,1)} %param.20), calls=%async_computation | async-start | bytes 4194304 | tf_op jit(solution)/shard_map/all_to_all | solution.py:827
  7.6 3.3 pack_self.1.refs_1_.refs_4_
  13.0 3.4 pack_cross.1.refs_2_.refs_4_.refs_7_
  16.3 5.4 %pack_feed.1.refs_1_.refs_4_.refs_6_ = bf16[4,592,1024]{2,1,0:T(8,128)(2,1)} custom-call(s32[3]{0:T(128)} %pad_add_fusion.ids_ref, bf16[1024,1024]{1,0:T(8,128)(2,1)} %up_ref.1, bf16[1024,1024]{1,0:T(8,128)(2,1)} %down_ref.1, bf16[1024,128]{1,0:T(8,128)(2,1)} %ain_ref.1, bf16[128,1024]{1,0:T(8,128)(2,1)} %aout_ref.1, f32[1,128]{1,0:T(1,128)} %bitcast.22), custom_call_target="tpu_custom_call" | custom-call | bytes 8388608 | tf_op jit(solution)/shard_map/pack_feed/pallas_call | solution.py:109
  21.8 9.9 %all-to-all-done = bf16[4,256,1024]{2,1,0:T(8,128)(2,1)S(1)} async-done(((bf16[4,256,1024]{2,1,0:T(8,128)(2,1)}), bf16[4,256,1024]{2,1,0:T(8,128)(2,1)S(1)}, u32[]{:S(2)}, u32[]{:S(2)}) %all-to-all-start) | async-done | bytes 2097184 | tf_op jit(solution)/shard_map/all_to_all | solution.py:827
  33.0 10.6 %self_attend.3 = (bf16[16,1024,1024]{2,1,0:T(8,128)(2,1)}, bf16[4,1024,1024]{2,1,0:T(8,128)(2,1)}, f32[16,1,1024]{2,1,0:T(1,128)}, bf16[1024,1024]{1,0:T(8,128)(2,1)}) custom-call(s32[3]{0:T(128)} %pad_add_fusion.ids_ref, bf16[1024,1024]{1,0:T(8,128)(2,1)} %bitcast.13, bf16[4,4,64,1024]{3,2,1,0:T(8,128)(2,1)} %pack_self.1.refs_1_.refs_4_), custom_call_target="tpu_custom_call" | custom-call | flops 10000000000 | bytes 12582912 | tf_op jit(solution)/shard_map/self_attend/pallas_call | solution.py:234
  43.6 9.7 %collective-permute-done.refs_1_.refs_5_ = bf16[4,4,64,1024]{3,2,1,0:T(8,128)(2,1)} collective-permute-done((bf16[4,4,64,1024]{3,2,1,0:T(8,128)(2,1)}, bf16[4,4,64,1024]{3,2,1,0:T(8,128)(2,1)}, u32[]{:S(2)}, u32[]{:S(2)}) %collective-permute-start) | collective-permute-done | bytes 2097184 | tf_op jit(solution)/shard_map/self_near/ppermute | solution.py:823
  59.0 4.7 %all-to-all-start.1 = ((bf16[4,256,1024]{2,1,0:T(8,128)(2,1)}), bf16[4,256,1024]{2,1,0:T(8,128)(2,1)}, u32[]{:S(2)}, u32[]{:S(2)}) async-start(bf16[4,256,1024]{2,1,0:T(8,128)(2,1)} %param.21), calls=%async_computation.1 | async-start | bytes 4194304 | tf_op jit(solution)/shard_map/all_to_all | solution.py:827
  63.7 17.0 %self_attend.4 = (bf16[16,1024,1024]{2,1,0:T(8,128)(2,1)}, bf16[4,1024,1024]{2,1,0:T(8,128)(2,1)}, f32[16,1,1024]{2,1,0:T(1,128)}, bf16[1024,1024]{1,0:T(8,128)(2,1)}) custom-call(s32[3]{0:T(128)} %pad_add_fusion.ids_ref, bf16[1024,1024]{1,0:T(8,128)(2,1)} %bitcast.14, ...), custom_call_target="tpu_custom_call", output_to_operand_aliasing={{0}: (4, {}), {1}: (5, {}), {2}: (6, {}), {3}: (7, {})} | custom-call | flops 20000000000 | bytes 25165824 | tf_op jit(solution)/shard_map/self_attend/pallas_call | solution.py:234
  80.7 5.3 %collective-permute-done.1.refs_1_.refs_7_ = bf16[2,4,64,1024]{3,2,1,0:T(8,128)(2,1)S(1)} collective-permute-done((bf16[2,4,64,1024]{3,2,1,0:T(8,128)(2,1)}, bf16[2,4,64,1024]{3,2,1,0:T(8,128)(2,1)S(1)}, u32[]{:S(2)}, u32[]{:S(2)}) %collective-permute-start.1) | collective-permute-done | bytes 1048608 | tf_op jit(solution)/shard_map/self_onward/ppermute | solution.py:823
  86.0 7.2 %all-to-all-done.1 = bf16[4,256,1024]{2,1,0:T(8,128)(2,1)} async-done(((bf16[4,256,1024]{2,1,0:T(8,128)(2,1)}), bf16[4,256,1024]{2,1,0:T(8,128)(2,1)}, u32[]{:S(2)}, u32[]{:S(2)}) %all-to-all-start.1) | async-done | bytes 2097184 | tf_op jit(solution)/shard_map/all_to_all | solution.py:827
  95.0 10.6 %self_attend.5 = (bf16[16,1024,1024]{2,1,0:T(8,128)(2,1)}, bf16[4,1024,1024]{2,1,0:T(8,128)(2,1)}, f32[16,1,1024]{2,1,0:T(1,128)}, bf16[1024,1024]{1,0:T(8,128)(2,1)}) custom-call(s32[3]{0:T(128)} %pad_add_fusion.ids_ref, bf16[1024,1024]{1,0:T(8,128)(2,1)} %bitcast.15, ...), custom_call_target="tpu_custom_call", output_to_operand_aliasing={{0}: (4, {}), {1}: (5, {}), {2}: (6, {}), {3}: (7, {})} | custom-call | flops 10000000000 | bytes 12582912 | tf_op jit(solution)/shard_map/self_attend/pallas_call | solution.py:234
  105.7 8.3 %out_norm.2 = (bf16[1024,1024]{1,0:T(8,128)(2,1)}, bf16[1024,1024]{1,0:T(8,128)(2,1)}, f32[1024,1]{1,0:T(8,128)}) custom-call(bf16[1024,1024]{1,0:T(8,128)(2,1)} %get-tuple-element.102.refs_0_, bf16[1024,1024]{1,0:T(8,128)(2,1)} %bitcast.16, f32[1,1024]{1,0:T(1,128)} %get-tuple-element.191.refs_2_.refs_6_, f32[1,1024]{1,0:T(1,128)} %get-tuple-element.185.refs_3_, ...), custom_call_target="tpu_custom_call" | custom-call | flops 2147483648 | bytes 10485760 | tf_op jit(solution)/shard_map/out_norm/pallas_call | solution.py:299
  114.0 5.3 %collective-permute-done.4.refs_3_.refs_5_.refs_8_ = bf16[4,4,64,1024]{3,2,1,0:T(8,128)(2,1)} collective-permute-done((bf16[4,4,64,1024]{3,2,1,0:T(8,128)(2,1)S(1)}, bf16[4,4,64,1024]{3,2,1,0:T(8,128)(2,1)}, u32[]{:S(2)}, u32[]{:S(2)}) %collective-permute-start.4) | collective-permute-done | bytes 2097184 | tf_op jit(solution)/shard_map/cross_near/ppermute | solution.py:823
  122.8 24.2 %cross_attend.2 = (bf16[16,1024,1024]{2,1,0:T(8,128)(2,1)}, bf16[4,1024,1024]{2,1,0:T(8,128)(2,1)}, f32[16,1,1024]{2,1,0:T(1,128)}, bf16[1024,1024]{1,0:T(8,128)(2,1)}) custom-call(s32[3]{0:T(128)} %pad_add_fusion.ids_ref, bf16[1024,1024]{1,0:T(8,128)(2,1)} %get-tuple-element.107.refs_0_.refs_1_, bf16[1024,1024]{1,0:T(8,128)(2,1)} %bitcast.4.refs_1_, ...), custom_call_target="tpu_custom_call" | custom-call | flops 20000000000 | bytes 25165824 | tf_op jit(solution)/shard_map/cross_attend/pallas_call | solution.py:234
  151.7 24.3 %cross_attend.3 = (bf16[16,1024,1024]{2,1,0:T(8,128)(2,1)}, bf16[4,1024,1024]{2,1,0:T(8,128)(2,1)}, f32[16,1,1024]{2,1,0:T(1,128)}, bf16[1024,1024]{1,0:T(8,128)(2,1)}) custom-call(s32[3]{0:T(128)} %pad_add_fusion.ids_ref, ...), custom_call_target="tpu_custom_call", output_to_operand_aliasing={{0}: (6, {}), {1}: (7, {}), {2}: (8, {}), {3}: (9, {})} | custom-call | flops 20000000000 | bytes 25165824 | tf_op jit(solution)/shard_map/cross_attend/pallas_call | solution.py:234
  176.0 8.8 %out_norm.3 = (bf16[1024,1024]{1,0:T(8,128)(2,1)}, bf16[1024,1024]{1,0:T(8,128)(2,1)}, f32[1024,1]{1,0:T(8,128)}) custom-call(bf16[1024,1024]{1,0:T(8,128)(2,1)} %get-tuple-element.113.refs_0_, bf16[1024,1024]{1,0:T(8,128)(2,1)} %get-tuple-element.107.refs_0_.refs_1_, f32[1,1024]{1,0:T(1,128)} %get-tuple-element.190.refs_2_.refs_5_, ...), custom_call_target="tpu_custom_call" | custom-call | flops 2147483648 | bytes 10485760 | tf_op jit(solution)/shard_map/out_norm/pallas_call | solution.py:299
  190.3 12.4 %feed.3 = (bf16[1024,4096]{1,0:T(8,128)(2,1)}, bf16[1024,512]{1,0:T(8,128)(2,1)}, bf16[1024,512]{1,0:T(8,128)(2,1)}, f32[1024,1024]{1,0:T(8,128)}) custom-call(s32[3]{0:T(128)} %pad_add_fusion.ids_ref, bf16[1024,1024]{1,0:T(8,128)(2,1)} %get-tuple-element.117.refs_0_.refs_1_, bf16[4,592,1024]{2,1,0:T(8,128)(2,1)} %pack_feed.1.refs_1_.refs_4_.refs_6_), custom_call_target="tpu_custom_call" | custom-call | flops 6000000000 | bytes 14680064 | tf_op jit(solution)/shard_map/feed/pallas_call | solution.py:448
  208.5 3.6 all-to-all-start.2
  213.9 21.8 %feed.4 = (bf16[1024,4096]{1,0:T(8,128)(2,1)}, bf16[1024,512]{1,0:T(8,128)(2,1)}, bf16[1024,512]{1,0:T(8,128)(2,1)}, f32[1024,1024]{1,0:T(8,128)}) custom-call(s32[3]{0:T(128)} %pad_add_fusion.ids_ref, bf16[1024,1024]{1,0:T(8,128)(2,1)} %get-tuple-element.117.refs_0_.refs_1_, ...), custom_call_target="tpu_custom_call", output_to_operand_aliasing={{0}: (5, {}), {1}: (6, {}), {2}: (7, {})} | custom-call | flops 12000000000 | bytes 29360128 | tf_op jit(solution)/shard_map/feed/pallas_call | solution.py:448
  235.8 5.3 %collective-permute-done.10.refs_2_.refs_8_.refs_10_ = bf16[1,592,1024]{2,1,0:T(8,128)(2,1)} collective-permute-done((bf16[1,592,1024]{2,1,0:T(8,128)(2,1)S(1)}, bf16[1,592,1024]{2,1,0:T(8,128)(2,1)}, u32[]{:S(2)}, u32[]{:S(2)}) %collective-permute-start.10) | collective-permute-done | bytes 1212448 | tf_op jit(solution)/shard_map/feed_far/ppermute | solution.py:814
  245.2 16.8 %feed.5 = (bf16[1024,4096]{1,0:T(8,128)(2,1)}, bf16[1024,512]{1,0:T(8,128)(2,1)}, bf16[1024,512]{1,0:T(8,128)(2,1)}, bf16[1024,1024]{1,0:T(8,128)(2,1)}, bf16[1024,1024]{1,0:T(8,128)(2,1)}, /*index=5*/f32[8,1024]{1,0:T(8,128)}) custom-call(s32[3]{0:T(128)} %pad_add_fusion.ids_ref, ...), custom_call_target="tpu_custom_call", output_to_operand_aliasing={{0}: (11, {}), {1}: (12, {}), {2}: (13, {})} | custom-call | flops 6000000000 | bytes 14680064 | tf_op jit(solution)/shard_map/feed/pallas_call | solution.py:448
  263.5 9.4 %adapter_back.1 = (bf16[1024,512]{1,0:T(8,128)(2,1)}, bf16[272,1024]{1,0:T(8,128)(2,1)}, bf16[272,1024]{1,0:T(8,128)(2,1)}, bf16[272,1024]{1,0:T(8,128)(2,1)}, bf16[272,1024]{1,0:T(8,128)(2,1)}) custom-call(s32[3]{0:T(128)} %pad_add_fusion.ids_ref, bf16[1024,1024]{1,0:T(8,128)(2,1)} %get-tuple-element.133.refs_0_, ...), custom_call_target="tpu_custom_call" | custom-call | flops 3221225472 | bytes 12582912 | tf_op jit(solution)/shard_map/adapter_back/pallas_call | solution.py:514
  276.5 3.8 all-to-all-start.3
  280.3 29.6 %feed_back.1 = (bf16[1024,1024]{1,0:T(8,128)(2,1)}, f32[8,1024]{1,0:T(8,128)}) custom-call(s32[3]{0:T(128)} %pad_add_fusion.ids_ref, bf16[1024,1024]{1,0:T(8,128)(2,1)} %get-tuple-element.133.refs_0_, bf16[1024,4096]{1,0:T(8,128)(2,1)} %get-tuple-element.134.refs_1_, bf16[1024,512]{1,0:T(8,128)(2,1)} %get-tuple-element.132.refs_2_, ...), custom_call_target="tpu_custom_call" | custom-call | flops 20000000000 | bytes 41943040 | tf_op jit(solution)/shard_map/feed_back/pallas_call | solution.py:605
  315.5 53.4 %cross_back.1 = (bf16[1024,1024]{1,0:T(8,128)(2,1)}, bf16[1024,1024]{1,0:T(8,128)(2,1)}, f32[8,1024]{1,0:T(8,128)}) custom-call(bf16[1024,1024]{1,0:T(8,128)(2,1)} %get-tuple-element.142.refs_0_, bf16[16,1024,1024]{2,1,0:T(8,128)(2,1)} %get-tuple-element.143.refs_1_, bf16[4,1024,1024]{2,1,0:T(8,128)(2,1)} %get-tuple-element.144.refs_2_, ...), custom_call_target="tpu_custom_call" | custom-call | flops 40000000000 | bytes 62914560 | tf_op jit(solution)/shard_map/cross_back/pallas_call | solution.py:774
  378.6 3.6 all-to-all-start.4
  382.2 40.0 %self_back.1 = (bf16[1024,1024]{1,0:T(8,128)(2,1)}, bf16[4,256,1024]{2,1,0:T(8,128)(2,1)}) custom-call(bf16[1024,1024]{1,0:T(8,128)(2,1)} %get-tuple-element.153.refs_0_, bf16[16,1024,1024]{2,1,0:T(8,128)(2,1)} %get-tuple-element.154.refs_1_, bf16[4,1024,1024]{2,1,0:T(8,128)(2,1)} %get-tuple-element.155.refs_2_, f32[16,1,1024]{2,1,0:T(1,128)} %get-tuple-element.156.refs_3_, ...), custom_call_target="tpu_custom_call" | custom-call | flops 40000000000 | bytes 62914560 | tf_op jit(solution)/shard_map/self_back/pallas_call | solution.py:774
  423.7 4.5 all-to-all-start.5
  433.9 10.4 %collective-permute-done.24 = f32[8,1024]{1,0:T(8,128)S(1)} collective-permute-done((f32[8,1024]{1,0:T(8,128)S(1)}, f32[8,1024]{1,0:T(8,128)S(1)}, u32[]{:S(2)}, u32[]{:S(2)}) %collective-permute-start.24) | collective-permute-done | bytes 32800 | tf_op jit(solution)/shard_map/small/ppermute | solution.py:814
  445.5 3.8 copied.1
  449.2 8.3 %collective-permute-done.25 = f32[8,1024]{1,0:T(8,128)S(1)} collective-permute-done((f32[8,1024]{1,0:T(8,128)S(1)}, f32[8,1024]{1,0:T(8,128)S(1)}, u32[]{:S(2)}, u32[]{:S(2)}) %collective-permute-start.25) | collective-permute-done | bytes 32800 | tf_op jit(solution)/shard_map/small/ppermute | solution.py:814
  (112 shorter events, 73.4 us)
Async XLA Ops:
  0.7 31.1 %all-to-all-start = ((bf16[4,256,1024]{2,1,0:T(8,128)(2,1)}), bf16[4,256,1024]{2,1,0:T(8,128)(2,1)S(1)}, u32[]{:S(2)}, u32[]{:S(2)}) async-start(bf16[4,256,1024]{2,1,0:T(8,128)(2,1)} %param.20), calls=%async_computation | async-start | bytes 4194304 | tf_op jit(solution)/shard_map/all_to_all | solution.py:827
  11.0 42.3 %collective-permute-start = (bf16[4,4,64,1024]{3,2,1,0:T(8,128)(2,1)}, bf16[4,4,64,1024]{3,2,1,0:T(8,128)(2,1)}, u32[]{:S(2)}, u32[]{:S(2)}) collective-permute-start(bf16[4,4,64,1024]{3,2,1,0:T(8,128)(2,1)} %pack_self.1.refs_1_.refs_4_), channel_id=1, source_target_pairs={{0,1},{1,0},{2,3},{3,2},{4,6},{5,7},{6,4},{7,5},{8,9},{9,8},{10,11... | collective-permute-start | bytes 6291464 | tf_op jit(solution)/shard_map/self_near/ppermute | solution.py:823
  53.3 4.4 collective-permute-start.2
  55.6 30.4 %collective-permute-start.1 = (bf16[2,4,64,1024]{3,2,1,0:T(8,128)(2,1)}, bf16[2,4,64,1024]{3,2,1,0:T(8,128)(2,1)S(1)}, u32[]{:S(2)}, u32[]{:S(2)}) collective-permute-start(bf16[2,4,64,1024]{3,2,1,0:T(8,128)(2,1)} %constant_dynamic-slice_fusion.2), channel_id=1, source_target_pairs={{0,2},{1,3},{2,0},{3,1},{4,5},{5,4},{6,7},{7,6},{8,10},{9,11},{10,... | collective-permute-start | bytes 3145736 | tf_op jit(solution)/shard_map/self_onward/ppermute | solution.py:823
  59.0 34.2 %all-to-all-start.1 = ((bf16[4,256,1024]{2,1,0:T(8,128)(2,1)}), bf16[4,256,1024]{2,1,0:T(8,128)(2,1)}, u32[]{:S(2)}, u32[]{:S(2)}) async-start(bf16[4,256,1024]{2,1,0:T(8,128)(2,1)} %param.21), calls=%async_computation.1 | async-start | bytes 4194304 | tf_op jit(solution)/shard_map/all_to_all | solution.py:827
  86.0 9.0 %collective-permute-start.3 = (bf16[2,4,64,1024]{3,2,1,0:T(8,128)(2,1)S(1)}, bf16[2,4,64,1024]{3,2,1,0:T(8,128)(2,1)}, u32[]{:S(2)}, u32[]{:S(2)}) collective-permute-start(bf16[2,4,64,1024]{3,2,1,0:T(8,128)(2,1)S(1)} %collective-permute-done.1.refs_1_.refs_7_), channel_id=1, source_target_pairs={{0,4},{4,0},{8,12},{12,8},{16,20},{20,16},{24,28},{28,24},{1,5},{5... | collective-permute-start | bytes 3145736 | tf_op jit(solution)/shard_map/self_core/ppermute | solution.py:814
  93.2 26.1 %collective-permute-start.4 = (bf16[4,4,64,1024]{3,2,1,0:T(8,128)(2,1)S(1)}, bf16[4,4,64,1024]{3,2,1,0:T(8,128)(2,1)}, u32[]{:S(2)}, u32[]{:S(2)}) collective-permute-start(bf16[4,4,64,1024]{3,2,1,0:T(8,128)(2,1)S(1)} %copy-done.2), channel_id=1, source_target_pairs={{0,1},{1,0},{2,3},{3,2},{4,6},{5,7},{6,4},{7,5},{8,9},{9,8},{10,11... | collective-permute-start | bytes 6291464 | tf_op jit(solution)/shard_map/cross_near/ppermute | solution.py:823
  120.7 29.4 %collective-permute-start.5 = (bf16[4,4,64,1024]{3,2,1,0:T(8,128)(2,1)}, bf16[4,4,64,1024]{3,2,1,0:T(8,128)(2,1)S(1)}, u32[]{:S(2)}, u32[]{:S(2)}) collective-permute-start(bf16[4,4,64,1024]{3,2,1,0:T(8,128)(2,1)} %collective-permute-done.4.refs_3_.refs_5_.refs_8_), channel_id=1, source_target_pairs={{0,4},{4,0},{8,12},{12,8},{16,20},{20,16},{24,28},{28,24},{1,5},{5... | collective-permute-start | bytes 6291464 | tf_op jit(solution)/shard_map/cross_core/ppermute | solution.py:814
  120.7 26.3 %collective-permute-start.6 = (bf16[2,4,64,1024]{3,2,1,0:T(8,128)(2,1)S(1)}, bf16[2,4,64,1024]{3,2,1,0:T(8,128)(2,1)}, u32[]{:S(2)}, u32[]{:S(2)}) collective-permute-start(bf16[2,4,64,1024]{3,2,1,0:T(8,128)(2,1)S(1)} %constant_dynamic-slice_fusion.1), channel_id=1, source_target_pairs={{0,2},{1,3},{2,0},{3,1},{4,5},{5,4},{6,7},{7,6},{8,10},{9,11},{10,... | collective-permute-start | bytes 3145736 | tf_op jit(solution)/shard_map/cross_onward/ppermute | solution.py:823
  122.2 64.9 %collective-permute-start.8 = (bf16[4,592,1024]{2,1,0:T(8,128)(2,1)}, bf16[4,592,1024]{2,1,0:T(8,128)(2,1)}, u32[]{:S(2)}, u32[]{:S(2)}) collective-permute-start(bf16[4,592,1024]{2,1,0:T(8,128)(2,1)} %pack_feed.1.refs_1_.refs_4_.refs_6_), channel_id=1, source_target_pairs={{0,1},{1,0},{2,3},{3,2},{4,6},{5,7},{6,4},{7,5},{8,9},{9,8},{10,11... | collective-permute-start | bytes 14549000 | tf_op jit(solution)/shard_map/feed_near/ppermute | solution.py:823
  147.1 2.9 collective-permute-start.7
  187.1 26.8 %collective-permute-start.11 = (bf16[4,592,1024]{2,1,0:T(8,128)(2,1)}, bf16[4,592,1024]{2,1,0:T(8,128)(2,1)}, u32[]{:S(2)}, u32[]{:S(2)}) collective-permute-start(bf16[4,592,1024]{2,1,0:T(8,128)(2,1)} %collective-permute-done.8.refs_1_.refs_5_.refs_7_), channel_id=1, source_target_pairs={{0,4},{4,0},{8,12},{12,8},{16,20},{20,16},{24,28},{28,24},{1,5},{5... | collective-permute-start | bytes 14549000 | tf_op jit(solution)/shard_map/feed_core/ppermute | solution.py:814
  188.9 16.6 %collective-permute-start.9 = (bf16[1,592,1024]{2,1,0:T(8,128)(2,1)S(1)}, bf16[1,592,1024]{2,1,0:T(8,128)(2,1)S(1)}, u32[]{:S(2)}, u32[]{:S(2)}) collective-permute-start(bf16[1,592,1024]{2,1,0:T(8,128)(2,1)S(1)} %constant_dynamic-slice_fusion), channel_id=1, source_target_pairs={{0,2},{1,3},{2,0},{3,1},{4,5},{5,4},{6,7},{7,6},{8,10},{9,11},{10,... | collective-permute-start | bytes 3637256 | tf_op jit(solution)/shard_map/feed_onward/ppermute | solution.py:823
  205.5 3.0 collective-permute-start.12
  208.5 32.5 %all-to-all-start.2 = ((bf16[4,256,1024]{2,1,0:T(8,128)(2,1)}), bf16[4,256,1024]{2,1,0:T(8,128)(2,1)S(1)}, u32[]{:S(2)}, u32[]{:S(2)}) async-start(bf16[4,256,1024]{2,1,0:T(8,128)(2,1)} %param.39), calls=%async_computation.2 | async-start | bytes 4194304 | tf_op jit(solution)/shard_map/all_to_all | solution.py:827
  212.1 28.9 %collective-permute-start.10 = (bf16[1,592,1024]{2,1,0:T(8,128)(2,1)S(1)}, bf16[1,592,1024]{2,1,0:T(8,128)(2,1)}, u32[]{:S(2)}, u32[]{:S(2)}) collective-permute-start(bf16[1,592,1024]{2,1,0:T(8,128)(2,1)S(1)} %collective-permute-done.9.refs_1_.refs_7_.refs_9_), channel_id=1, source_target_pairs={{0,8},{4,12},{8,0},{12,4},{16,24},{20,28},{24,16},{28,20},{1,9},{5... | collective-permute-start | bytes 3637256 | tf_op jit(solution)/shard_map/feed_far/ppermute | solution.py:814
  241.0 3.1 collective-permute-start.13
  272.9 37.8 %collective-permute-start.14 = (bf16[272,1024]{1,0:T(8,128)(2,1)}, bf16[272,1024]{1,0:T(8,128)(2,1)S(1)}, u32[]{:S(2)}, u32[]{:S(2)}) collective-permute-start(bf16[272,1024]{1,0:T(8,128)(2,1)} %get-tuple-element.139), channel_id=1, source_target_pairs={{0,1},{1,0},{2,3},{3,2},{4,6},{5,7},{6,4},{7,5},{8,9},{9,8},{10,11... | collective-permute-start | bytes 1671176 | tf_op jit(solution)/shard_map/adapter/ppermute | solution.py:823
  274.6 39.1 %collective-permute-start.15 = (bf16[272,1024]{1,0:T(8,128)(2,1)}, bf16[272,1024]{1,0:T(8,128)(2,1)}, u32[]{:S(2)}, u32[]{:S(2)}) collective-permute-start(bf16[272,1024]{1,0:T(8,128)(2,1)} %get-tuple-element.140), channel_id=1, source_target_pairs={{0,2},{1,3},{2,0},{3,1},{4,5},{5,4},{6,7},{7,6},{8,10},{9,11},{10,... | collective-permute-start | bytes 1671176 | tf_op jit(solution)/shard_map/adapter/ppermute | solution.py:823
  276.1 37.6 %collective-permute-start.16 = (bf16[272,1024]{1,0:T(8,128)(2,1)}, bf16[272,1024]{1,0:T(8,128)(2,1)}, u32[]{:S(2)}, u32[]{:S(2)}) collective-permute-start(bf16[272,1024]{1,0:T(8,128)(2,1)} %get-tuple-element.141), channel_id=1, source_target_pairs={{0,3},{1,2},{2,1},{3,0},{4,7},{5,6},{6,5},{7,4},{8,11},{9,10},{10,... | collective-permute-start | bytes 1671176 | tf_op jit(solution)/shard_map/adapter/ppermute | solution.py:814
  276.5 100.8 %all-to-all-start.3 = ((bf16[4,256,1024]{2,1,0:T(8,128)(2,1)}), bf16[4,256,1024]{2,1,0:T(8,128)(2,1)S(1)}, u32[]{:S(2)}, u32[]{:S(2)}) async-start(bf16[4,256,1024]{2,1,0:T(8,128)(2,1)} %bitcast.7), calls=%async_computation.3 | async-start | bytes 4194304 | tf_op jit(solution)/shard_map/all_to_all | solution.py:827
  315.5 58.0 %collective-permute-start.17 = (bf16[272,1024]{1,0:T(8,128)(2,1)S(1)}, bf16[272,1024]{1,0:T(8,128)(2,1)S(1)}, u32[]{:S(2)}, u32[]{:S(2)}) collective-permute-start(bf16[272,1024]{1,0:T(8,128)(2,1)S(1)} %add_convert_fusion.3), channel_id=1, source_target_pairs={{0,4},{4,0},{8,12},{12,8},{16,20},{20,16},{24,28},{28,24},{1,5},{5... | collective-permute-start | bytes 1671176 | tf_op jit(solution)/shard_map/adapter/ppermute | solution.py:814
  369.9 52.3 %collective-permute-start.18 = (f32[8,1024]{1,0:T(8,128)S(1)}, f32[8,1024]{1,0:T(8,128)S(1)}, u32[]{:S(2)}, u32[]{:S(2)}) collective-permute-start(f32[8,1024]{1,0:T(8,128)S(1)} %concatenate.4), channel_id=1, source_target_pairs={{0,1},{1,0},{2,3},{3,2},{4,5},{5,4},{6,7},{7,6},{8,9},{9,8},{10,11... | collective-permute-start | bytes 98312 | tf_op jit(solution)/shard_map/small/ppermute | solution.py:814
  370.0 52.2 %collective-permute-start.19 = (f32[8,1024]{1,0:T(8,128)S(1)}, f32[8,1024]{1,0:T(8,128)S(1)}, u32[]{:S(2)}, u32[]{:S(2)}) collective-permute-start(f32[8,1024]{1,0:T(8,128)S(1)} %concatenate.4), channel_id=1, source_target_pairs={{0,2},{1,3},{2,0},{3,1},{4,6},{5,7},{6,4},{7,5},{8,10},{9,11},{10,... | collective-permute-start | bytes 98312 | tf_op jit(solution)/shard_map/small/ppermute | solution.py:814
  371.5 50.7 %collective-permute-start.20 = (f32[8,1024]{1,0:T(8,128)S(1)}, f32[8,1024]{1,0:T(8,128)S(1)}, u32[]{:S(2)}, u32[]{:S(2)}) collective-permute-start(f32[8,1024]{1,0:T(8,128)S(1)} %concatenate.4), channel_id=1, source_target_pairs={{0,3},{1,2},{2,1},{3,0},{4,7},{5,6},{6,5},{7,4},{8,11},{9,10},{10,... | collective-permute-start | bytes 98312 | tf_op jit(solution)/shard_map/small/ppermute | solution.py:814
  375.5 46.7 %collective-permute-start.21 = (bf16[272,1024]{1,0:T(8,128)(2,1)S(1)}, bf16[272,1024]{1,0:T(8,128)(2,1)S(1)}, u32[]{:S(2)}, u32[]{:S(2)}) collective-permute-start(bf16[272,1024]{1,0:T(8,128)(2,1)S(1)} %add_convert_fusion.2), channel_id=1, source_target_pairs={{0,8},{4,12},{8,0},{12,4},{16,24},{20,28},{24,16},{28,20},{1,9},{5... | collective-permute-start | bytes 1671176 | tf_op jit(solution)/shard_map/adapter/ppermute | solution.py:814
  378.6 43.7 %all-to-all-start.4 = ((bf16[4,256,1024]{2,1,0:T(8,128)(2,1)}), bf16[4,256,1024]{2,1,0:T(8,128)(2,1)S(1)}, u32[]{:S(2)}, u32[]{:S(2)}) async-start(bf16[4,256,1024]{2,1,0:T(8,128)(2,1)} %bitcast.19), calls=%async_computation.4 | async-start | bytes 4194304 | tf_op jit(solution)/shard_map/all_to_all | solution.py:827
  423.7 37.6 %all-to-all-start.5 = ((bf16[4,256,1024]{2,1,0:T(8,128)(2,1)}), bf16[4,256,1024]{2,1,0:T(8,128)(2,1)}, u32[]{:S(2)}, u32[]{:S(2)}) async-start(bf16[4,256,1024]{2,1,0:T(8,128)(2,1)} %bitcast.18), calls=%async_computation.5 | async-start | bytes 4194304 | tf_op jit(solution)/shard_map/all_to_all | solution.py:827
  429.5 29.2 %collective-permute-start.22 = (bf16[272,1024]{1,0:T(8,128)(2,1)S(1)}, bf16[272,1024]{1,0:T(8,128)(2,1)S(1)}, u32[]{:S(2)}, u32[]{:S(2)}) collective-permute-start(bf16[272,1024]{1,0:T(8,128)(2,1)S(1)} %add_convert_fusion.1), channel_id=1, source_target_pairs={{0,16},{4,20},{8,24},{12,28},{16,0},{20,4},{24,8},{28,12},{1,17},{... | collective-permute-start | bytes 1671176 | tf_op jit(solution)/shard_map/adapter/ppermute | solution.py:814
  432.1 1.3 collective-permute-start.23
  433.4 10.9 %collective-permute-start.24 = (f32[8,1024]{1,0:T(8,128)S(1)}, f32[8,1024]{1,0:T(8,128)S(1)}, u32[]{:S(2)}, u32[]{:S(2)}) collective-permute-start(f32[8,1024]{1,0:T(8,128)S(1)} %add.78), channel_id=1, source_target_pairs={{0,8},{4,12},{8,0},{12,4},{16,24},{20,28},{24,16},{28,20},{1,9},{5... | collective-permute-start | bytes 98312 | tf_op jit(solution)/shard_map/small/ppermute | solution.py:814
  444.3 13.2 %collective-permute-start.25 = (f32[8,1024]{1,0:T(8,128)S(1)}, f32[8,1024]{1,0:T(8,128)S(1)}, u32[]{:S(2)}, u32[]{:S(2)}) collective-permute-start(f32[8,1024]{1,0:T(8,128)S(1)} %add.79), channel_id=1, source_target_pairs={{0,16},{4,20},{8,24},{12,28},{16,0},{20,4},{24,8},{28,12},{1,17},{... | collective-permute-start | bytes 98312 | tf_op jit(solution)/shard_map/small/ppermute | solution.py:814
  (18 other events, 162.1 us)
